TPU v7x, 32 devices: a whole 2x2x4 slice. The times are simulated.
32 devices in a mesh: layer: 4 (over y, core), feat: 8 (over z, x).
Axes of the slice: x: 2, y: 2, z: 4, core: 2. Of those that a mesh axis runs over, the one named last changes fastest.
Arguments:
- top_grad: bfloat16 [64, 4608], P('feat'), may hold values from -6 to 6
- decoder: bfloat16 [4, 4096, 4608], P('layer', 'feat'), may hold values from -0.09375 to 0.09375
- encoder: bfloat16 [4, 4096, 4608], P('layer', 'feat'), may hold values from -0.0625 to 0.0625
- activations: bfloat16 [4, 64, 4096], P('layer', None, 'feat'), may hold values from 0.099609375 to 3
- block_ids: int32 [4, 8, 16], P('layer'), may hold values from 0 to 31, all different within a row
- block_counts: int32 [4, 8], P('layer'), may hold values from 1 to 16, 64 in all within a row
Outputs:
- attribution: bfloat16 [4, 64, 4096], P('layer', None, 'feat')
- grads: float32 [4, 64, 4608], P('layer', 'feat')
Inputs may be any that keep to these rules, and one draw needn't show every extreme that they name: `block_ids`: within one row of the last dimension the ids are distinct; every block id appears somewhere. `block_counts`: for each layer the counts sum to 64, and some tile of each layer has exactly 16.
All inputs are finite; a program needn't handle non-finite values.
Results may differ from a plain program's by a relative error of at most 0.024.
Values may be sent and summed in bfloat16 or wider, within the bound.
No kernel may reach another device: no remote copies, remote signals or barrier semaphores. Data moves between devices by JAX's collectives and lax.ppermute only.
A program may use at most 64 MiB of HBM per device.

v0:
```python
import jax
import jax.numpy as jnp
from jax import lax
from jax.sharding import PartitionSpec as P

BLOCK = 128


def passed_along(value, axis, steps):
    count = lax.axis_size(axis)
    first, last = (max(0, -steps), min(count, count - steps))
    return lax.ppermute(value, axis, [(source, source + steps) for source in range(first, last)])


def body(top_grad, decoder, encoder, activations, block_ids, block_counts):
    layer_count = lax.axis_size("layer")
    tile_count = lax.axis_size("feat")
    section_index = lax.axis_index("layer")
    feat_index = lax.axis_index("feat")
    dec_rows = decoder[0]
    enc_rows = encoder[0]
    feat_dev = dec_rows.shape[0]
    model_width = dec_rows.shape[1]
    blk_dev = feat_dev // BLOCK
    tok_dev = top_grad.shape[0]
    list_width = block_ids.shape[2]
    listed = jnp.arange(list_width, dtype=jnp.int32)[None, :] < block_counts[0][:, None]
    owned = feat_index * blk_dev + jnp.arange(blk_dev, dtype=jnp.int32)
    matches = (block_ids[0][:, :, None] == owned[None, None, :]) & listed[:, :, None]
    tile_mask = jnp.any(matches, axis=1).astype(jnp.bfloat16)
    gated = (
        activations[0].reshape(tile_count, tok_dev, blk_dev, BLOCK) * tile_mask[:, None, :, None]
    )
    gated = gated.reshape(tile_count, tok_dev, feat_dev)
    group_count = 4
    group_rows = tok_dev // group_count
    step_total = group_count + layer_count - 1
    is_top = section_index == layer_count - 1

    def advance(step_count, carry):
        incoming, attr_buf, grad_buf = carry
        group_index = step_count - (layer_count - 1 - section_index)
        is_live = (group_index >= 0) & (group_index < group_count)
        group_slot = jnp.clip(group_index, 0, group_count - 1)
        row_offset = group_slot * group_rows
        top_rows = lax.dynamic_slice_in_dim(top_grad, row_offset, group_rows, 0).astype(jnp.float32)
        upstream = jnp.where(is_top, top_rows, incoming)
        gate_rows = lax.dynamic_slice_in_dim(gated, row_offset, group_rows, 1).reshape(
            tile_count * group_rows, feat_dev
        )
        scores = lax.dot_general(
            lax.all_gather(upstream.astype(jnp.bfloat16), "feat", axis=0, tiled=True),
            dec_rows,
            (((1,), (1,)), ((), ())),
            preferred_element_type=jnp.float32,
        )
        attributed = (scores * gate_rows).astype(jnp.bfloat16)
        summed = lax.psum_scatter(
            jnp.dot(attributed, enc_rows, preferred_element_type=jnp.float32).astype(jnp.bfloat16),
            "feat",
            scatter_dimension=0,
            tiled=True,
        ).astype(jnp.float32)
        updated = upstream + summed
        old_attr = lax.dynamic_slice_in_dim(attr_buf, row_offset, group_rows, 1)
        new_attr = jnp.where(
            is_live, attributed.reshape(tile_count, group_rows, feat_dev), old_attr
        )
        attr_buf = lax.dynamic_update_slice_in_dim(attr_buf, new_attr, row_offset, 1)
        old_grad = lax.dynamic_slice_in_dim(grad_buf, row_offset, group_rows, 0)
        new_grad = jnp.where(is_live, updated, old_grad)
        grad_buf = lax.dynamic_update_slice_in_dim(grad_buf, new_grad, row_offset, 0)
        passed = passed_along(updated.astype(jnp.bfloat16), "layer", -1).astype(updated.dtype)
        return (passed, attr_buf, grad_buf)

    start_state = (
        jnp.zeros((group_rows, model_width), jnp.float32),
        jnp.zeros((tile_count, tok_dev, feat_dev), jnp.bfloat16),
        jnp.zeros((tok_dev, model_width), jnp.float32),
    )
    final_state = lax.fori_loop(0, step_total, advance, start_state)
    attr_out = final_state[1].reshape(1, tile_count * tok_dev, feat_dev)
    grad_out = final_state[2][None]
    return (attr_out, grad_out)


def solution(mesh):
    placed = (
        P("feat", None),
        P("layer", "feat", None),
        P("layer", "feat", None),
        P("layer", None, "feat"),
        P("layer", None, None),
        P("layer", None),
    )
    return jax.shard_map(
        body,
        mesh=mesh,
        in_specs=placed,
        out_specs=(P("layer", None, "feat"), P("layer", "feat", None)),
        check_vma=False,
    )
```

profile of v0, /device:TPU:0, one launch (start us, length us, event | category | flops | bytes accessed | tf_op | source)
XLA Modules:
  0.0 793.1 jit_solution(7280959467495547660)
XLA Ops:
  9.8 775.8 %while.20 = (s32[]{:T(128)}, f32[2,4608]{1,0:T(2,128)S(1)}, bf16[8,8,512]{2,1,0:T(8,128)(2,1)S(1)}, f32[8,4608]{1,0:T(8,128)S(1)}, pred[]{:T(512)}, /*index=5*/s...) while((s32[]{:T(128)}, f32[2,4608]{1,0:T(2,128)S(1)}, ...), condition=%wide.region_3.4_spmd.clone, body=%wide.region_1.3_spmd.clone.sunk | while | flops 151276560 | bytes 30583788 | solution.py:81
  10.9 32.3 %all-gather.3 = bf16[8,2,4608]{2,1,0:T(2,128)(2,1)S(1)} all-gather(bf16[1,2,4608]{2,1,0:T(2,128)(2,1)S(1)} %convert_bitcast_fusion.2), channel_id=1, replica_groups=mesh['layer'=4,'feat'=8] {'feat'}, dimensions={0}, use_global_device_ids=true | all-gather | bytes 165888 | tf_op jit(solution)/shard_map/while/body/eval_jaxpr/all_gather | solution.py:52
  43.3 3.8 fusion.17
  49.9 69.5 %all-reduce.5.cloned.1.call-done = bf16[16,4608]{1,0:T(8,128)(2,1)} async-done(((bf16[16,4608]{1,0:T(8,128)(2,1)}), bf16[16,4608]{1,0:T(8,128)(2,1)}) %all-reduce.5.cloned.1.call-update) | async-done | bytes 147472 | tf_op jit(solution)/shard_map/while
  121.7 1.7 collective-permute-done
  124.5 30.6 %all-gather.3 = bf16[8,2,4608]{2,1,0:T(2,128)(2,1)S(1)} all-gather(bf16[1,2,4608]{2,1,0:T(2,128)(2,1)S(1)} %convert_bitcast_fusion.2), channel_id=1, replica_groups=mesh['layer'=4,'feat'=8] {'feat'}, dimensions={0}, use_global_device_ids=true | all-gather | bytes 165888 | tf_op jit(solution)/shard_map/while/body/eval_jaxpr/all_gather | solution.py:52
  155.3 3.8 fusion.17
  161.8 67.9 %all-reduce.5.cloned.1.call-done = bf16[16,4608]{1,0:T(8,128)(2,1)} async-done(((bf16[16,4608]{1,0:T(8,128)(2,1)}), bf16[16,4608]{1,0:T(8,128)(2,1)}) %all-reduce.5.cloned.1.call-update) | async-done | bytes 147472 | tf_op jit(solution)/shard_map/while
  232.1 1.7 collective-permute-done
  234.9 30.6 %all-gather.3 = bf16[8,2,4608]{2,1,0:T(2,128)(2,1)S(1)} all-gather(bf16[1,2,4608]{2,1,0:T(2,128)(2,1)S(1)} %convert_bitcast_fusion.2), channel_id=1, replica_groups=mesh['layer'=4,'feat'=8] {'feat'}, dimensions={0}, use_global_device_ids=true | all-gather | bytes 165888 | tf_op jit(solution)/shard_map/while/body/eval_jaxpr/all_gather | solution.py:52
  265.6 3.8 fusion.17
  272.2 67.9 %all-reduce.5.cloned.1.call-done = bf16[16,4608]{1,0:T(8,128)(2,1)} async-done(((bf16[16,4608]{1,0:T(8,128)(2,1)}), bf16[16,4608]{1,0:T(8,128)(2,1)}) %all-reduce.5.cloned.1.call-update) | async-done | bytes 147472 | tf_op jit(solution)/shard_map/while
  342.4 1.7 collective-permute-done
  345.3 30.6 %all-gather.3 = bf16[8,2,4608]{2,1,0:T(2,128)(2,1)S(1)} all-gather(bf16[1,2,4608]{2,1,0:T(2,128)(2,1)S(1)} %convert_bitcast_fusion.2), channel_id=1, replica_groups=mesh['layer'=4,'feat'=8] {'feat'}, dimensions={0}, use_global_device_ids=true | all-gather | bytes 165888 | tf_op jit(solution)/shard_map/while/body/eval_jaxpr/all_gather | solution.py:52
  376.0 3.8 fusion.17
  379.8 1.4 convolution_convert_fusion.2
  382.5 67.9 %all-reduce.5.cloned.1.call-done = bf16[16,4608]{1,0:T(8,128)(2,1)} async-done(((bf16[16,4608]{1,0:T(8,128)(2,1)}), bf16[16,4608]{1,0:T(8,128)(2,1)}) %all-reduce.5.cloned.1.call-update) | async-done | bytes 147472 | tf_op jit(solution)/shard_map/while
  452.8 1.7 collective-permute-done
  455.6 30.6 %all-gather.3 = bf16[8,2,4608]{2,1,0:T(2,128)(2,1)S(1)} all-gather(bf16[1,2,4608]{2,1,0:T(2,128)(2,1)S(1)} %convert_bitcast_fusion.2), channel_id=1, replica_groups=mesh['layer'=4,'feat'=8] {'feat'}, dimensions={0}, use_global_device_ids=true | all-gather | bytes 165888 | tf_op jit(solution)/shard_map/while/body/eval_jaxpr/all_gather | solution.py:52
  486.3 3.8 fusion.17
  490.1 1.4 convolution_convert_fusion.2
  492.9 67.9 %all-reduce.5.cloned.1.call-done = bf16[16,4608]{1,0:T(8,128)(2,1)} async-done(((bf16[16,4608]{1,0:T(8,128)(2,1)}), bf16[16,4608]{1,0:T(8,128)(2,1)}) %all-reduce.5.cloned.1.call-update) | async-done | bytes 147472 | tf_op jit(solution)/shard_map/while
  563.2 1.7 collective-permute-done
  566.0 30.6 %all-gather.3 = bf16[8,2,4608]{2,1,0:T(2,128)(2,1)S(1)} all-gather(bf16[1,2,4608]{2,1,0:T(2,128)(2,1)S(1)} %convert_bitcast_fusion.2), channel_id=1, replica_groups=mesh['layer'=4,'feat'=8] {'feat'}, dimensions={0}, use_global_device_ids=true | all-gather | bytes 165888 | tf_op jit(solution)/shard_map/while/body/eval_jaxpr/all_gather | solution.py:52
  596.7 3.8 fusion.17
  600.5 1.4 convolution_convert_fusion.2
  603.2 67.9 %all-reduce.5.cloned.1.call-done = bf16[16,4608]{1,0:T(8,128)(2,1)} async-done(((bf16[16,4608]{1,0:T(8,128)(2,1)}), bf16[16,4608]{1,0:T(8,128)(2,1)}) %all-reduce.5.cloned.1.call-update) | async-done | bytes 147472 | tf_op jit(solution)/shard_map/while
  673.5 1.7 collective-permute-done
  676.3 30.6 %all-gather.3 = bf16[8,2,4608]{2,1,0:T(2,128)(2,1)S(1)} all-gather(bf16[1,2,4608]{2,1,0:T(2,128)(2,1)S(1)} %convert_bitcast_fusion.2), channel_id=1, replica_groups=mesh['layer'=4,'feat'=8] {'feat'}, dimensions={0}, use_global_device_ids=true | all-gather | bytes 165888 | tf_op jit(solution)/shard_map/while/body/eval_jaxpr/all_gather | solution.py:52
  707.0 3.8 fusion.17
  713.6 67.9 %all-reduce.5.cloned.1.call-done = bf16[16,4608]{1,0:T(8,128)(2,1)} async-done(((bf16[16,4608]{1,0:T(8,128)(2,1)}), bf16[16,4608]{1,0:T(8,128)(2,1)}) %all-reduce.5.cloned.1.call-update) | async-done | bytes 147472 | tf_op jit(solution)/shard_map/while
  783.9 1.7 collective-permute-done
  (129 shorter events, 37.7 us)
Async XLA Ops:
  9.8 109.6 %all-reduce.5.cloned.1.call-start = ((), (), s32[]{:S(2)}) async-start(), calls=%async_computation | async-start | bytes 294912 | tf_op jit(solution)/shard_map/while
  43.3 3.8 copy-start
  43.3 5.3 copy-start.3
  120.4 3.1 collective-permute-start
  123.5 106.2 %all-reduce.5.cloned.1.call-start = ((), (), s32[]{:S(2)}) async-start(), calls=%async_computation | async-start | bytes 294912 | tf_op jit(solution)/shard_map/while
  155.2 3.8 copy-start
  155.2 5.3 copy-start.3
  230.7 3.1 collective-permute-start
  233.9 106.2 %all-reduce.5.cloned.1.call-start = ((), (), s32[]{:S(2)}) async-start(), calls=%async_computation | async-start | bytes 294912 | tf_op jit(solution)/shard_map/while
  265.6 3.8 copy-start
  265.6 5.3 copy-start.3
  341.1 3.1 collective-permute-start
  344.2 106.2 %all-reduce.5.cloned.1.call-start = ((), (), s32[]{:S(2)}) async-start(), calls=%async_computation | async-start | bytes 294912 | tf_op jit(solution)/shard_map/while
  375.9 3.8 copy-start
  375.9 5.3 copy-start.3
  451.5 3.1 collective-permute-start
  454.6 106.2 %all-reduce.5.cloned.1.call-start = ((), (), s32[]{:S(2)}) async-start(), calls=%async_computation | async-start | bytes 294912 | tf_op jit(solution)/shard_map/while
  486.3 3.8 copy-start
  486.3 5.3 copy-start.3
  561.8 3.1 collective-permute-start
  564.9 106.2 %all-reduce.5.cloned.1.call-start = ((), (), s32[]{:S(2)}) async-start(), calls=%async_computation | async-start | bytes 294912 | tf_op jit(solution)/shard_map/while
  596.6 3.8 copy-start
  596.7 5.3 copy-start.3
  672.2 3.1 collective-permute-start
  675.3 106.2 %all-reduce.5.cloned.1.call-start = ((), (), s32[]{:S(2)}) async-start(), calls=%async_computation | async-start | bytes 294912 | tf_op jit(solution)/shard_map/while
  707.0 3.8 copy-start
  707.0 5.3 copy-start.3
  782.5 3.1 collective-permute-start
  785.6 0.7 copy-start.1
  785.6 0.7 copy-start.2
Sparse Core Ops, SparseCore 0:
  48.7 70.6 all-reduce.4
  160.6 69.0 all-reduce.4
  271.0 69.0 all-reduce.4
  381.3 69.0 all-reduce.4
  491.7 69.0 all-reduce.4
  602.0 69.0 all-reduce.4
  712.4 69.0 all-reduce.4
where the time goes:
time: 796 us; the launch traced here: 793 us
  waiting for transfers between devices  489 us (61%)
  blocking collectives  216 us (27%)
  matrix products  36.5 us (5%)
  other arithmetic  16.6 us (2%)
  between operations  14.1 us (2%)
  starting transfers between devices  9.32 us (1%)
    while x14, waiting for transfers between devices  477 us
    all_gather x7, blocking collectives, advance(): lax.all_gather(upstream.astype(jnp.bfloat16), 'feat', axis=0, tiled=True)  216 us
    dot_general x7, matrix products, advance(): lax.dot_general(lax.all_gather(upstream.astype(jnp.bfloat16), 'feat', axi...  26.6 us
  transfers between devices with their start and end apart: 14, of which 14 were waited for; matrix products, arithmetic and copies ran while one was open for 1% of the time, Pallas kernels for 0%

commit v1 on v0

v1 whole, which is shorter than its diff:
```python
import jax
import jax.numpy as jnp
from jax import lax
from jax.sharding import PartitionSpec as P

BLOCK = 128
AXES = ("layer", "feat")


def body(top_grad, decoder, encoder, activations, block_ids, block_counts):
    layers = lax.axis_size("layer")
    tiles = lax.axis_size("feat")
    layer_index = lax.axis_index("layer")
    feat_index = lax.axis_index("feat")
    dec = decoder[0]
    enc = encoder[0]
    feat_dev = dec.shape[0]
    blk_dev = feat_dev // BLOCK
    tok_dev = top_grad.shape[0]

    def link(layer, to_layer, k):
        return [(layer * tiles + i, (to_layer % layers) * tiles + (i ^ k)) for i in range(tiles)]

    def within(value, layer, k):
        pairs = []
        for l in range(layers):
            pairs += link(l, l, k) if (l - layer) % 2 == 0 else link(l, l + 2, 0)
        return lax.ppermute(value, AXES, pairs)

    def below(value, layer, k):
        pairs = []
        for l in range(layers):
            pairs += link(l, l - 1, k if (l - layer) % 2 == 0 else 0)
        return lax.ppermute(value, AXES, pairs)

    direct = tiles <= 8
    order = jnp.arange(tiles, dtype=jnp.int32)
    if direct:
        order = feat_index ^ order

    def spread(value, layer):
        if direct:
            return [value] + [within(value, layer, k) for k in range(1, tiles)]
        copies = jnp.broadcast_to(value[None], (tiles,) + value.shape)
        return list(lax.all_to_all(copies, "feat", 0, 0, tiled=True))

    def collect(parts, layer):
        if direct:
            return [parts[0]] + [within(parts[k], layer, k) for k in range(1, tiles)]
        return list(lax.all_to_all(parts, "feat", 0, 0, tiled=True))

    listed = jnp.arange(block_ids.shape[2], dtype=jnp.int32)[None, :] < block_counts[0][:, None]
    owned = feat_index * blk_dev + jnp.arange(blk_dev, dtype=jnp.int32)
    matches = (block_ids[0][:, :, None] == owned[None, None, :]) & listed[:, :, None]
    tile_mask = jnp.any(matches, axis=1).astype(jnp.bfloat16)
    gate = (
        activations[0].reshape(tiles, tok_dev, blk_dev, BLOCK) * tile_mask[:, None, :, None]
    ).reshape(tiles, tok_dev, feat_dev)
    gate = jnp.take(gate, order, axis=0).reshape(tiles * tok_dev, feat_dev)

    attr_out = None
    grad_out = None
    updated = top_grad.astype(jnp.float32)
    for layer in reversed(range(layers)):
        sent = updated.astype(jnp.bfloat16)
        if layer == layers - 1:
            upstream = updated
            rows = spread(sent, layer)
        elif direct:
            rows = [below(sent, layer + 1, k) for k in range(tiles)]
            upstream = rows[0].astype(jnp.float32)
        else:
            passed = below(sent, layer + 1, 0)
            rows = spread(passed, layer)
            upstream = passed.astype(jnp.float32)
        scores = lax.dot_general(
            jnp.concatenate(rows, 0),
            dec,
            (((1,), (1,)), ((), ())),
            preferred_element_type=jnp.float32,
        )
        attributed = (scores * gate.astype(jnp.float32)).astype(jnp.bfloat16)
        part = jnp.dot(attributed, enc, preferred_element_type=jnp.float32).astype(jnp.bfloat16)
        terms = collect(part.reshape(tiles, tok_dev, -1), layer)
        updated = upstream
        for term in terms:
            updated = updated + term.astype(jnp.float32)
        mine = layer_index == layer
        attr_out = attributed if attr_out is None else jnp.where(mine, attributed, attr_out)
        grad_out = updated if grad_out is None else jnp.where(mine, updated, grad_out)
    attr_out = jnp.take(attr_out.reshape(tiles, tok_dev, feat_dev), order, axis=0)
    return attr_out.reshape(1, tiles * tok_dev, feat_dev), grad_out[None]


def solution(mesh):
    placed = (
        P("feat", None),
        P("layer", "feat", None),
        P("layer", "feat", None),
        P("layer", None, "feat"),
        P("layer", None, None),
        P("layer", None),
    )
    return jax.shard_map(
        body,
        mesh=mesh,
        in_specs=placed,
        out_specs=(P("layer", None, "feat"), P("layer", "feat", None)),
        check_vma=False,
    )
```

time: 796 us -> 140 us (0.18)
  waiting for transfers between devices: 489 us -> 32.3 us
  blocking collectives: 216 us -> 0 us
  starting transfers between devices: 9.32 us -> 82.5 us
  matrix products: 36.5 us -> 17.1 us
  between operations: 14.1 us -> 1.05 us
  other arithmetic: 16.6 us -> 4.32 us
    while x14 -> x0, waiting for transfers between devices: 477 us -> none
    all_gather x7 -> x0, blocking collectives: 216 us -> none  [advance(): lax.all_gather(upstream.astype(jnp.bfloat16), 'feat', axis=0, tiled=True)]
    ppermute x7 -> x59, starting transfers between devices: 9.03 us -> 82.5 us  [the longest x35 46.8 us: within(): return lax.ppermute(value, AXES, pairs)]
    ppermute x7 -> x59, waiting for transfers between devices: 12.1 us -> 32.3 us  [the longest x35 19 us: within(): return lax.ppermute(value, AXES, pairs)]
    dot_general x14 -> x8, matrix products: 36.5 us -> 17.1 us  [the longest x4 11 us: body(): lax.dot_general(jnp.concatenate(rows, 0), dec, (((1,), (1,)), ((), ())),...]
  transfers between devices with their start and end apart: 14 -> 59, of which waited for: 14 -> 23; matrix products, arithmetic and copies ran while one was open for 1% -> 4% of each run, Pallas kernels for 0% -> 0%
where the time goes in v1:
time: 140 us
  starting transfers between devices  82.5 us (59%)
  waiting for transfers between devices  32.3 us (23%)
  matrix products  17.1 us (12%)
  other arithmetic  4.32 us (3%)
  local copies, waits for them, and re-layouts  2.46 us (2%)
    ppermute x35, starting transfers between devices, within(): return lax.ppermute(value, AXES, pairs)  46.8 us
    ppermute x24, starting transfers between devices, below(): return lax.ppermute(value, AXES, pairs)  35.7 us
    ppermute x35, waiting for transfers between devices, within(): return lax.ppermute(value, AXES, pairs)  19 us
    ppermute x24, waiting for transfers between devices, below(): return lax.ppermute(value, AXES, pairs)  13.3 us
    dot_general x4, matrix products, body(): lax.dot_general(jnp.concatenate(rows, 0), dec, (((1,), (1,)), ((), ())),...  11 us
    dot_general x4, matrix products, body(): jnp.dot(attributed, enc, preferred_element_type=jnp.float32)  6.11 us
  transfers between devices with their start and end apart: 59, of which 23 were waited for; matrix products, arithmetic and copies ran while one was open for 4% of the time, Pallas kernels for 0%

profile of v1, /device:TPU:0, one launch (start us, length us, event | category | flops | bytes accessed | tf_op | source)
XLA Modules:
  0.0 139.8 jit_solution(3604716181237276578)
XLA Ops:
  0.6 3.0 %collective-permute-start = (bf16[8,4608]{1,0:T(8,128)(2,1)}, bf16[8,4608]{1,0:T(8,128)(2,1)S(1)}, u32[]{:S(2)}, u32[]{:S(2)}) collective-permute-start(bf16[8,4608]{1,0:T(8,128)(2,1)} %param.8), channel_id=1, source_target_pairs={{0,16},{1,17},{2,18},{3,19},{4,20},{5,21},{6,22},{7,23},{8,9},{9,8... | collective-permute-start | bytes 221192 | tf_op jit(solution)/shard_map/ppermute | solution.py:28
  3.7 1.9 %collective-permute-start.2 = (bf16[8,4608]{1,0:T(8,128)(2,1)}, bf16[8,4608]{1,0:T(8,128)(2,1)S(1)}, u32[]{:S(2)}, u32[]{:S(2)}) collective-permute-start(bf16[8,4608]{1,0:T(8,128)(2,1)} %param.8), channel_id=1, source_target_pairs={{0,16},{1,17},{2,18},{3,19},{4,20},{5,21},{6,22},{7,23},{8,11},{9,... | collective-permute-start | bytes 221192 | tf_op jit(solution)/shard_map/ppermute | solution.py:28
  5.8 1.9 %collective-permute-start.4 = (bf16[8,4608]{1,0:T(8,128)(2,1)}, bf16[8,4608]{1,0:T(8,128)(2,1)S(1)}, u32[]{:S(2)}, u32[]{:S(2)}) collective-permute-start(bf16[8,4608]{1,0:T(8,128)(2,1)} %param.8), channel_id=1, source_target_pairs={{0,16},{1,17},{2,18},{3,19},{4,20},{5,21},{6,22},{7,23},{8,13},{9,... | collective-permute-start | bytes 221192 | tf_op jit(solution)/shard_map/ppermute | solution.py:28
  12.0 2.0 %collective-permute-start.6 = (bf16[8,4608]{1,0:T(8,128)(2,1)}, bf16[8,4608]{1,0:T(8,128)(2,1)S(1)}, u32[]{:S(2)}, u32[]{:S(2)}) collective-permute-start(bf16[8,4608]{1,0:T(8,128)(2,1)} %param.8), channel_id=1, source_target_pairs={{0,16},{1,17},{2,18},{3,19},{4,20},{5,21},{6,22},{7,23},{8,15},{9,... | collective-permute-start | bytes 221192 | tf_op jit(solution)/shard_map/ppermute | solution.py:28
  14.1 2.4 %collective-permute-done.5 = bf16[8,4608]{1,0:T(8,128)(2,1)S(1)} collective-permute-done((bf16[8,4608]{1,0:T(8,128)(2,1)}, bf16[8,4608]{1,0:T(8,128)(2,1)S(1)}, u32[]{:S(2)}, u32[]{:S(2)}) %collective-permute-start.5) | collective-permute-done | bytes 73760 | tf_op jit(solution)/shard_map/ppermute | solution.py:28
  17.3 4.0 %fusion.33 = bf16[64,512]{1,0:T(8,128)(2,1)S(1)} fusion(bf16[64,4608]{1,0:T(8,128)(2,1)S(1)} %constant_dynamic-update-slice_fusion, bf16[1,512,4608]{2,1,0:T(8,128)(2,1)} %param.9, bf16[8,8,512]{2,1,0:T(8,128)(2,1)S(1)} %gather_fusion, pred[8]{0:T(512)(128)(4,1)S(1)} %compare_and_fusion), kind=kOutput, calls=%fused_computation.25 | convolution fusion | flops 302120960 | bytes 5439496 | tf_op jit(solution)/shard_map/dot_general | solution.py:76
  33.0 6.7 %collective-permute-start.14 = (bf16[8,4608]{1,0:T(8,128)(2,1)S(1)}, bf16[8,4608]{1,0:T(8,128)(2,1)S(1)}, u32[]{:S(2)}, u32[]{:S(2)}) collective-permute-start(bf16[8,4608]{1,0:T(8,128)(2,1)S(1)} %get-tuple-element.7), channel_id=1, source_target_pairs={{0,24},{1,25},{2,26},{3,27},{4,28},{5,29},{6,30},{7,31},{8,0},{9,1... | collective-permute-start | bytes 221192 | tf_op jit(solution)/shard_map/ppermute | solution.py:34
  41.0 2.6 %collective-permute-start.18 = (bf16[8,4608]{1,0:T(8,128)(2,1)S(1)}, bf16[8,4608]{1,0:T(8,128)(2,1)S(1)}, u32[]{:S(2)}, u32[]{:S(2)}) collective-permute-start(bf16[8,4608]{1,0:T(8,128)(2,1)S(1)} %get-tuple-element.7), channel_id=1, source_target_pairs={{0,24},{1,25},{2,26},{3,27},{4,28},{5,29},{6,30},{7,31},{8,4},{9,5... | collective-permute-start | bytes 221192 | tf_op jit(solution)/shard_map/ppermute | solution.py:34
  46.4 4.3 %collective-permute-done.19 = bf16[8,4608]{1,0:T(8,128)(2,1)S(1)} collective-permute-done((bf16[8,4608]{1,0:T(8,128)(2,1)S(1)}, bf16[8,4608]{1,0:T(8,128)(2,1)S(1)}, u32[]{:S(2)}, u32[]{:S(2)}) %collective-permute-start.19) | collective-permute-done | bytes 73760 | tf_op jit(solution)/shard_map/ppermute | solution.py:34
  52.0 1.5 %fusion.30 = bf16[64,512]{1,0:T(8,128)(2,1)S(1)} fusion(bf16[64,4608]{1,0:T(8,128)(2,1)S(1)} %constant_dynamic-update-slice_fusion.8, bf16[1,512,4608]{2,1,0:T(8,128)(2,1)S(1)} %bitcast.61, bf16[8,8,512]{2,1,0:T(8,128)(2,1)S(1)} %gather_fusion, pred[8]{0:T(512)(128)(4,1)S(1)} %compare_and_fusion), kind=kOutput, calls=%fused_computation.24 | convolution fusion | flops 302120960 | bytes 5439496 | tf_op jit(solution)/shard_map/dot_general | solution.py:76
  55.5 2.1 %collective-permute-start.23 = (bf16[8,4608]{1,0:T(8,128)(2,1)S(1)}, bf16[8,4608]{1,0:T(8,128)(2,1)S(1)}, u32[]{:S(2)}, u32[]{:S(2)}) collective-permute-start(bf16[8,4608]{1,0:T(8,128)(2,1)S(1)} %get-tuple-element.29), channel_id=1, source_target_pairs={{0,2},{1,3},{2,0},{3,1},{4,6},{5,7},{6,4},{7,5},{8,24},{9,25},{10,... | collective-permute-start | bytes 221192 | tf_op jit(solution)/shard_map/ppermute | solution.py:28
  58.1 1.5 %collective-permute-start.25 = (bf16[8,4608]{1,0:T(8,128)(2,1)S(1)}, bf16[8,4608]{1,0:T(8,128)(2,1)S(1)}, u32[]{:S(2)}, u32[]{:S(2)}) collective-permute-start(bf16[8,4608]{1,0:T(8,128)(2,1)S(1)} %get-tuple-element.27), channel_id=1, source_target_pairs={{0,4},{1,5},{2,6},{3,7},{4,0},{5,1},{6,2},{7,3},{8,24},{9,25},{10,... | collective-permute-start | bytes 221192 | tf_op jit(solution)/shard_map/ppermute | solution.py:28
  59.6 1.8 %collective-permute-start.26 = (bf16[8,4608]{1,0:T(8,128)(2,1)S(1)}, bf16[8,4608]{1,0:T(8,128)(2,1)S(1)}, u32[]{:S(2)}, u32[]{:S(2)}) collective-permute-start(bf16[8,4608]{1,0:T(8,128)(2,1)S(1)} %get-tuple-element.26), channel_id=1, source_target_pairs={{0,5},{1,4},{2,7},{3,6},{4,1},{5,0},{6,3},{7,2},{8,24},{9,25},{10,... | collective-permute-start | bytes 221192 | tf_op jit(solution)/shard_map/ppermute | solution.py:28
  61.4 2.4 %collective-permute-start.27 = (bf16[8,4608]{1,0:T(8,128)(2,1)S(1)}, bf16[8,4608]{1,0:T(8,128)(2,1)S(1)}, u32[]{:S(2)}, u32[]{:S(2)}) collective-permute-start(bf16[8,4608]{1,0:T(8,128)(2,1)S(1)} %get-tuple-element.25), channel_id=1, source_target_pairs={{0,6},{1,7},{2,4},{3,5},{4,2},{5,3},{6,0},{7,1},{8,24},{9,25},{10,... | collective-permute-start | bytes 221192 | tf_op jit(solution)/shard_map/ppermute | solution.py:28
  63.9 1.9 %collective-permute-start.28 = (bf16[8,4608]{1,0:T(8,128)(2,1)S(1)}, bf16[8,4608]{1,0:T(8,128)(2,1)S(1)}, u32[]{:S(2)}, u32[]{:S(2)}) collective-permute-start(bf16[8,4608]{1,0:T(8,128)(2,1)S(1)} %get-tuple-element.24), channel_id=1, source_target_pairs={{0,7},{1,6},{2,5},{3,4},{4,3},{5,2},{6,1},{7,0},{8,24},{9,25},{10,... | collective-permute-start | bytes 221192 | tf_op jit(solution)/shard_map/ppermute | solution.py:28
  67.7 3.2 %collective-permute-done.28 = bf16[8,4608]{1,0:T(8,128)(2,1)S(1)} collective-permute-done((bf16[8,4608]{1,0:T(8,128)(2,1)S(1)}, bf16[8,4608]{1,0:T(8,128)(2,1)S(1)}, u32[]{:S(2)}, u32[]{:S(2)}) %collective-permute-start.28) | collective-permute-done | bytes 73760 | tf_op jit(solution)/shard_map/ppermute | solution.py:28
  71.1 1.9 %collective-permute-start.30 = (bf16[8,4608]{1,0:T(8,128)(2,1)S(1)}, bf16[8,4608]{1,0:T(8,128)(2,1)S(1)}, u32[]{:S(2)}, u32[]{:S(2)}) collective-permute-start(bf16[8,4608]{1,0:T(8,128)(2,1)S(1)} %get-tuple-element.5), channel_id=1, source_target_pairs={{0,25},{1,24},{2,27},{3,26},{4,29},{5,28},{6,31},{7,30},{8,0},{9,1... | collective-permute-start | bytes 221192 | tf_op jit(solution)/shard_map/ppermute | solution.py:34
  74.2 2.9 %collective-permute-start.34 = (bf16[8,4608]{1,0:T(8,128)(2,1)S(1)}, bf16[8,4608]{1,0:T(8,128)(2,1)S(1)}, u32[]{:S(2)}, u32[]{:S(2)}) collective-permute-start(bf16[8,4608]{1,0:T(8,128)(2,1)S(1)} %get-tuple-element.5), channel_id=1, source_target_pairs={{0,29},{1,28},{2,31},{3,30},{4,25},{5,24},{6,27},{7,26},{8,0},{9,1... | collective-permute-start | bytes 221192 | tf_op jit(solution)/shard_map/ppermute | solution.py:34
  77.2 1.5 %collective-permute-start.35 = (bf16[8,4608]{1,0:T(8,128)(2,1)S(1)}, bf16[8,4608]{1,0:T(8,128)(2,1)S(1)}, u32[]{:S(2)}, u32[]{:S(2)}) collective-permute-start(bf16[8,4608]{1,0:T(8,128)(2,1)S(1)} %get-tuple-element.5), channel_id=1, source_target_pairs={{0,30},{1,31},{2,28},{3,29},{4,26},{5,27},{6,24},{7,25},{8,0},{9,1... | collective-permute-start | bytes 221192 | tf_op jit(solution)/shard_map/ppermute | solution.py:34
  84.7 1.6 %collective-permute-start.37 = (bf16[8,4608]{1,0:T(8,128)(2,1)S(1)}, bf16[8,4608]{1,0:T(8,128)(2,1)S(1)}, u32[]{:S(2)}, u32[]{:S(2)}) collective-permute-start(bf16[8,4608]{1,0:T(8,128)(2,1)S(1)} %get-tuple-element.16), channel_id=1, source_target_pairs={{0,16},{1,17},{2,18},{3,19},{4,20},{5,21},{6,22},{7,23},{8,9},{9,8... | collective-permute-start | bytes 221192 | tf_op jit(solution)/shard_map/ppermute | solution.py:28
  95.6 5.9 %collective-permute-start.44 = (bf16[8,4608]{1,0:T(8,128)(2,1)S(1)}, bf16[8,4608]{1,0:T(8,128)(2,1)S(1)}, u32[]{:S(2)}, u32[]{:S(2)}) collective-permute-start(bf16[8,4608]{1,0:T(8,128)(2,1)S(1)} %get-tuple-element.3), channel_id=1, source_target_pairs={{0,24},{1,25},{2,26},{3,27},{4,28},{5,29},{6,30},{7,31},{8,0},{9,1... | collective-permute-start | bytes 221192 | tf_op jit(solution)/shard_map/ppermute | solution.py:34
  101.6 2.0 %collective-permute-start.46 = (bf16[8,4608]{1,0:T(8,128)(2,1)S(1)}, bf16[8,4608]{1,0:T(8,128)(2,1)S(1)}, u32[]{:S(2)}, u32[]{:S(2)}) collective-permute-start(bf16[8,4608]{1,0:T(8,128)(2,1)S(1)} %get-tuple-element.3), channel_id=1, source_target_pairs={{0,24},{1,25},{2,26},{3,27},{4,28},{5,29},{6,30},{7,31},{8,2},{9,3... | collective-permute-start | bytes 221192 | tf_op jit(solution)/shard_map/ppermute | solution.py:34
  104.0 1.6 %collective-permute-start.49 = (bf16[8,4608]{1,0:T(8,128)(2,1)S(1)}, bf16[8,4608]{1,0:T(8,128)(2,1)S(1)}, u32[]{:S(2)}, u32[]{:S(2)}) collective-permute-start(bf16[8,4608]{1,0:T(8,128)(2,1)S(1)} %get-tuple-element.3), channel_id=1, source_target_pairs={{0,24},{1,25},{2,26},{3,27},{4,28},{5,29},{6,30},{7,31},{8,5},{9,4... | collective-permute-start | bytes 221192 | tf_op jit(solution)/shard_map/ppermute | solution.py:34
  105.6 2.6 %collective-permute-start.50 = (bf16[8,4608]{1,0:T(8,128)(2,1)S(1)}, bf16[8,4608]{1,0:T(8,128)(2,1)S(1)}, u32[]{:S(2)}, u32[]{:S(2)}) collective-permute-start(bf16[8,4608]{1,0:T(8,128)(2,1)S(1)} %get-tuple-element.3), channel_id=1, source_target_pairs={{0,24},{1,25},{2,26},{3,27},{4,28},{5,29},{6,30},{7,31},{8,6},{9,7... | collective-permute-start | bytes 221192 | tf_op jit(solution)/shard_map/ppermute | solution.py:34
  111.8 3.0 %collective-permute-done.51 = bf16[8,4608]{1,0:T(8,128)(2,1)S(1)} collective-permute-done((bf16[8,4608]{1,0:T(8,128)(2,1)S(1)}, bf16[8,4608]{1,0:T(8,128)(2,1)S(1)}, u32[]{:S(2)}, u32[]{:S(2)}) %collective-permute-start.51) | collective-permute-done | bytes 73760 | tf_op jit(solution)/shard_map/ppermute | solution.py:34
  114.8 3.9 %fusion.24 = bf16[64,512]{1,0:T(8,128)(2,1)S(1)} fusion(bf16[64,4608]{1,0:T(8,128)(2,1)S(1)} %constant_dynamic-update-slice_fusion.24, bf16[1,512,4608]{2,1,0:T(8,128)(2,1)} %param.9, bf16[8,8,512]{2,1,0:T(8,128)(2,1)S(1)} %gather_fusion, pred[8]{0:T(512)(128)(4,1)S(1)} %compare_and_fusion), kind=kOutput, calls=%fused_computation.22 | convolution fusion | flops 302120960 | bytes 5439496 | tf_op jit(solution)/shard_map/dot_general | solution.py:76
  118.7 3.3 %convolution_convert_fusion = bf16[64,4608]{1,0:T(8,128)(2,1)S(1)} fusion(bf16[64,512]{1,0:T(8,128)(2,1)S(1)} %fusion.24, bf16[1,512,4608]{2,1,0:T(8,128)(2,1)} %param.10), kind=kOutput, calls=%fused_computation.2 | convolution fusion | flops 302284800 | bytes 5373952 | tf_op jit(solution)/shard_map/dot_general | solution.py:83
  122.9 2.6 %collective-permute-start.54 = (bf16[8,4608]{1,0:T(8,128)(2,1)S(1)}, bf16[8,4608]{1,0:T(8,128)(2,1)S(1)}, u32[]{:S(2)}, u32[]{:S(2)}) collective-permute-start(bf16[8,4608]{1,0:T(8,128)(2,1)S(1)} %get-tuple-element.14), channel_id=1, source_target_pairs={{0,3},{1,2},{2,1},{3,0},{4,7},{5,6},{6,5},{7,4},{8,24},{9,25},{10,... | collective-permute-start | bytes 221192 | tf_op jit(solution)/shard_map/ppermute | solution.py:28
  126.3 2.5 %collective-permute-start.56 = (bf16[8,4608]{1,0:T(8,128)(2,1)S(1)}, bf16[8,4608]{1,0:T(8,128)(2,1)S(1)}, u32[]{:S(2)}, u32[]{:S(2)}) collective-permute-start(bf16[8,4608]{1,0:T(8,128)(2,1)S(1)} %get-tuple-element.12), channel_id=1, source_target_pairs={{0,5},{1,4},{2,7},{3,6},{4,1},{5,0},{6,3},{7,2},{8,24},{9,25},{10,... | collective-permute-start | bytes 221192 | tf_op jit(solution)/shard_map/ppermute | solution.py:28
  129.4 2.6 %collective-permute-start.57 = (bf16[8,4608]{1,0:T(8,128)(2,1)S(1)}, bf16[8,4608]{1,0:T(8,128)(2,1)S(1)}, u32[]{:S(2)}, u32[]{:S(2)}) collective-permute-start(bf16[8,4608]{1,0:T(8,128)(2,1)S(1)} %get-tuple-element.11), channel_id=1, source_target_pairs={{0,6},{1,7},{2,4},{3,5},{4,2},{5,3},{6,0},{7,1},{8,24},{9,25},{10,... | collective-permute-start | bytes 221192 | tf_op jit(solution)/shard_map/ppermute | solution.py:28
  132.0 1.9 %collective-permute-start.58 = (bf16[8,4608]{1,0:T(8,128)(2,1)S(1)}, bf16[8,4608]{1,0:T(8,128)(2,1)S(1)}, u32[]{:S(2)}, u32[]{:S(2)}) collective-permute-start(bf16[8,4608]{1,0:T(8,128)(2,1)S(1)} %get-tuple-element.10), channel_id=1, source_target_pairs={{0,7},{1,6},{2,5},{3,4},{4,3},{5,2},{6,1},{7,0},{8,24},{9,25},{10,... | collective-permute-start | bytes 221192 | tf_op jit(solution)/shard_map/ppermute | solution.py:28
  135.7 3.3 %collective-permute-done.58 = bf16[8,4608]{1,0:T(8,128)(2,1)S(1)} collective-permute-done((bf16[8,4608]{1,0:T(8,128)(2,1)S(1)}, bf16[8,4608]{1,0:T(8,128)(2,1)S(1)}, u32[]{:S(2)}, u32[]{:S(2)}) %collective-permute-start.58) | collective-permute-done | bytes 73760 | tf_op jit(solution)/shard_map/ppermute | solution.py:28
  (156 shorter events, 52.0 us)
Async XLA Ops:
  0.6 11.2 %collective-permute-start = (bf16[8,4608]{1,0:T(8,128)(2,1)}, bf16[8,4608]{1,0:T(8,128)(2,1)S(1)}, u32[]{:S(2)}, u32[]{:S(2)}) collective-permute-start(bf16[8,4608]{1,0:T(8,128)(2,1)} %param.8), channel_id=1, source_target_pairs={{0,16},{1,17},{2,18},{3,19},{4,20},{5,21},{6,22},{7,23},{8,9},{9,8... | collective-permute-start | bytes 221192 | tf_op jit(solution)/shard_map/ppermute | solution.py:28
  3.7 8.3 %collective-permute-start.1 = (bf16[8,4608]{1,0:T(8,128)(2,1)}, bf16[8,4608]{1,0:T(8,128)(2,1)S(1)}, u32[]{:S(2)}, u32[]{:S(2)}) collective-permute-start(bf16[8,4608]{1,0:T(8,128)(2,1)} %param.8), channel_id=1, source_target_pairs={{0,16},{1,17},{2,18},{3,19},{4,20},{5,21},{6,22},{7,23},{8,10},{9,... | collective-permute-start | bytes 221192 | tf_op jit(solution)/shard_map/ppermute | solution.py:28
  3.7 10.3 %collective-permute-start.2 = (bf16[8,4608]{1,0:T(8,128)(2,1)}, bf16[8,4608]{1,0:T(8,128)(2,1)S(1)}, u32[]{:S(2)}, u32[]{:S(2)}) collective-permute-start(bf16[8,4608]{1,0:T(8,128)(2,1)} %param.8), channel_id=1, source_target_pairs={{0,16},{1,17},{2,18},{3,19},{4,20},{5,21},{6,22},{7,23},{8,11},{9,... | collective-permute-start | bytes 221192 | tf_op jit(solution)/shard_map/ppermute | solution.py:28
  5.7 8.4 %collective-permute-start.3 = (bf16[8,4608]{1,0:T(8,128)(2,1)}, bf16[8,4608]{1,0:T(8,128)(2,1)S(1)}, u32[]{:S(2)}, u32[]{:S(2)}) collective-permute-start(bf16[8,4608]{1,0:T(8,128)(2,1)} %param.8), channel_id=1, source_target_pairs={{0,16},{1,17},{2,18},{3,19},{4,20},{5,21},{6,22},{7,23},{8,12},{9,... | collective-permute-start | bytes 221192 | tf_op jit(solution)/shard_map/ppermute | solution.py:28
  5.8 8.3 %collective-permute-start.4 = (bf16[8,4608]{1,0:T(8,128)(2,1)}, bf16[8,4608]{1,0:T(8,128)(2,1)S(1)}, u32[]{:S(2)}, u32[]{:S(2)}) collective-permute-start(bf16[8,4608]{1,0:T(8,128)(2,1)} %param.8), channel_id=1, source_target_pairs={{0,16},{1,17},{2,18},{3,19},{4,20},{5,21},{6,22},{7,23},{8,13},{9,... | collective-permute-start | bytes 221192 | tf_op jit(solution)/shard_map/ppermute | solution.py:28
  33.0 10.6 %collective-permute-start.14 = (bf16[8,4608]{1,0:T(8,128)(2,1)S(1)}, bf16[8,4608]{1,0:T(8,128)(2,1)S(1)}, u32[]{:S(2)}, u32[]{:S(2)}) collective-permute-start(bf16[8,4608]{1,0:T(8,128)(2,1)S(1)} %get-tuple-element.7), channel_id=1, source_target_pairs={{0,24},{1,25},{2,26},{3,27},{4,28},{5,29},{6,30},{7,31},{8,0},{9,1... | collective-permute-start | bytes 221192 | tf_op jit(solution)/shard_map/ppermute | solution.py:34
  43.6 7.2 %collective-permute-start.19 = (bf16[8,4608]{1,0:T(8,128)(2,1)S(1)}, bf16[8,4608]{1,0:T(8,128)(2,1)S(1)}, u32[]{:S(2)}, u32[]{:S(2)}) collective-permute-start(bf16[8,4608]{1,0:T(8,128)(2,1)S(1)} %get-tuple-element.7), channel_id=1, source_target_pairs={{0,24},{1,25},{2,26},{3,27},{4,28},{5,29},{6,30},{7,31},{8,5},{9,4... | collective-permute-start | bytes 221192 | tf_op jit(solution)/shard_map/ppermute | solution.py:34
  43.8 6.9 %collective-permute-start.20 = (bf16[8,4608]{1,0:T(8,128)(2,1)S(1)}, bf16[8,4608]{1,0:T(8,128)(2,1)S(1)}, u32[]{:S(2)}, u32[]{:S(2)}) collective-permute-start(bf16[8,4608]{1,0:T(8,128)(2,1)S(1)} %get-tuple-element.7), channel_id=1, source_target_pairs={{0,24},{1,25},{2,26},{3,27},{4,28},{5,29},{6,30},{7,31},{8,6},{9,7... | collective-permute-start | bytes 221192 | tf_op jit(solution)/shard_map/ppermute | solution.py:34
  45.3 6.6 %collective-permute-start.21 = (bf16[8,4608]{1,0:T(8,128)(2,1)S(1)}, bf16[8,4608]{1,0:T(8,128)(2,1)S(1)}, u32[]{:S(2)}, u32[]{:S(2)}) collective-permute-start(bf16[8,4608]{1,0:T(8,128)(2,1)S(1)} %get-tuple-element.7), channel_id=1, source_target_pairs={{0,24},{1,25},{2,26},{3,27},{4,28},{5,29},{6,30},{7,31},{8,7},{9,6... | collective-permute-start | bytes 221192 | tf_op jit(solution)/shard_map/ppermute | solution.py:34
  54.5 6.9 %collective-permute-start.22 = (bf16[8,4608]{1,0:T(8,128)(2,1)S(1)}, bf16[8,4608]{1,0:T(8,128)(2,1)S(1)}, u32[]{:S(2)}, u32[]{:S(2)}) collective-permute-start(bf16[8,4608]{1,0:T(8,128)(2,1)S(1)} %get-tuple-element.23), channel_id=1, source_target_pairs={{0,1},{1,0},{2,3},{3,2},{4,5},{5,4},{6,7},{7,6},{8,24},{9,25},{10,... | collective-permute-start | bytes 221192 | tf_op jit(solution)/shard_map/ppermute | solution.py:28
  55.5 8.3 %collective-permute-start.23 = (bf16[8,4608]{1,0:T(8,128)(2,1)S(1)}, bf16[8,4608]{1,0:T(8,128)(2,1)S(1)}, u32[]{:S(2)}, u32[]{:S(2)}) collective-permute-start(bf16[8,4608]{1,0:T(8,128)(2,1)S(1)} %get-tuple-element.29), channel_id=1, source_target_pairs={{0,2},{1,3},{2,0},{3,1},{4,6},{5,7},{6,4},{7,5},{8,24},{9,25},{10,... | collective-permute-start | bytes 221192 | tf_op jit(solution)/shard_map/ppermute | solution.py:28
  57.6 8.1 %collective-permute-start.24 = (bf16[8,4608]{1,0:T(8,128)(2,1)S(1)}, bf16[8,4608]{1,0:T(8,128)(2,1)S(1)}, u32[]{:S(2)}, u32[]{:S(2)}) collective-permute-start(bf16[8,4608]{1,0:T(8,128)(2,1)S(1)} %get-tuple-element.28), channel_id=1, source_target_pairs={{0,3},{1,2},{2,1},{3,0},{4,7},{5,6},{6,5},{7,4},{8,24},{9,25},{10,... | collective-permute-start | bytes 221192 | tf_op jit(solution)/shard_map/ppermute | solution.py:28
  58.1 7.7 %collective-permute-start.25 = (bf16[8,4608]{1,0:T(8,128)(2,1)S(1)}, bf16[8,4608]{1,0:T(8,128)(2,1)S(1)}, u32[]{:S(2)}, u32[]{:S(2)}) collective-permute-start(bf16[8,4608]{1,0:T(8,128)(2,1)S(1)} %get-tuple-element.27), channel_id=1, source_target_pairs={{0,4},{1,5},{2,6},{3,7},{4,0},{5,1},{6,2},{7,3},{8,24},{9,25},{10,... | collective-permute-start | bytes 221192 | tf_op jit(solution)/shard_map/ppermute | solution.py:28
  59.6 7.2 %collective-permute-start.26 = (bf16[8,4608]{1,0:T(8,128)(2,1)S(1)}, bf16[8,4608]{1,0:T(8,128)(2,1)S(1)}, u32[]{:S(2)}, u32[]{:S(2)}) collective-permute-start(bf16[8,4608]{1,0:T(8,128)(2,1)S(1)} %get-tuple-element.26), channel_id=1, source_target_pairs={{0,5},{1,4},{2,7},{3,6},{4,1},{5,0},{6,3},{7,2},{8,24},{9,25},{10,... | collective-permute-start | bytes 221192 | tf_op jit(solution)/shard_map/ppermute | solution.py:28
  61.4 6.3 %collective-permute-start.27 = (bf16[8,4608]{1,0:T(8,128)(2,1)S(1)}, bf16[8,4608]{1,0:T(8,128)(2,1)S(1)}, u32[]{:S(2)}, u32[]{:S(2)}) collective-permute-start(bf16[8,4608]{1,0:T(8,128)(2,1)S(1)} %get-tuple-element.25), channel_id=1, source_target_pairs={{0,6},{1,7},{2,4},{3,5},{4,2},{5,3},{6,0},{7,1},{8,24},{9,25},{10,... | collective-permute-start | bytes 221192 | tf_op jit(solution)/shard_map/ppermute | solution.py:28
  63.9 7.1 %collective-permute-start.28 = (bf16[8,4608]{1,0:T(8,128)(2,1)S(1)}, bf16[8,4608]{1,0:T(8,128)(2,1)S(1)}, u32[]{:S(2)}, u32[]{:S(2)}) collective-permute-start(bf16[8,4608]{1,0:T(8,128)(2,1)S(1)} %get-tuple-element.24), channel_id=1, source_target_pairs={{0,7},{1,6},{2,5},{3,4},{4,3},{5,2},{6,1},{7,0},{8,24},{9,25},{10,... | collective-permute-start | bytes 221192 | tf_op jit(solution)/shard_map/ppermute | solution.py:28
  71.1 6.1 %collective-permute-start.30 = (bf16[8,4608]{1,0:T(8,128)(2,1)S(1)}, bf16[8,4608]{1,0:T(8,128)(2,1)S(1)}, u32[]{:S(2)}, u32[]{:S(2)}) collective-permute-start(bf16[8,4608]{1,0:T(8,128)(2,1)S(1)} %get-tuple-element.5), channel_id=1, source_target_pairs={{0,25},{1,24},{2,27},{3,26},{4,29},{5,28},{6,31},{7,30},{8,0},{9,1... | collective-permute-start | bytes 221192 | tf_op jit(solution)/shard_map/ppermute | solution.py:34
  73.0 7.2 %collective-permute-start.32 = (bf16[8,4608]{1,0:T(8,128)(2,1)S(1)}, bf16[8,4608]{1,0:T(8,128)(2,1)S(1)}, u32[]{:S(2)}, u32[]{:S(2)}) collective-permute-start(bf16[8,4608]{1,0:T(8,128)(2,1)S(1)} %get-tuple-element.5), channel_id=1, source_target_pairs={{0,27},{1,26},{2,25},{3,24},{4,31},{5,30},{6,29},{7,28},{8,0},{9,1... | collective-permute-start | bytes 221192 | tf_op jit(solution)/shard_map/ppermute | solution.py:34
  73.0 7.3 %collective-permute-start.33 = (bf16[8,4608]{1,0:T(8,128)(2,1)S(1)}, bf16[8,4608]{1,0:T(8,128)(2,1)S(1)}, u32[]{:S(2)}, u32[]{:S(2)}) collective-permute-start(bf16[8,4608]{1,0:T(8,128)(2,1)S(1)} %get-tuple-element.5), channel_id=1, source_target_pairs={{0,28},{1,29},{2,30},{3,31},{4,24},{5,25},{6,26},{7,27},{8,0},{9,1... | collective-permute-start | bytes 221192 | tf_op jit(solution)/shard_map/ppermute | solution.py:34
  74.2 6.0 %collective-permute-start.34 = (bf16[8,4608]{1,0:T(8,128)(2,1)S(1)}, bf16[8,4608]{1,0:T(8,128)(2,1)S(1)}, u32[]{:S(2)}, u32[]{:S(2)}) collective-permute-start(bf16[8,4608]{1,0:T(8,128)(2,1)S(1)} %get-tuple-element.5), channel_id=1, source_target_pairs={{0,29},{1,28},{2,31},{3,30},{4,25},{5,24},{6,27},{7,26},{8,0},{9,1... | collective-permute-start | bytes 221192 | tf_op jit(solution)/shard_map/ppermute | solution.py:34
  95.6 8.4 %collective-permute-start.44 = (bf16[8,4608]{1,0:T(8,128)(2,1)S(1)}, bf16[8,4608]{1,0:T(8,128)(2,1)S(1)}, u32[]{:S(2)}, u32[]{:S(2)}) collective-permute-start(bf16[8,4608]{1,0:T(8,128)(2,1)S(1)} %get-tuple-element.3), channel_id=1, source_target_pairs={{0,24},{1,25},{2,26},{3,27},{4,28},{5,29},{6,30},{7,31},{8,0},{9,1... | collective-permute-start | bytes 221192 | tf_op jit(solution)/shard_map/ppermute | solution.py:34
  101.6 6.6 %collective-permute-start.46 = (bf16[8,4608]{1,0:T(8,128)(2,1)S(1)}, bf16[8,4608]{1,0:T(8,128)(2,1)S(1)}, u32[]{:S(2)}, u32[]{:S(2)}) collective-permute-start(bf16[8,4608]{1,0:T(8,128)(2,1)S(1)} %get-tuple-element.3), channel_id=1, source_target_pairs={{0,24},{1,25},{2,26},{3,27},{4,28},{5,29},{6,30},{7,31},{8,2},{9,3... | collective-permute-start | bytes 221192 | tf_op jit(solution)/shard_map/ppermute | solution.py:34
  104.0 6.5 %collective-permute-start.49 = (bf16[8,4608]{1,0:T(8,128)(2,1)S(1)}, bf16[8,4608]{1,0:T(8,128)(2,1)S(1)}, u32[]{:S(2)}, u32[]{:S(2)}) collective-permute-start(bf16[8,4608]{1,0:T(8,128)(2,1)S(1)} %get-tuple-element.3), channel_id=1, source_target_pairs={{0,24},{1,25},{2,26},{3,27},{4,28},{5,29},{6,30},{7,31},{8,5},{9,4... | collective-permute-start | bytes 221192 | tf_op jit(solution)/shard_map/ppermute | solution.py:34
  105.6 6.2 %collective-permute-start.50 = (bf16[8,4608]{1,0:T(8,128)(2,1)S(1)}, bf16[8,4608]{1,0:T(8,128)(2,1)S(1)}, u32[]{:S(2)}, u32[]{:S(2)}) collective-permute-start(bf16[8,4608]{1,0:T(8,128)(2,1)S(1)} %get-tuple-element.3), channel_id=1, source_target_pairs={{0,24},{1,25},{2,26},{3,27},{4,28},{5,29},{6,30},{7,31},{8,6},{9,7... | collective-permute-start | bytes 221192 | tf_op jit(solution)/shard_map/ppermute | solution.py:34
  108.3 6.5 %collective-permute-start.51 = (bf16[8,4608]{1,0:T(8,128)(2,1)S(1)}, bf16[8,4608]{1,0:T(8,128)(2,1)S(1)}, u32[]{:S(2)}, u32[]{:S(2)}) collective-permute-start(bf16[8,4608]{1,0:T(8,128)(2,1)S(1)} %get-tuple-element.3), channel_id=1, source_target_pairs={{0,24},{1,25},{2,26},{3,27},{4,28},{5,29},{6,30},{7,31},{8,7},{9,6... | collective-permute-start | bytes 221192 | tf_op jit(solution)/shard_map/ppermute | solution.py:34
  122.0 7.4 %collective-permute-start.52 = (bf16[8,4608]{1,0:T(8,128)(2,1)S(1)}, bf16[8,4608]{1,0:T(8,128)(2,1)S(1)}, u32[]{:S(2)}, u32[]{:S(2)}) collective-permute-start(bf16[8,4608]{1,0:T(8,128)(2,1)S(1)} %get-tuple-element.9), channel_id=1, source_target_pairs={{0,1},{1,0},{2,3},{3,2},{4,5},{5,4},{6,7},{7,6},{8,24},{9,25},{10,... | collective-permute-start | bytes 221192 | tf_op jit(solution)/shard_map/ppermute | solution.py:28
  122.9 9.0 %collective-permute-start.53 = (bf16[8,4608]{1,0:T(8,128)(2,1)S(1)}, bf16[8,4608]{1,0:T(8,128)(2,1)S(1)}, u32[]{:S(2)}, u32[]{:S(2)}) collective-permute-start(bf16[8,4608]{1,0:T(8,128)(2,1)S(1)} %get-tuple-element.15), channel_id=1, source_target_pairs={{0,2},{1,3},{2,0},{3,1},{4,6},{5,7},{6,4},{7,5},{8,24},{9,25},{10,... | collective-permute-start | bytes 221192 | tf_op jit(solution)/shard_map/ppermute | solution.py:28
  122.9 11.6 %collective-permute-start.54 = (bf16[8,4608]{1,0:T(8,128)(2,1)S(1)}, bf16[8,4608]{1,0:T(8,128)(2,1)S(1)}, u32[]{:S(2)}, u32[]{:S(2)}) collective-permute-start(bf16[8,4608]{1,0:T(8,128)(2,1)S(1)} %get-tuple-element.14), channel_id=1, source_target_pairs={{0,3},{1,2},{2,1},{3,0},{4,7},{5,6},{6,5},{7,4},{8,24},{9,25},{10,... | collective-permute-start | bytes 221192 | tf_op jit(solution)/shard_map/ppermute | solution.py:28
  125.6 9.0 %collective-permute-start.55 = (bf16[8,4608]{1,0:T(8,128)(2,1)S(1)}, bf16[8,4608]{1,0:T(8,128)(2,1)S(1)}, u32[]{:S(2)}, u32[]{:S(2)}) collective-permute-start(bf16[8,4608]{1,0:T(8,128)(2,1)S(1)} %get-tuple-element.13), channel_id=1, source_target_pairs={{0,4},{1,5},{2,6},{3,7},{4,0},{5,1},{6,2},{7,3},{8,24},{9,25},{10,... | collective-permute-start | bytes 221192 | tf_op jit(solution)/shard_map/ppermute | solution.py:28
  126.3 8.3 %collective-permute-start.56 = (bf16[8,4608]{1,0:T(8,128)(2,1)S(1)}, bf16[8,4608]{1,0:T(8,128)(2,1)S(1)}, u32[]{:S(2)}, u32[]{:S(2)}) collective-permute-start(bf16[8,4608]{1,0:T(8,128)(2,1)S(1)} %get-tuple-element.12), channel_id=1, source_target_pairs={{0,5},{1,4},{2,7},{3,6},{4,1},{5,0},{6,3},{7,2},{8,24},{9,25},{10,... | collective-permute-start | bytes 221192 | tf_op jit(solution)/shard_map/ppermute | solution.py:28
  129.4 6.3 %collective-permute-start.57 = (bf16[8,4608]{1,0:T(8,128)(2,1)S(1)}, bf16[8,4608]{1,0:T(8,128)(2,1)S(1)}, u32[]{:S(2)}, u32[]{:S(2)}) collective-permute-start(bf16[8,4608]{1,0:T(8,128)(2,1)S(1)} %get-tuple-element.11), channel_id=1, source_target_pairs={{0,6},{1,7},{2,4},{3,5},{4,2},{5,3},{6,0},{7,1},{8,24},{9,25},{10,... | collective-permute-start | bytes 221192 | tf_op jit(solution)/shard_map/ppermute | solution.py:28
  132.0 7.1 %collective-permute-start.58 = (bf16[8,4608]{1,0:T(8,128)(2,1)S(1)}, bf16[8,4608]{1,0:T(8,128)(2,1)S(1)}, u32[]{:S(2)}, u32[]{:S(2)}) collective-permute-start(bf16[8,4608]{1,0:T(8,128)(2,1)S(1)} %get-tuple-element.10), channel_id=1, source_target_pairs={{0,7},{1,6},{2,5},{3,4},{4,3},{5,2},{6,1},{7,0},{8,24},{9,25},{10,... | collective-permute-start | bytes 221192 | tf_op jit(solution)/shard_map/ppermute | solution.py:28
  (31 other events, 218.7 us)

commit v2 on v1

v2 whole, which is shorter than its diff:
```python
import functools

import jax
import jax.numpy as jnp
from jax import lax
from jax.experimental import pallas as pl
from jax.experimental.pallas import tpu as pltpu
from jax.sharding import PartitionSpec as P

BLOCK = 128
AXES = ("layer", "feat")


def fetch(source, target, sems, chunks):
    rows = target.shape[0] // chunks
    moves = []
    for i in range(chunks):
        part = pl.ds(i * rows, rows)
        moves.append(pltpu.make_async_copy(source.at[0, part], target.at[part], sems.at[i]))
    return moves


CHUNKS = 4


def stage_kernel(
    by_xor, act_ref, ids_ref, counts_ref, dec_ref, enc_ref, gate_ref, attr_ref, dec_out, enc_out,
    act, ids, counts, sems, dec_sems, enc_sems,
):
    del attr_ref
    top = lax.axis_index("layer") == lax.axis_size("layer") - 1
    weights = fetch(dec_ref, dec_out, dec_sems, CHUNKS) + fetch(enc_ref, enc_out, enc_sems, CHUNKS)
    small = [
        pltpu.make_async_copy(counts_ref, counts, sems.at[0]),
        pltpu.make_async_copy(ids_ref, ids, sems.at[1]),
        pltpu.make_async_copy(act_ref, act, sems.at[2]),
    ]
    for move in small:
        move.start()

    @pl.when(top)
    def _():
        for move in weights:
            move.start()

    for move in small:
        move.wait()
    feat_index = lax.axis_index("feat")
    tiles, tok_dev, feat_dev = act_ref.shape
    blk_dev = feat_dev // BLOCK
    width = ids_ref.shape[2]
    lane = lax.broadcasted_iota(jnp.int32, (1, width), 1)
    for k in range(tiles):
        tile = feat_index ^ k if by_xor else k
        listed = lane < counts[0, tile]
        mask = []
        for block in range(blk_dev):
            match = (ids[0, pl.ds(tile, 1), :] == feat_index * blk_dev + block) & listed
            hit = jnp.max(jnp.where(match, 1.0, 0.0), axis=1, keepdims=True)
            mask.append(jnp.broadcast_to(hit, (1, BLOCK)))
        row = jnp.concatenate(mask, axis=1)
        gate_ref[k * tok_dev : (k + 1) * tok_dev, :] = act[tile].astype(jnp.float32) * row

    @pl.when(top)
    def _():
        for move in weights:
            move.wait()


def attribute_kernel(layer, tiles, *refs):
    rows, (gate_ref, dec, enc), refs = refs[:tiles], refs[tiles : tiles + 3], refs[tiles + 3 :]
    if layer:
        dec_ref, enc_ref = refs[:2]
        refs = refs[2:]
    refs = refs[1:]
    attr_ref, parts, refs = refs[0], refs[1 : tiles + 1], refs[tiles + 1 :]
    layer_index = lax.axis_index("layer")
    if layer:
        dec_out, enc_out, h_ref, a_ref, b_ref, sem, dec_sems, enc_sems = refs
        weights = fetch(dec_ref, dec_out, dec_sems, CHUNKS)
        weights += fetch(enc_ref, enc_out, enc_sems, CHUNKS)

        @pl.when(layer_index == layer - 1)
        def _():
            for move in weights:
                move.start()
            for move in weights:
                move.wait()
    else:
        h_ref, a_ref, b_ref, sem = refs
    tok_dev, width = rows[0].shape
    feat_dev = dec.shape[0]
    feat_index = lax.axis_index("feat")

    @pl.when(layer_index == layer)
    def _():
        for k in range(0, tiles, 2):
            pair = jnp.concatenate([rows[k][...], rows[k + 1][...]], axis=0)
            h_ref[k * tok_dev : (k + 2) * tok_dev, :] = pair
        cut = 256
        for f in range(0, feat_dev, cut):
            scores = lax.dot_general(
                h_ref[...],
                dec[f : f + cut, :],
                (((1,), (1,)), ((), ())),
                preferred_element_type=jnp.float32,
            )
            attributed = scores * gate_ref[:, f : f + cut]
            a_ref[:, f : f + cut] = attributed.astype(jnp.bfloat16)
            for k in range(tiles):
                block = attributed[k * tok_dev : (k + 1) * tok_dev, :]
                b_ref[feat_index ^ k, :, f : f + cut] = block.astype(jnp.bfloat16)
        done = pltpu.make_async_copy(b_ref, attr_ref, sem.at[0])
        done.start()
        cut = 512
        for c in range(0, width, cut):
            product = jnp.dot(
                a_ref[...], enc[:, c : c + cut], preferred_element_type=jnp.float32
            )
            for k in range(tiles):
                part = product[k * tok_dev : (k + 1) * tok_dev, :]
                parts[k][:, c : c + cut] = part.astype(jnp.bfloat16)
        done.wait()


def body(top_grad, decoder, encoder, activations, block_ids, block_counts):
    layers = lax.axis_size("layer")
    tiles = lax.axis_size("feat")
    layer_index = lax.axis_index("layer")
    feat_index = lax.axis_index("feat")
    feat_dev, width = decoder.shape[1:]
    tok_dev = top_grad.shape[0]
    direct = tiles <= 8

    vmem = pl.BlockSpec(memory_space=pltpu.VMEM)
    hbm = pl.BlockSpec(memory_space=pl.ANY)
    weight_bytes = 4 * feat_dev * width
    dec_hbm = pltpu.with_memory_space_constraint(decoder, pltpu.HBM)
    enc_hbm = pltpu.with_memory_space_constraint(encoder, pltpu.HBM)
    staged = [
        pltpu.VMEM((feat_dev, width), decoder.dtype),
        pltpu.VMEM((feat_dev, width), encoder.dtype),
    ]
    chunk_sems = [pltpu.SemaphoreType.DMA((CHUNKS,))] * 2

    act_tiles = activations.reshape(tiles, tok_dev, feat_dev)
    gate, attr, dec, enc = pl.pallas_call(
        functools.partial(stage_kernel, direct),
        out_shape=(
            jax.ShapeDtypeStruct((tiles * tok_dev, feat_dev), jnp.float32),
            pltpu.HBM(act_tiles.shape, act_tiles.dtype),
            *staged,
        ),
        in_specs=[hbm] * 5,
        out_specs=(vmem, hbm, hbm, hbm),
        scratch_shapes=[
            pltpu.VMEM(act_tiles.shape, act_tiles.dtype),
            pltpu.VMEM(block_ids.shape, block_ids.dtype),
            pltpu.SMEM(block_counts.shape, block_counts.dtype),
            pltpu.SemaphoreType.DMA((3,)),
            *chunk_sems,
        ],
        compiler_params=pltpu.CompilerParams(vmem_limit_bytes=8 * 2**20),
        cost_estimate=pl.CostEstimate(
            flops=0, bytes_accessed=2 * weight_bytes, transcendentals=0
        ),
    )(
        pltpu.with_memory_space_constraint(act_tiles, pltpu.HBM),
        pltpu.with_memory_space_constraint(block_ids, pltpu.HBM),
        pltpu.with_memory_space_constraint(block_counts, pltpu.HBM),
        dec_hbm,
        enc_hbm,
    )

    def link(layer, to_layer, k):
        return [(layer * tiles + i, (to_layer % layers) * tiles + (i ^ k)) for i in range(tiles)]

    def within(value, k):
        pairs = []
        for l in range(layers):
            pairs += link(l, l, k) if l % 2 else link(l, l + 2, 0)
        return lax.ppermute(value, AXES, pairs)

    def down(value, k):
        pairs = []
        for l in range(layers):
            pairs += link(l, l - 1, k) if l % 2 else link(l, l + 1, 0)
        return lax.ppermute(value, AXES, pairs)

    def up(value, k):
        pairs = []
        for l in range(layers):
            pairs += link(l, l - 1, 0) if l % 2 else link(l, l + 1, k)
        return lax.ppermute(value, AXES, pairs)

    def skip(value, top, k):
        pairs = link(top, top - 2, k) + link(top - 2, top - 3, 0)
        pairs += link(top - 3, top - 1, 0) + link(top - 1, top, 0)
        for l in range(layers):
            if not top - 3 <= l <= top:
                pairs += link(l, l ^ 1, 0)
        return lax.ppermute(value, AXES, pairs)

    def attribute_direct(layer, rows, attr, dec, enc):
        block = jax.ShapeDtypeStruct((tok_dev, width), jnp.bfloat16)
        more = 2 if layer else 0
        outs = pl.pallas_call(
            functools.partial(attribute_kernel, layer, tiles),
            out_shape=(
                pltpu.HBM(attr.shape, attr.dtype),
                *[block] * tiles,
                *staged[:more],
            ),
            in_specs=[vmem] * (tiles + 3) + [hbm] * (more + 1),
            out_specs=(hbm,) + (vmem,) * tiles + (hbm,) * more,
            scratch_shapes=[
                pltpu.VMEM((tiles * tok_dev, width), jnp.bfloat16),
                pltpu.VMEM((tiles * tok_dev, feat_dev), jnp.bfloat16),
                pltpu.VMEM(attr.shape, attr.dtype),
                pltpu.SemaphoreType.DMA((1,)),
                *chunk_sems[:more],
            ],
            input_output_aliases={tiles + 3 + more: 0},
            compiler_params=pltpu.CompilerParams(vmem_limit_bytes=8 * 2**20),
            cost_estimate=pl.CostEstimate(
                flops=4 * tiles * tok_dev * feat_dev * width,
                bytes_accessed=weight_bytes,
                transcendentals=0,
            ),
        )(
            *rows,
            gate,
            pltpu.with_memory_space_constraint(dec, pltpu.VMEM),
            pltpu.with_memory_space_constraint(enc, pltpu.VMEM),
            *[dec_hbm, enc_hbm][:more],
            attr,
        )
        return outs[0], list(outs[1 : tiles + 1]), list(outs[tiles + 1 :]) or [dec, enc]

    def attribute(rows):
        scores = lax.dot_general(
            jnp.concatenate(rows, 0),
            decoder[0],
            (((1,), (1,)), ((), ())),
            preferred_element_type=jnp.float32,
        )
        attributed = (scores * gate).astype(jnp.bfloat16)
        part = jnp.dot(attributed, encoder[0], preferred_element_type=jnp.float32).astype(jnp.bfloat16)
        return attributed, part.reshape(tiles, tok_dev, width)

    def total(start, terms):
        for term in terms:
            start = start + term.astype(jnp.float32)
        return start

    def exchanged(values):
        return list(lax.all_to_all(values, "feat", 0, 0, tiled=True))

    grads = [None] * layers
    grad = top_grad.astype(jnp.float32)
    sent = top_grad
    if direct:
        for high in range(layers - 1, 0, -2):
            if high == layers - 1:
                rows = [sent] + [within(sent, k) for k in range(1, tiles)]
            else:
                rows = [skip(sent, high + 2, k) for k in range(tiles)]
                grad = rows[0].astype(jnp.float32)
            attr, part, (dec, enc) = attribute_direct(high, rows, attr, dec, enc)
            grad = total(grad, [part[0]] + [within(part[k], k) for k in range(1, tiles)])
            grads[high] = grad
            sent = grad.astype(jnp.bfloat16)
            rows = [down(sent, k) for k in range(tiles)]
            low = high - 1
            attr, part, (dec, enc) = attribute_direct(low, rows, attr, dec, enc)
            grad = total(grad, [up(part[k], k) for k in range(tiles)])
            grads[high - 1] = grad
            sent = grad.astype(jnp.bfloat16)
        lower = grads[0]
        for high in range(3, layers, 2):
            lower = jnp.where(layer_index == high, grads[high - 1], lower)
        lower = down(lower, 0)
        grad = jnp.where(layer_index % 2 == 1, grad, lower)
        for high in range(1, layers, 2):
            grad = jnp.where(layer_index == high, grads[high], grad)
    else:
        for layer in range(layers - 1, -1, -1):
            rows = exchanged(jnp.broadcast_to(sent[None], (tiles,) + sent.shape))
            attributed, part = attribute(rows)
            attributed = attributed.reshape(attr.shape)
            attr = jnp.where(layer_index == layer, attributed, attr)
            grads[layer] = grad = total(grad, exchanged(part))
            pairs = [q for l in range(layers) for q in link(l, l - 1, 0)]
            sent = lax.ppermute(grad.astype(jnp.bfloat16), AXES, pairs)
            grad = sent.astype(jnp.float32)
        grad = grads[0]
        for layer in range(1, layers):
            grad = jnp.where(layer_index == layer, grads[layer], grad)
    return attr.reshape(1, tiles * tok_dev, feat_dev), grad[None]


def solution(mesh):
    placed = (
        P("feat", None),
        P("layer", "feat", None),
        P("layer", "feat", None),
        P("layer", None, "feat"),
        P("layer", None, None),
        P("layer", None),
    )
    return jax.shard_map(
        body,
        mesh=mesh,
        in_specs=placed,
        out_specs=(P("layer", None, "feat"), P("layer", "feat", None)),
        check_vma=False,
    )
```

time: 140 us -> 115 us (0.82)
  matrix products: 17.1 us -> 0 us
  Pallas kernels: 0 us -> 7.51 us
  starting transfers between devices: 82.5 us -> 75.6 us
  other arithmetic: 4.32 us -> 1.08 us
  local copies, waits for them, and re-layouts: 2.46 us -> 0.01 us
  waiting for transfers between devices: 32.3 us -> 30.1 us
    ppermute x35 -> x21, starting transfers between devices: 46.8 us -> 26.4 us  [within(): return lax.ppermute(value, AXES, pairs)]
    dot_general x8 -> x0, matrix products: 17.1 us -> none  [the longest x4 11 us: body(): lax.dot_general(jnp.concatenate(rows, 0), dec, (((1,), (1,)), ((), ())),...]
    ppermute x24 -> x41, starting transfers between devices: 35.7 us -> 49.1 us  [the longest x17 20.4 us: down(): return lax.ppermute(value, AXES, pairs)]
    ppermute x35 -> x21, waiting for transfers between devices: 19 us -> 9.59 us  [within(): return lax.ppermute(value, AXES, pairs)]
    pallas_call x0 -> x5, Pallas kernels: none -> 7.51 us  [the longest x4 6.41 us: attribute_direct(): pl.pallas_call(functools.partial(attribute_kernel, layer, tiles), out_sha...]
    ppermute x24 -> x41, waiting for transfers between devices: 13.3 us -> 20.5 us  [the longest x17 14.1 us: down(): return lax.ppermute(value, AXES, pairs)]
  transfers between devices with their start and end apart: 59 -> 62, of which waited for: 23 -> 29; matrix products, arithmetic and copies ran while one was open for 4% -> 0% of each run, Pallas kernels for 0% -> 1%
where the time goes in v2:
time: 115 us
  starting transfers between devices  75.6 us (66%)
  waiting for transfers between devices  30.1 us (26%)
  Pallas kernels  7.51 us (7%)
    ppermute x21, starting transfers between devices, within(): return lax.ppermute(value, AXES, pairs)  26.4 us
    ppermute x17, starting transfers between devices, down(): return lax.ppermute(value, AXES, pairs)  20.4 us
    ppermute x16, starting transfers between devices, up(): return lax.ppermute(value, AXES, pairs)  15.3 us
    ppermute x17, waiting for transfers between devices, down(): return lax.ppermute(value, AXES, pairs)  14.1 us
    ppermute x8, starting transfers between devices, skip(): return lax.ppermute(value, AXES, pairs)  13.4 us
    ppermute x21, waiting for transfers between devices, within(): return lax.ppermute(value, AXES, pairs)  9.59 us
    pallas_call x4, Pallas kernels, attribute_direct(): pl.pallas_call(functools.partial(attribute_kernel, layer, tiles), out_sha...  6.41 us
    ppermute x16, waiting for transfers between devices, up(): return lax.ppermute(value, AXES, pairs)  3.97 us
  transfers between devices with their start and end apart: 62, of which 29 were waited for; matrix products, arithmetic and copies ran while one was open for 0% of the time, Pallas kernels for 1%

profile of v2, /device:TPU:0, one launch (start us, length us, event | category | flops | bytes accessed | tf_op | source)
XLA Modules:
  0.0 115.0 jit_solution(10128512826174067690)
XLA Ops:
  0.6 3.0 %collective-permute-start = (bf16[8,4608]{1,0:T(8,128)(2,1)}, bf16[8,4608]{1,0:T(8,128)(2,1)S(1)}, u32[]{:S(2)}, u32[]{:S(2)}) collective-permute-start(bf16[8,4608]{1,0:T(8,128)(2,1)} %refs_0_.1), channel_id=1, source_target_pairs={{0,16},{1,17},{2,18},{3,19},{4,20},{5,21},{6,22},{7,23},{8,9},{9,8... | collective-permute-start | bytes 221192 | tf_op jit(solution)/shard_map/ppermute | solution.py:182
  3.7 1.9 %collective-permute-start.2 = (bf16[8,4608]{1,0:T(8,128)(2,1)}, bf16[8,4608]{1,0:T(8,128)(2,1)S(1)}, u32[]{:S(2)}, u32[]{:S(2)}) collective-permute-start(bf16[8,4608]{1,0:T(8,128)(2,1)} %refs_0_.1), channel_id=1, source_target_pairs={{0,16},{1,17},{2,18},{3,19},{4,20},{5,21},{6,22},{7,23},{8,11},{9,... | collective-permute-start | bytes 221192 | tf_op jit(solution)/shard_map/ppermute | solution.py:182
  5.8 1.9 %collective-permute-start.4 = (bf16[8,4608]{1,0:T(8,128)(2,1)}, bf16[8,4608]{1,0:T(8,128)(2,1)S(1)}, u32[]{:S(2)}, u32[]{:S(2)}) collective-permute-start(bf16[8,4608]{1,0:T(8,128)(2,1)} %refs_0_.1), channel_id=1, source_target_pairs={{0,16},{1,17},{2,18},{3,19},{4,20},{5,21},{6,22},{7,23},{8,13},{9,... | collective-permute-start | bytes 221192 | tf_op jit(solution)/shard_map/ppermute | solution.py:182
  8.2 1.5 %collective-permute-start.6 = (bf16[8,4608]{1,0:T(8,128)(2,1)}, bf16[8,4608]{1,0:T(8,128)(2,1)S(1)}, u32[]{:S(2)}, u32[]{:S(2)}) collective-permute-start(bf16[8,4608]{1,0:T(8,128)(2,1)} %refs_0_.1), channel_id=1, source_target_pairs={{0,16},{1,17},{2,18},{3,19},{4,20},{5,21},{6,22},{7,23},{8,15},{9,... | collective-permute-start | bytes 221192 | tf_op jit(solution)/shard_map/ppermute | solution.py:182
  13.2 5.0 %collective-permute-start.10 = (bf16[8,4608]{1,0:T(8,128)(2,1)S(1)}, bf16[8,4608]{1,0:T(8,128)(2,1)S(1)}, u32[]{:S(2)}, u32[]{:S(2)}) collective-permute-start(bf16[8,4608]{1,0:T(8,128)(2,1)S(1)} %get-tuple-element.56), channel_id=1, source_target_pairs={{0,16},{1,17},{2,18},{3,19},{4,20},{5,21},{6,22},{7,23},{8,12},{9,... | collective-permute-start | bytes 221192 | tf_op jit(solution)/shard_map/ppermute | solution.py:182
  18.3 1.9 %collective-permute-start.12 = (bf16[8,4608]{1,0:T(8,128)(2,1)S(1)}, bf16[8,4608]{1,0:T(8,128)(2,1)S(1)}, u32[]{:S(2)}, u32[]{:S(2)}) collective-permute-start(bf16[8,4608]{1,0:T(8,128)(2,1)S(1)} %get-tuple-element.58), channel_id=1, source_target_pairs={{0,16},{1,17},{2,18},{3,19},{4,20},{5,21},{6,22},{7,23},{8,14},{9,... | collective-permute-start | bytes 221192 | tf_op jit(solution)/shard_map/ppermute | solution.py:182
  20.3 1.9 %collective-permute-start.7 = (bf16[8,4608]{1,0:T(8,128)(2,1)S(1)}, bf16[8,4608]{1,0:T(8,128)(2,1)S(1)}, u32[]{:S(2)}, u32[]{:S(2)}) collective-permute-start(bf16[8,4608]{1,0:T(8,128)(2,1)S(1)} %get-tuple-element.53), channel_id=1, source_target_pairs={{0,16},{1,17},{2,18},{3,19},{4,20},{5,21},{6,22},{7,23},{8,9},{9,8... | collective-permute-start | bytes 221192 | tf_op jit(solution)/shard_map/ppermute | solution.py:182
  22.5 1.7 %collective-permute-start.9 = (bf16[8,4608]{1,0:T(8,128)(2,1)S(1)}, bf16[8,4608]{1,0:T(8,128)(2,1)S(1)}, u32[]{:S(2)}, u32[]{:S(2)}) collective-permute-start(bf16[8,4608]{1,0:T(8,128)(2,1)S(1)} %get-tuple-element.55), channel_id=1, source_target_pairs={{0,16},{1,17},{2,18},{3,19},{4,20},{5,21},{6,22},{7,23},{8,11},{9,... | collective-permute-start | bytes 221192 | tf_op jit(solution)/shard_map/ppermute | solution.py:182
  27.5 1.9 %collective-permute-start.14 = (bf16[8,4608]{1,0:T(8,128)(2,1)S(1)}, bf16[8,4608]{1,0:T(8,128)(2,1)S(1)}, u32[]{:S(2)}, u32[]{:S(2)}) collective-permute-start(bf16[8,4608]{1,0:T(8,128)(2,1)S(1)} %get-tuple-element.100), channel_id=1, source_target_pairs={{0,8},{1,9},{2,10},{3,11},{4,12},{5,13},{6,14},{7,15},{8,0},{9,1},... | collective-permute-start | bytes 221192 | tf_op jit(solution)/shard_map/ppermute | solution.py:188
  30.5 1.5 %collective-permute-start.18 = (bf16[8,4608]{1,0:T(8,128)(2,1)S(1)}, bf16[8,4608]{1,0:T(8,128)(2,1)S(1)}, u32[]{:S(2)}, u32[]{:S(2)}) collective-permute-start(bf16[8,4608]{1,0:T(8,128)(2,1)S(1)} %get-tuple-element.100), channel_id=1, source_target_pairs={{0,8},{1,9},{2,10},{3,11},{4,12},{5,13},{6,14},{7,15},{8,4},{9,5},... | collective-permute-start | bytes 221192 | tf_op jit(solution)/shard_map/ppermute | solution.py:188
  35.3 4.0 %collective-permute-done.19.refs_5_ = bf16[8,4608]{1,0:T(8,128)(2,1)S(1)} collective-permute-done((bf16[8,4608]{1,0:T(8,128)(2,1)S(1)}, bf16[8,4608]{1,0:T(8,128)(2,1)S(1)}, u32[]{:S(2)}, u32[]{:S(2)}) %collective-permute-start.19) | collective-permute-done | bytes 73760 | tf_op jit(solution)/shard_map/ppermute | solution.py:188
  39.3 1.8 %collective-permute-done.21.refs_7_ = bf16[8,4608]{1,0:T(8,128)(2,1)S(1)} collective-permute-done((bf16[8,4608]{1,0:T(8,128)(2,1)S(1)}, bf16[8,4608]{1,0:T(8,128)(2,1)S(1)}, u32[]{:S(2)}, u32[]{:S(2)}) %collective-permute-start.21) | collective-permute-done | bytes 73760 | tf_op jit(solution)/shard_map/ppermute | solution.py:188
  42.3 2.0 %collective-permute-start.24 = (bf16[8,4608]{1,0:T(8,128)(2,1)S(1)}, bf16[8,4608]{1,0:T(8,128)(2,1)S(1)}, u32[]{:S(2)}, u32[]{:S(2)}) collective-permute-start(bf16[8,4608]{1,0:T(8,128)(2,1)S(1)} %get-tuple-element.65), channel_id=1, source_target_pairs={{0,10},{1,11},{2,8},{3,9},{4,14},{5,15},{6,12},{7,13},{8,0},{9,1},... | collective-permute-start | bytes 221192 | tf_op jit(solution)/shard_map/ppermute | solution.py:194
  47.8 1.5 %collective-permute-start.29 = (bf16[8,4608]{1,0:T(8,128)(2,1)S(1)}, bf16[8,4608]{1,0:T(8,128)(2,1)S(1)}, u32[]{:S(2)}, u32[]{:S(2)}) collective-permute-start(bf16[8,4608]{1,0:T(8,128)(2,1)S(1)} %get-tuple-element.70), channel_id=1, source_target_pairs={{0,15},{1,14},{2,13},{3,12},{4,11},{5,10},{6,9},{7,8},{8,0},{9,1},... | collective-permute-start | bytes 221192 | tf_op jit(solution)/shard_map/ppermute | solution.py:194
  49.8 1.5 %collective-permute-done.29 = bf16[8,4608]{1,0:T(8,128)(2,1)S(1)} collective-permute-done((bf16[8,4608]{1,0:T(8,128)(2,1)S(1)}, bf16[8,4608]{1,0:T(8,128)(2,1)S(1)}, u32[]{:S(2)}, u32[]{:S(2)}) %collective-permute-start.29) | collective-permute-done | bytes 73760 | tf_op jit(solution)/shard_map/ppermute | solution.py:194
  51.3 5.5 %collective-permute-start.30 = (bf16[8,4608]{1,0:T(8,128)(2,1)S(1)}, bf16[8,4608]{1,0:T(8,128)(2,1)S(1)}, u32[]{:S(2)}, u32[]{:S(2)}) collective-permute-start(bf16[8,4608]{1,0:T(8,128)(2,1)S(1)} %get-tuple-element.98), channel_id=1, source_target_pairs={{24,8},{25,9},{26,10},{27,11},{28,12},{29,13},{30,14},{31,15},{8,0... | collective-permute-start | bytes 221192 | tf_op jit(solution)/shard_map/ppermute | solution.py:202
  56.8 2.6 %collective-permute-start.31 = (bf16[8,4608]{1,0:T(8,128)(2,1)S(1)}, bf16[8,4608]{1,0:T(8,128)(2,1)S(1)}, u32[]{:S(2)}, u32[]{:S(2)}) collective-permute-start(bf16[8,4608]{1,0:T(8,128)(2,1)S(1)} %get-tuple-element.98), channel_id=1, source_target_pairs={{24,9},{25,8},{26,11},{27,10},{28,13},{29,12},{30,15},{31,14},{8,0... | collective-permute-start | bytes 221192 | tf_op jit(solution)/shard_map/ppermute | solution.py:202
  59.5 1.6 %collective-permute-start.34 = (bf16[8,4608]{1,0:T(8,128)(2,1)S(1)}, bf16[8,4608]{1,0:T(8,128)(2,1)S(1)}, u32[]{:S(2)}, u32[]{:S(2)}) collective-permute-start(bf16[8,4608]{1,0:T(8,128)(2,1)S(1)} %get-tuple-element.98), channel_id=1, source_target_pairs={{24,12},{25,13},{26,14},{27,15},{28,8},{29,9},{30,10},{31,11},{8,0... | collective-permute-start | bytes 221192 | tf_op jit(solution)/shard_map/ppermute | solution.py:202
  61.1 2.6 %collective-permute-start.35 = (bf16[8,4608]{1,0:T(8,128)(2,1)S(1)}, bf16[8,4608]{1,0:T(8,128)(2,1)S(1)}, u32[]{:S(2)}, u32[]{:S(2)}) collective-permute-start(bf16[8,4608]{1,0:T(8,128)(2,1)S(1)} %get-tuple-element.98), channel_id=1, source_target_pairs={{24,13},{25,12},{26,15},{27,14},{28,9},{29,8},{30,11},{31,10},{8,0... | collective-permute-start | bytes 221192 | tf_op jit(solution)/shard_map/ppermute | solution.py:202
  67.2 3.8 %shard_map.80 = (bf16[8,8,512]{2,1,0:T(8,128)(2,1)}, bf16[8,4608]{1,0:T(8,128)(2,1)S(1)}, bf16[8,4608]{1,0:T(8,128)(2,1)S(1)}, bf16[8,4608]{1,0:T(8,128)(2,1)S(1...) custom-call(bf16[8,4608]{1,0:T(8,128)(2,1)S(1)} %collective-permute-, ...), custom_call_target="tpu_custom_call", output_to_operand_aliasing={{0}: (13, {})} | custom-call | flops 603979776 | bytes 9437184 | tf_op jit(solution)/shard_map/pallas_call | solution.py:207
  71.0 2.0 %collective-permute-start.39 = (bf16[8,4608]{1,0:T(8,128)(2,1)S(1)}, bf16[8,4608]{1,0:T(8,128)(2,1)S(1)}, u32[]{:S(2)}, u32[]{:S(2)}) collective-permute-start(bf16[8,4608]{1,0:T(8,128)(2,1)S(1)} %get-tuple-element.76), channel_id=1, source_target_pairs={{0,16},{1,17},{2,18},{3,19},{4,20},{5,21},{6,22},{7,23},{8,10},{9,... | collective-permute-start | bytes 221192 | tf_op jit(solution)/shard_map/ppermute | solution.py:182
  73.1 1.9 %collective-permute-start.41 = (bf16[8,4608]{1,0:T(8,128)(2,1)S(1)}, bf16[8,4608]{1,0:T(8,128)(2,1)S(1)}, u32[]{:S(2)}, u32[]{:S(2)}) collective-permute-start(bf16[8,4608]{1,0:T(8,128)(2,1)S(1)} %get-tuple-element.78), channel_id=1, source_target_pairs={{0,16},{1,17},{2,18},{3,19},{4,20},{5,21},{6,22},{7,23},{8,12},{9,... | collective-permute-start | bytes 221192 | tf_op jit(solution)/shard_map/ppermute | solution.py:182
  75.4 1.7 %collective-permute-start.43 = (bf16[8,4608]{1,0:T(8,128)(2,1)S(1)}, bf16[8,4608]{1,0:T(8,128)(2,1)S(1)}, u32[]{:S(2)}, u32[]{:S(2)}) collective-permute-start(bf16[8,4608]{1,0:T(8,128)(2,1)S(1)} %get-tuple-element.80), channel_id=1, source_target_pairs={{0,16},{1,17},{2,18},{3,19},{4,20},{5,21},{6,22},{7,23},{8,14},{9,... | collective-permute-start | bytes 221192 | tf_op jit(solution)/shard_map/ppermute | solution.py:182
  81.5 5.9 %collective-permute-start.45 = (bf16[8,4608]{1,0:T(8,128)(2,1)S(1)}, bf16[8,4608]{1,0:T(8,128)(2,1)S(1)}, u32[]{:S(2)}, u32[]{:S(2)}) collective-permute-start(bf16[8,4608]{1,0:T(8,128)(2,1)S(1)} %get-tuple-element.96), channel_id=1, source_target_pairs={{0,8},{1,9},{2,10},{3,11},{4,12},{5,13},{6,14},{7,15},{8,0},{9,1},... | collective-permute-start | bytes 221192 | tf_op jit(solution)/shard_map/ppermute | solution.py:188
  88.8 1.4 %collective-permute-start.50 = (bf16[8,4608]{1,0:T(8,128)(2,1)S(1)}, bf16[8,4608]{1,0:T(8,128)(2,1)S(1)}, u32[]{:S(2)}, u32[]{:S(2)}) collective-permute-start(bf16[8,4608]{1,0:T(8,128)(2,1)S(1)} %get-tuple-element.96), channel_id=1, source_target_pairs={{0,8},{1,9},{2,10},{3,11},{4,12},{5,13},{6,14},{7,15},{8,5},{9,4},... | collective-permute-start | bytes 221192 | tf_op jit(solution)/shard_map/ppermute | solution.py:188
  93.8 1.5 %collective-permute-done.50.refs_5_ = bf16[8,4608]{1,0:T(8,128)(2,1)S(1)} collective-permute-done((bf16[8,4608]{1,0:T(8,128)(2,1)S(1)}, bf16[8,4608]{1,0:T(8,128)(2,1)S(1)}, u32[]{:S(2)}, u32[]{:S(2)}) %collective-permute-start.50) | collective-permute-done | bytes 73760 | tf_op jit(solution)/shard_map/ppermute | solution.py:188
  95.3 1.6 %collective-permute-done.51.refs_6_ = bf16[8,4608]{1,0:T(8,128)(2,1)S(1)} collective-permute-done((bf16[8,4608]{1,0:T(8,128)(2,1)S(1)}, bf16[8,4608]{1,0:T(8,128)(2,1)S(1)}, u32[]{:S(2)}, u32[]{:S(2)}) %collective-permute-start.51) | collective-permute-done | bytes 73760 | tf_op jit(solution)/shard_map/ppermute | solution.py:188
  96.9 1.9 %collective-permute-done.52.refs_7_ = bf16[8,4608]{1,0:T(8,128)(2,1)S(1)} collective-permute-done((bf16[8,4608]{1,0:T(8,128)(2,1)S(1)}, bf16[8,4608]{1,0:T(8,128)(2,1)S(1)}, u32[]{:S(2)}, u32[]{:S(2)}) %collective-permute-start.52) | collective-permute-done | bytes 73760 | tf_op jit(solution)/shard_map/ppermute | solution.py:188
  98.7 2.5 %shard_map.81 = (bf16[8,8,512]{2,1,0:T(8,128)(2,1)}, bf16[8,4608]{1,0:T(8,128)(2,1)S(1)}, bf16[8,4608]{1,0:T(8,128)(2,1)S(1)}, bf16[8,4608]{1,0:T(8,128)(2,1)S(1...) custom-call(bf16[8,4608]{1,0:T(8,128)(2,1)S(1)} %collective-permute-, ...), custom_call_target="tpu_custom_call", output_to_operand_aliasing={{0}: (11, {})} | custom-call | flops 603979776 | bytes 9437184 | tf_op jit(solution)/shard_map/pallas_call | solution.py:207
  102.5 1.5 %collective-permute-start.56 = (bf16[8,4608]{1,0:T(8,128)(2,1)S(1)}, bf16[8,4608]{1,0:T(8,128)(2,1)S(1)}, u32[]{:S(2)}, u32[]{:S(2)}) collective-permute-start(bf16[8,4608]{1,0:T(8,128)(2,1)S(1)} %get-tuple-element.89), channel_id=1, source_target_pairs={{0,11},{1,10},{2,9},{3,8},{4,15},{5,14},{6,13},{7,12},{8,0},{9,1},... | collective-permute-start | bytes 221192 | tf_op jit(solution)/shard_map/ppermute | solution.py:194
  104.1 2.0 %collective-permute-start.58 = (bf16[8,4608]{1,0:T(8,128)(2,1)S(1)}, bf16[8,4608]{1,0:T(8,128)(2,1)S(1)}, u32[]{:S(2)}, u32[]{:S(2)}) collective-permute-start(bf16[8,4608]{1,0:T(8,128)(2,1)S(1)} %get-tuple-element.91), channel_id=1, source_target_pairs={{0,13},{1,12},{2,15},{3,14},{4,9},{5,8},{6,11},{7,10},{8,0},{9,1},... | collective-permute-start | bytes 221192 | tf_op jit(solution)/shard_map/ppermute | solution.py:194
  110.6 2.7 %collective-permute-start.61 = (f32[8,4608]{1,0:T(8,128)S(1)}, f32[8,4608]{1,0:T(8,128)S(1)}, u32[]{:S(2)}, u32[]{:S(2)}) collective-permute-start(f32[8,4608]{1,0:T(8,128)S(1)} %get-tuple-element.94), channel_id=1, source_target_pairs={{0,8},{1,9},{2,10},{3,11},{4,12},{5,13},{6,14},{7,15},{8,0},{9,1},... | collective-permute-start | bytes 442376 | tf_op jit(solution)/shard_map/ppermute | solution.py:188
  (104 shorter events, 38.3 us)
Async XLA Ops:
  0.6 7.1 %collective-permute-start = (bf16[8,4608]{1,0:T(8,128)(2,1)}, bf16[8,4608]{1,0:T(8,128)(2,1)S(1)}, u32[]{:S(2)}, u32[]{:S(2)}) collective-permute-start(bf16[8,4608]{1,0:T(8,128)(2,1)} %refs_0_.1), channel_id=1, source_target_pairs={{0,16},{1,17},{2,18},{3,19},{4,20},{5,21},{6,22},{7,23},{8,9},{9,8... | collective-permute-start | bytes 221192 | tf_op jit(solution)/shard_map/ppermute | solution.py:182
  3.7 7.1 %collective-permute-start.2 = (bf16[8,4608]{1,0:T(8,128)(2,1)}, bf16[8,4608]{1,0:T(8,128)(2,1)S(1)}, u32[]{:S(2)}, u32[]{:S(2)}) collective-permute-start(bf16[8,4608]{1,0:T(8,128)(2,1)} %refs_0_.1), channel_id=1, source_target_pairs={{0,16},{1,17},{2,18},{3,19},{4,20},{5,21},{6,22},{7,23},{8,11},{9,... | collective-permute-start | bytes 221192 | tf_op jit(solution)/shard_map/ppermute | solution.py:182
  5.7 5.2 %collective-permute-start.3 = (bf16[8,4608]{1,0:T(8,128)(2,1)}, bf16[8,4608]{1,0:T(8,128)(2,1)S(1)}, u32[]{:S(2)}, u32[]{:S(2)}) collective-permute-start(bf16[8,4608]{1,0:T(8,128)(2,1)} %refs_0_.1), channel_id=1, source_target_pairs={{0,16},{1,17},{2,18},{3,19},{4,20},{5,21},{6,22},{7,23},{8,12},{9,... | collective-permute-start | bytes 221192 | tf_op jit(solution)/shard_map/ppermute | solution.py:182
  5.8 5.3 %collective-permute-start.4 = (bf16[8,4608]{1,0:T(8,128)(2,1)}, bf16[8,4608]{1,0:T(8,128)(2,1)S(1)}, u32[]{:S(2)}, u32[]{:S(2)}) collective-permute-start(bf16[8,4608]{1,0:T(8,128)(2,1)} %refs_0_.1), channel_id=1, source_target_pairs={{0,16},{1,17},{2,18},{3,19},{4,20},{5,21},{6,22},{7,23},{8,13},{9,... | collective-permute-start | bytes 221192 | tf_op jit(solution)/shard_map/ppermute | solution.py:182
  8.2 4.8 %collective-permute-start.6 = (bf16[8,4608]{1,0:T(8,128)(2,1)}, bf16[8,4608]{1,0:T(8,128)(2,1)S(1)}, u32[]{:S(2)}, u32[]{:S(2)}) collective-permute-start(bf16[8,4608]{1,0:T(8,128)(2,1)} %refs_0_.1), channel_id=1, source_target_pairs={{0,16},{1,17},{2,18},{3,19},{4,20},{5,21},{6,22},{7,23},{8,15},{9,... | collective-permute-start | bytes 221192 | tf_op jit(solution)/shard_map/ppermute | solution.py:182
  13.2 9.1 %collective-permute-start.10 = (bf16[8,4608]{1,0:T(8,128)(2,1)S(1)}, bf16[8,4608]{1,0:T(8,128)(2,1)S(1)}, u32[]{:S(2)}, u32[]{:S(2)}) collective-permute-start(bf16[8,4608]{1,0:T(8,128)(2,1)S(1)} %get-tuple-element.56), channel_id=1, source_target_pairs={{0,16},{1,17},{2,18},{3,19},{4,20},{5,21},{6,22},{7,23},{8,12},{9,... | collective-permute-start | bytes 221192 | tf_op jit(solution)/shard_map/ppermute | solution.py:182
  18.3 6.0 %collective-permute-start.12 = (bf16[8,4608]{1,0:T(8,128)(2,1)S(1)}, bf16[8,4608]{1,0:T(8,128)(2,1)S(1)}, u32[]{:S(2)}, u32[]{:S(2)}) collective-permute-start(bf16[8,4608]{1,0:T(8,128)(2,1)S(1)} %get-tuple-element.58), channel_id=1, source_target_pairs={{0,16},{1,17},{2,18},{3,19},{4,20},{5,21},{6,22},{7,23},{8,14},{9,... | collective-permute-start | bytes 221192 | tf_op jit(solution)/shard_map/ppermute | solution.py:182
  20.3 5.1 %collective-permute-start.7 = (bf16[8,4608]{1,0:T(8,128)(2,1)S(1)}, bf16[8,4608]{1,0:T(8,128)(2,1)S(1)}, u32[]{:S(2)}, u32[]{:S(2)}) collective-permute-start(bf16[8,4608]{1,0:T(8,128)(2,1)S(1)} %get-tuple-element.53), channel_id=1, source_target_pairs={{0,16},{1,17},{2,18},{3,19},{4,20},{5,21},{6,22},{7,23},{8,9},{9,8... | collective-permute-start | bytes 221192 | tf_op jit(solution)/shard_map/ppermute | solution.py:182
  22.5 4.8 %collective-permute-start.9 = (bf16[8,4608]{1,0:T(8,128)(2,1)S(1)}, bf16[8,4608]{1,0:T(8,128)(2,1)S(1)}, u32[]{:S(2)}, u32[]{:S(2)}) collective-permute-start(bf16[8,4608]{1,0:T(8,128)(2,1)S(1)} %get-tuple-element.55), channel_id=1, source_target_pairs={{0,16},{1,17},{2,18},{3,19},{4,20},{5,21},{6,22},{7,23},{8,11},{9,... | collective-permute-start | bytes 221192 | tf_op jit(solution)/shard_map/ppermute | solution.py:182
  29.4 5.1 %collective-permute-start.16 = (bf16[8,4608]{1,0:T(8,128)(2,1)S(1)}, bf16[8,4608]{1,0:T(8,128)(2,1)S(1)}, u32[]{:S(2)}, u32[]{:S(2)}) collective-permute-start(bf16[8,4608]{1,0:T(8,128)(2,1)S(1)} %get-tuple-element.100), channel_id=1, source_target_pairs={{0,8},{1,9},{2,10},{3,11},{4,12},{5,13},{6,14},{7,15},{8,2},{9,3},... | collective-permute-start | bytes 221192 | tf_op jit(solution)/shard_map/ppermute | solution.py:188
  30.2 4.9 %collective-permute-start.17 = (bf16[8,4608]{1,0:T(8,128)(2,1)S(1)}, bf16[8,4608]{1,0:T(8,128)(2,1)S(1)}, u32[]{:S(2)}, u32[]{:S(2)}) collective-permute-start(bf16[8,4608]{1,0:T(8,128)(2,1)S(1)} %get-tuple-element.100), channel_id=1, source_target_pairs={{0,8},{1,9},{2,10},{3,11},{4,12},{5,13},{6,14},{7,15},{8,3},{9,2},... | collective-permute-start | bytes 221192 | tf_op jit(solution)/shard_map/ppermute | solution.py:188
  30.5 4.8 %collective-permute-start.18 = (bf16[8,4608]{1,0:T(8,128)(2,1)S(1)}, bf16[8,4608]{1,0:T(8,128)(2,1)S(1)}, u32[]{:S(2)}, u32[]{:S(2)}) collective-permute-start(bf16[8,4608]{1,0:T(8,128)(2,1)S(1)} %get-tuple-element.100), channel_id=1, source_target_pairs={{0,8},{1,9},{2,10},{3,11},{4,12},{5,13},{6,14},{7,15},{8,4},{9,5},... | collective-permute-start | bytes 221192 | tf_op jit(solution)/shard_map/ppermute | solution.py:188
  32.0 7.2 %collective-permute-start.19 = (bf16[8,4608]{1,0:T(8,128)(2,1)S(1)}, bf16[8,4608]{1,0:T(8,128)(2,1)S(1)}, u32[]{:S(2)}, u32[]{:S(2)}) collective-permute-start(bf16[8,4608]{1,0:T(8,128)(2,1)S(1)} %get-tuple-element.100), channel_id=1, source_target_pairs={{0,8},{1,9},{2,10},{3,11},{4,12},{5,13},{6,14},{7,15},{8,5},{9,4},... | collective-permute-start | bytes 221192 | tf_op jit(solution)/shard_map/ppermute | solution.py:188
  33.2 6.1 %collective-permute-start.20 = (bf16[8,4608]{1,0:T(8,128)(2,1)S(1)}, bf16[8,4608]{1,0:T(8,128)(2,1)S(1)}, u32[]{:S(2)}, u32[]{:S(2)}) collective-permute-start(bf16[8,4608]{1,0:T(8,128)(2,1)S(1)} %get-tuple-element.100), channel_id=1, source_target_pairs={{0,8},{1,9},{2,10},{3,11},{4,12},{5,13},{6,14},{7,15},{8,6},{9,7},... | collective-permute-start | bytes 221192 | tf_op jit(solution)/shard_map/ppermute | solution.py:188
  34.5 6.6 %collective-permute-start.21 = (bf16[8,4608]{1,0:T(8,128)(2,1)S(1)}, bf16[8,4608]{1,0:T(8,128)(2,1)S(1)}, u32[]{:S(2)}, u32[]{:S(2)}) collective-permute-start(bf16[8,4608]{1,0:T(8,128)(2,1)S(1)} %get-tuple-element.100), channel_id=1, source_target_pairs={{0,8},{1,9},{2,10},{3,11},{4,12},{5,13},{6,14},{7,15},{8,7},{9,6},... | collective-permute-start | bytes 221192 | tf_op jit(solution)/shard_map/ppermute | solution.py:188
  42.3 5.5 %collective-permute-start.24 = (bf16[8,4608]{1,0:T(8,128)(2,1)S(1)}, bf16[8,4608]{1,0:T(8,128)(2,1)S(1)}, u32[]{:S(2)}, u32[]{:S(2)}) collective-permute-start(bf16[8,4608]{1,0:T(8,128)(2,1)S(1)} %get-tuple-element.65), channel_id=1, source_target_pairs={{0,10},{1,11},{2,8},{3,9},{4,14},{5,15},{6,12},{7,13},{8,0},{9,1},... | collective-permute-start | bytes 221192 | tf_op jit(solution)/shard_map/ppermute | solution.py:194
  44.3 4.9 %collective-permute-start.25 = (bf16[8,4608]{1,0:T(8,128)(2,1)S(1)}, bf16[8,4608]{1,0:T(8,128)(2,1)S(1)}, u32[]{:S(2)}, u32[]{:S(2)}) collective-permute-start(bf16[8,4608]{1,0:T(8,128)(2,1)S(1)} %get-tuple-element.66), channel_id=1, source_target_pairs={{0,11},{1,10},{2,9},{3,8},{4,15},{5,14},{6,13},{7,12},{8,0},{9,1},... | collective-permute-start | bytes 221192 | tf_op jit(solution)/shard_map/ppermute | solution.py:194
  51.3 9.8 %collective-permute-start.30 = (bf16[8,4608]{1,0:T(8,128)(2,1)S(1)}, bf16[8,4608]{1,0:T(8,128)(2,1)S(1)}, u32[]{:S(2)}, u32[]{:S(2)}) collective-permute-start(bf16[8,4608]{1,0:T(8,128)(2,1)S(1)} %get-tuple-element.98), channel_id=1, source_target_pairs={{24,8},{25,9},{26,10},{27,11},{28,12},{29,13},{30,14},{31,15},{8,0... | collective-permute-start | bytes 221192 | tf_op jit(solution)/shard_map/ppermute | solution.py:202
  56.8 6.9 %collective-permute-start.31 = (bf16[8,4608]{1,0:T(8,128)(2,1)S(1)}, bf16[8,4608]{1,0:T(8,128)(2,1)S(1)}, u32[]{:S(2)}, u32[]{:S(2)}) collective-permute-start(bf16[8,4608]{1,0:T(8,128)(2,1)S(1)} %get-tuple-element.98), channel_id=1, source_target_pairs={{24,9},{25,8},{26,11},{27,10},{28,13},{29,12},{30,15},{31,14},{8,0... | collective-permute-start | bytes 221192 | tf_op jit(solution)/shard_map/ppermute | solution.py:202
  59.5 5.3 %collective-permute-start.33 = (bf16[8,4608]{1,0:T(8,128)(2,1)S(1)}, bf16[8,4608]{1,0:T(8,128)(2,1)S(1)}, u32[]{:S(2)}, u32[]{:S(2)}) collective-permute-start(bf16[8,4608]{1,0:T(8,128)(2,1)S(1)} %get-tuple-element.98), channel_id=1, source_target_pairs={{24,11},{25,10},{26,9},{27,8},{28,15},{29,14},{30,13},{31,12},{8,0... | collective-permute-start | bytes 221192 | tf_op jit(solution)/shard_map/ppermute | solution.py:202
  59.5 5.2 %collective-permute-start.34 = (bf16[8,4608]{1,0:T(8,128)(2,1)S(1)}, bf16[8,4608]{1,0:T(8,128)(2,1)S(1)}, u32[]{:S(2)}, u32[]{:S(2)}) collective-permute-start(bf16[8,4608]{1,0:T(8,128)(2,1)S(1)} %get-tuple-element.98), channel_id=1, source_target_pairs={{24,12},{25,13},{26,14},{27,15},{28,8},{29,9},{30,10},{31,11},{8,0... | collective-permute-start | bytes 221192 | tf_op jit(solution)/shard_map/ppermute | solution.py:202
  71.0 6.1 %collective-permute-start.39 = (bf16[8,4608]{1,0:T(8,128)(2,1)S(1)}, bf16[8,4608]{1,0:T(8,128)(2,1)S(1)}, u32[]{:S(2)}, u32[]{:S(2)}) collective-permute-start(bf16[8,4608]{1,0:T(8,128)(2,1)S(1)} %get-tuple-element.76), channel_id=1, source_target_pairs={{0,16},{1,17},{2,18},{3,19},{4,20},{5,21},{6,22},{7,23},{8,10},{9,... | collective-permute-start | bytes 221192 | tf_op jit(solution)/shard_map/ppermute | solution.py:182
  73.1 5.1 %collective-permute-start.41 = (bf16[8,4608]{1,0:T(8,128)(2,1)S(1)}, bf16[8,4608]{1,0:T(8,128)(2,1)S(1)}, u32[]{:S(2)}, u32[]{:S(2)}) collective-permute-start(bf16[8,4608]{1,0:T(8,128)(2,1)S(1)} %get-tuple-element.78), channel_id=1, source_target_pairs={{0,16},{1,17},{2,18},{3,19},{4,20},{5,21},{6,22},{7,23},{8,12},{9,... | collective-permute-start | bytes 221192 | tf_op jit(solution)/shard_map/ppermute | solution.py:182
  75.4 4.8 %collective-permute-start.43 = (bf16[8,4608]{1,0:T(8,128)(2,1)S(1)}, bf16[8,4608]{1,0:T(8,128)(2,1)S(1)}, u32[]{:S(2)}, u32[]{:S(2)}) collective-permute-start(bf16[8,4608]{1,0:T(8,128)(2,1)S(1)} %get-tuple-element.80), channel_id=1, source_target_pairs={{0,16},{1,17},{2,18},{3,19},{4,20},{5,21},{6,22},{7,23},{8,14},{9,... | collective-permute-start | bytes 221192 | tf_op jit(solution)/shard_map/ppermute | solution.py:182
  81.5 7.3 %collective-permute-start.45 = (bf16[8,4608]{1,0:T(8,128)(2,1)S(1)}, bf16[8,4608]{1,0:T(8,128)(2,1)S(1)}, u32[]{:S(2)}, u32[]{:S(2)}) collective-permute-start(bf16[8,4608]{1,0:T(8,128)(2,1)S(1)} %get-tuple-element.96), channel_id=1, source_target_pairs={{0,8},{1,9},{2,10},{3,11},{4,12},{5,13},{6,14},{7,15},{8,0},{9,1},... | collective-permute-start | bytes 221192 | tf_op jit(solution)/shard_map/ppermute | solution.py:188
  88.6 5.3 %collective-permute-start.48 = (bf16[8,4608]{1,0:T(8,128)(2,1)S(1)}, bf16[8,4608]{1,0:T(8,128)(2,1)S(1)}, u32[]{:S(2)}, u32[]{:S(2)}) collective-permute-start(bf16[8,4608]{1,0:T(8,128)(2,1)S(1)} %get-tuple-element.96), channel_id=1, source_target_pairs={{0,8},{1,9},{2,10},{3,11},{4,12},{5,13},{6,14},{7,15},{8,3},{9,2},... | collective-permute-start | bytes 221192 | tf_op jit(solution)/shard_map/ppermute | solution.py:188
  88.6 5.3 %collective-permute-start.49 = (bf16[8,4608]{1,0:T(8,128)(2,1)S(1)}, bf16[8,4608]{1,0:T(8,128)(2,1)S(1)}, u32[]{:S(2)}, u32[]{:S(2)}) collective-permute-start(bf16[8,4608]{1,0:T(8,128)(2,1)S(1)} %get-tuple-element.96), channel_id=1, source_target_pairs={{0,8},{1,9},{2,10},{3,11},{4,12},{5,13},{6,14},{7,15},{8,4},{9,5},... | collective-permute-start | bytes 221192 | tf_op jit(solution)/shard_map/ppermute | solution.py:188
  88.8 6.5 %collective-permute-start.50 = (bf16[8,4608]{1,0:T(8,128)(2,1)S(1)}, bf16[8,4608]{1,0:T(8,128)(2,1)S(1)}, u32[]{:S(2)}, u32[]{:S(2)}) collective-permute-start(bf16[8,4608]{1,0:T(8,128)(2,1)S(1)} %get-tuple-element.96), channel_id=1, source_target_pairs={{0,8},{1,9},{2,10},{3,11},{4,12},{5,13},{6,14},{7,15},{8,5},{9,4},... | collective-permute-start | bytes 221192 | tf_op jit(solution)/shard_map/ppermute | solution.py:188
  91.2 5.6 %collective-permute-start.51 = (bf16[8,4608]{1,0:T(8,128)(2,1)S(1)}, bf16[8,4608]{1,0:T(8,128)(2,1)S(1)}, u32[]{:S(2)}, u32[]{:S(2)}) collective-permute-start(bf16[8,4608]{1,0:T(8,128)(2,1)S(1)} %get-tuple-element.96), channel_id=1, source_target_pairs={{0,8},{1,9},{2,10},{3,11},{4,12},{5,13},{6,14},{7,15},{8,6},{9,7},... | collective-permute-start | bytes 221192 | tf_op jit(solution)/shard_map/ppermute | solution.py:188
  92.2 6.6 %collective-permute-start.52 = (bf16[8,4608]{1,0:T(8,128)(2,1)S(1)}, bf16[8,4608]{1,0:T(8,128)(2,1)S(1)}, u32[]{:S(2)}, u32[]{:S(2)}) collective-permute-start(bf16[8,4608]{1,0:T(8,128)(2,1)S(1)} %get-tuple-element.96), channel_id=1, source_target_pairs={{0,8},{1,9},{2,10},{3,11},{4,12},{5,13},{6,14},{7,15},{8,7},{9,6},... | collective-permute-start | bytes 221192 | tf_op jit(solution)/shard_map/ppermute | solution.py:188
  101.3 4.8 %collective-permute-start.54 = (bf16[8,4608]{1,0:T(8,128)(2,1)S(1)}, bf16[8,4608]{1,0:T(8,128)(2,1)S(1)}, u32[]{:S(2)}, u32[]{:S(2)}) collective-permute-start(bf16[8,4608]{1,0:T(8,128)(2,1)S(1)} %get-tuple-element.87), channel_id=1, source_target_pairs={{0,9},{1,8},{2,11},{3,10},{4,13},{5,12},{6,15},{7,14},{8,0},{9,1},... | collective-permute-start | bytes 221192 | tf_op jit(solution)/shard_map/ppermute | solution.py:194
  102.5 6.0 %collective-permute-start.56 = (bf16[8,4608]{1,0:T(8,128)(2,1)S(1)}, bf16[8,4608]{1,0:T(8,128)(2,1)S(1)}, u32[]{:S(2)}, u32[]{:S(2)}) collective-permute-start(bf16[8,4608]{1,0:T(8,128)(2,1)S(1)} %get-tuple-element.89), channel_id=1, source_target_pairs={{0,11},{1,10},{2,9},{3,8},{4,15},{5,14},{6,13},{7,12},{8,0},{9,1},... | collective-permute-start | bytes 221192 | tf_op jit(solution)/shard_map/ppermute | solution.py:194
  (31 other events, 124.4 us)

commit v3 on v2

--- a/solution.py
+++ b/solution.py
@@ -9,6 +9,13 @@
 
 BLOCK = 128
 AXES = ("layer", "feat")
+PLANS = {
+    "first": ((6, 1, 4, 2, 3), (6, 4)),
+    "within": ((7, 2, 4, 6, 1), (4, 2)),
+    "down": ((0, 1, 2, 4, 6, 7), (4, 2)),
+    "up": ((6, 0, 1, 4, 2, 5), (6, 2)),
+    "skip": ((3, 1, 2, 0, 4, 5, 6, 7), ()),
+}
 
 
 def fetch(source, target, sems, chunks):
@@ -23,19 +30,19 @@
 CHUNKS = 4
 
 
-def stage_kernel(
-    by_xor, act_ref, ids_ref, counts_ref, dec_ref, enc_ref, gate_ref, attr_ref, dec_out, enc_out,
-    act, ids, counts, sems, dec_sems, enc_sems,
+def gate_kernel(
+    by_xor, act_ref, ids_ref, counts_ref, dec_ref, gate_ref, attr_ref, dec_out,
+    act, ids, counts, sems, dec_sems,
 ):
     del attr_ref
     top = lax.axis_index("layer") == lax.axis_size("layer") - 1
-    weights = fetch(dec_ref, dec_out, dec_sems, CHUNKS) + fetch(enc_ref, enc_out, enc_sems, CHUNKS)
-    small = [
+    weights = fetch(dec_ref, dec_out, dec_sems, CHUNKS)
+    moves = [
         pltpu.make_async_copy(counts_ref, counts, sems.at[0]),
         pltpu.make_async_copy(ids_ref, ids, sems.at[1]),
         pltpu.make_async_copy(act_ref, act, sems.at[2]),
     ]
-    for move in small:
+    for move in moves:
         move.start()
 
     @pl.when(top)
@@ -43,7 +50,7 @@
         for move in weights:
             move.start()
 
-    for move in small:
+    for move in moves:
         move.wait()
     feat_index = lax.axis_index("feat")
     tiles, tok_dev, feat_dev = act_ref.shape
@@ -68,7 +75,10 @@
 
 
 def attribute_kernel(layer, tiles, *refs):
-    rows, (gate_ref, dec, enc), refs = refs[:tiles], refs[tiles : tiles + 3], refs[tiles + 3 :]
+    rows, (gate_ref, dec), refs = refs[:tiles], refs[tiles : tiles + 2], refs[tiles + 2 :]
+    top = layer == lax.axis_size("layer") - 1
+    if not top:
+        enc, refs = refs[0], refs[1:]
     if layer:
         dec_ref, enc_ref = refs[:2]
         refs = refs[2:]
@@ -77,14 +87,16 @@
     layer_index = lax.axis_index("layer")
     if layer:
         dec_out, enc_out, h_ref, a_ref, b_ref, sem, dec_sems, enc_sems = refs
-        weights = fetch(dec_ref, dec_out, dec_sems, CHUNKS)
-        weights += fetch(enc_ref, enc_out, enc_sems, CHUNKS)
+        dec_moves = fetch(dec_ref, dec_out, dec_sems, CHUNKS)
+        enc_moves = fetch(enc_ref, enc_out, enc_sems, CHUNKS)
+        if top:
+            enc = enc_out
 
         @pl.when(layer_index == layer - 1)
         def _():
-            for move in weights:
+            for move in dec_moves + enc_moves:
                 move.start()
-            for move in weights:
+            for move in dec_moves + enc_moves:
                 move.wait()
     else:
         h_ref, a_ref, b_ref, sem = refs
@@ -94,6 +106,9 @@
 
     @pl.when(layer_index == layer)
     def _():
+        if top:
+            for move in enc_moves:
+                move.start()
         for k in range(0, tiles, 2):
             pair = jnp.concatenate([rows[k][...], rows[k + 1][...]], axis=0)
             h_ref[k * tok_dev : (k + 2) * tok_dev, :] = pair
@@ -112,6 +127,9 @@
                 b_ref[feat_index ^ k, :, f : f + cut] = block.astype(jnp.bfloat16)
         done = pltpu.make_async_copy(b_ref, attr_ref, sem.at[0])
         done.start()
+        if top:
+            for move in enc_moves:
+                move.wait()
         cut = 512
         for c in range(0, width, cut):
             product = jnp.dot(
@@ -130,7 +148,7 @@
     feat_index = lax.axis_index("feat")
     feat_dev, width = decoder.shape[1:]
     tok_dev = top_grad.shape[0]
-    direct = tiles <= 8
+    direct = tiles == 8
 
     vmem = pl.BlockSpec(memory_space=pltpu.VMEM)
     hbm = pl.BlockSpec(memory_space=pl.ANY)
@@ -144,41 +162,39 @@
     chunk_sems = [pltpu.SemaphoreType.DMA((CHUNKS,))] * 2
 
     act_tiles = activations.reshape(tiles, tok_dev, feat_dev)
-    gate, attr, dec, enc = pl.pallas_call(
-        functools.partial(stage_kernel, direct),
+    gate, attr, dec = pl.pallas_call(
+        functools.partial(gate_kernel, direct),
         out_shape=(
             jax.ShapeDtypeStruct((tiles * tok_dev, feat_dev), jnp.float32),
             pltpu.HBM(act_tiles.shape, act_tiles.dtype),
-            *staged,
+            staged[0],
         ),
-        in_specs=[hbm] * 5,
-        out_specs=(vmem, hbm, hbm, hbm),
+        in_specs=[hbm] * 4,
+        out_specs=(vmem, hbm, hbm),
         scratch_shapes=[
             pltpu.VMEM(act_tiles.shape, act_tiles.dtype),
             pltpu.VMEM(block_ids.shape, block_ids.dtype),
             pltpu.SMEM(block_counts.shape, block_counts.dtype),
             pltpu.SemaphoreType.DMA((3,)),
-            *chunk_sems,
+            chunk_sems[0],
         ],
         compiler_params=pltpu.CompilerParams(vmem_limit_bytes=8 * 2**20),
-        cost_estimate=pl.CostEstimate(
-            flops=0, bytes_accessed=2 * weight_bytes, transcendentals=0
-        ),
+        cost_estimate=pl.CostEstimate(flops=0, bytes_accessed=weight_bytes, transcendentals=0),
     )(
         pltpu.with_memory_space_constraint(act_tiles, pltpu.HBM),
         pltpu.with_memory_space_constraint(block_ids, pltpu.HBM),
         pltpu.with_memory_space_constraint(block_counts, pltpu.HBM),
         dec_hbm,
-        enc_hbm,
     )
+    enc = None
 
     def link(layer, to_layer, k):
         return [(layer * tiles + i, (to_layer % layers) * tiles + (i ^ k)) for i in range(tiles)]
 
-    def within(value, k):
+    def within(value, k, odd=1):
         pairs = []
         for l in range(layers):
-            pairs += link(l, l, k) if l % 2 else link(l, l + 2, 0)
+            pairs += link(l, l, k) if l % 2 == odd else link(l, l + 2, 0)
         return lax.ppermute(value, AXES, pairs)
 
     def down(value, k):
@@ -193,7 +209,7 @@
             pairs += link(l, l - 1, 0) if l % 2 else link(l, l + 1, k)
         return lax.ppermute(value, AXES, pairs)
 
-    def skip(value, top, k):
+    def skip(value, k, top):
         pairs = link(top, top - 2, k) + link(top - 2, top - 3, 0)
         pairs += link(top - 3, top - 1, 0) + link(top - 1, top, 0)
         for l in range(layers):
@@ -204,6 +220,9 @@
     def attribute_direct(layer, rows, attr, dec, enc):
         block = jax.ShapeDtypeStruct((tok_dev, width), jnp.bfloat16)
         more = 2 if layer else 0
+        held = [dec] if enc is None else [dec, enc]
+        held = [pltpu.with_memory_space_constraint(w, pltpu.VMEM) for w in held]
+        given = tiles + 1 + len(held)
         outs = pl.pallas_call(
             functools.partial(attribute_kernel, layer, tiles),
             out_shape=(
@@ -211,8 +230,8 @@
                 *[block] * tiles,
                 *staged[:more],
             ),
-            in_specs=[vmem] * (tiles + 3) + [hbm] * (more + 1),
-            out_specs=(hbm,) + (vmem,) * tiles + (hbm,) * more,
+            in_specs=[vmem] * given + [hbm] * (more + 1),
+            out_specs=(hbm,) + (vmem,) * (tiles + more),
             scratch_shapes=[
                 pltpu.VMEM((tiles * tok_dev, width), jnp.bfloat16),
                 pltpu.VMEM((tiles * tok_dev, feat_dev), jnp.bfloat16),
@@ -220,7 +239,7 @@
                 pltpu.SemaphoreType.DMA((1,)),
                 *chunk_sems[:more],
             ],
-            input_output_aliases={tiles + 3 + more: 0},
+            input_output_aliases={given + more: 0},
             compiler_params=pltpu.CompilerParams(vmem_limit_bytes=8 * 2**20),
             cost_estimate=pl.CostEstimate(
                 flops=4 * tiles * tok_dev * feat_dev * width,
@@ -230,8 +249,7 @@
         )(
             *rows,
             gate,
-            pltpu.with_memory_space_constraint(dec, pltpu.VMEM),
-            pltpu.with_memory_space_constraint(enc, pltpu.VMEM),
+            *held,
             *[dec_hbm, enc_hbm][:more],
             attr,
         )
@@ -256,25 +274,47 @@
     def exchanged(values):
         return list(lax.all_to_all(values, "feat", 0, 0, tiled=True))
 
+    def gather(value, move, odd, plan):
+        order, joined = plan
+        rows = {0: value}
+        for k in order:
+            rows[k] = move(value, k)
+        for k in joined:
+            rows[k ^ 1] = within(rows[k], 1, odd)
+        return [rows[k] for k in range(tiles)]
+
+    def collect(start, part, move, odd, plan):
+        order, joined = plan
+        side = {k: within(part[k ^ 1], 1, odd) for k in joined}
+        terms = [] if 0 in order else [part[0]]
+        for k in order:
+            term = part[k]
+            if k in side:
+                both = term.astype(jnp.float32) + side[k].astype(jnp.float32)
+                term = lax.optimization_barrier(both.astype(jnp.bfloat16))
+            terms.append(move(term, k))
+        return total(start, terms)
+
     grads = [None] * layers
     grad = top_grad.astype(jnp.float32)
     sent = top_grad
     if direct:
         for high in range(layers - 1, 0, -2):
             if high == layers - 1:
-                rows = [sent] + [within(sent, k) for k in range(1, tiles)]
+                rows = gather(sent, within, 1, PLANS["first"])
             else:
-                rows = [skip(sent, high + 2, k) for k in range(tiles)]
+                move = functools.partial(skip, top=high + 2)
+                rows = gather(sent, move, 1, PLANS["skip"])
                 grad = rows[0].astype(jnp.float32)
             attr, part, (dec, enc) = attribute_direct(high, rows, attr, dec, enc)
-            grad = total(grad, [part[0]] + [within(part[k], k) for k in range(1, tiles)])
+            grad = collect(grad, part, within, 1, PLANS["within"])
             grads[high] = grad
             sent = grad.astype(jnp.bfloat16)
-            rows = [down(sent, k) for k in range(tiles)]
+            rows = gather(sent, down, 0, PLANS["down"])
             low = high - 1
             attr, part, (dec, enc) = attribute_direct(low, rows, attr, dec, enc)
-            grad = total(grad, [up(part[k], k) for k in range(tiles)])
-            grads[high - 1] = grad
+            grad = collect(grad, part, up, 0, PLANS["up"])
+            grads[low] = grad
             sent = grad.astype(jnp.bfloat16)
         lower = grads[0]
         for high in range(3, layers, 2):

time: 115 us -> 105 us (0.913)
  starting transfers between devices: 75.6 us -> 68.4 us
  waiting for transfers between devices: 30.1 us -> 27 us
    ppermute x21 -> x29, starting transfers between devices: 26.4 us -> 34.9 us  [within(): return lax.ppermute(value, AXES, pairs)]
    ppermute x17 -> x13, starting transfers between devices: 20.4 us -> 13.4 us  [down(): return lax.ppermute(value, AXES, pairs)]
    ppermute x17 -> x13, waiting for transfers between devices: 14.1 us -> 8.79 us  [down(): return lax.ppermute(value, AXES, pairs)]
    ppermute x8, starting transfers between devices: 13.4 us -> 9.06 us  [skip(): return lax.ppermute(value, AXES, pairs)]
    ppermute x16 -> x12, starting transfers between devices: 15.3 us -> 11 us  [up(): return lax.ppermute(value, AXES, pairs)]
    ppermute x21 -> x29, waiting for transfers between devices: 9.59 us -> 12.1 us  [within(): return lax.ppermute(value, AXES, pairs)]
    ppermute x16 -> x12, waiting for transfers between devices: 3.97 us -> 4.16 us  [up(): return lax.ppermute(value, AXES, pairs)]
  transfers between devices with their start and end apart: 62 -> 62, of which waited for: 29 -> 30; matrix products, arithmetic and copies ran while one was open for 0% -> 0% of each run, Pallas kernels for 1% -> 1%
where the time goes in v3:
time: 105 us
  starting transfers between devices  68.4 us (65%)
  waiting for transfers between devices  27 us (26%)
  Pallas kernels  7.44 us (7%)
  other arithmetic  1.19 us (1%)
    ppermute x29, starting transfers between devices, within(): return lax.ppermute(value, AXES, pairs)  34.9 us
    ppermute x13, starting transfers between devices, down(): return lax.ppermute(value, AXES, pairs)  13.4 us
    ppermute x29, waiting for transfers between devices, within(): return lax.ppermute(value, AXES, pairs)  12.1 us
    ppermute x12, starting transfers between devices, up(): return lax.ppermute(value, AXES, pairs)  11 us
    ppermute x8, starting transfers between devices, skip(): return lax.ppermute(value, AXES, pairs)  9.06 us
    ppermute x13, waiting for transfers between devices, down(): return lax.ppermute(value, AXES, pairs)  8.79 us
    pallas_call x4, Pallas kernels, attribute_direct(): pl.pallas_call(functools.partial(attribute_kernel, layer, tiles), out_sha...  6.41 us
    ppermute x12, waiting for transfers between devices, up(): return lax.ppermute(value, AXES, pairs)  4.16 us
  transfers between devices with their start and end apart: 62, of which 30 were waited for; matrix products, arithmetic and copies ran while one was open for 0% of the time, Pallas kernels for 1%

profile of v3, /device:TPU:0, one launch (start us, length us, event | category | flops | bytes accessed | tf_op | source)
XLA Modules:
  0.0 104.9 jit_solution(6623106452812785287)
XLA Ops:
  0.6 3.0 %collective-permute-start.3 = (bf16[8,4608]{1,0:T(8,128)(2,1)}, bf16[8,4608]{1,0:T(8,128)(2,1)S(1)}, u32[]{:S(2)}, u32[]{:S(2)}) collective-permute-start(bf16[8,4608]{1,0:T(8,128)(2,1)} %refs_0_.1), channel_id=1, source_target_pairs={{0,16},{1,17},{2,18},{3,19},{4,20},{5,21},{6,22},{7,23},{8,12},{9,... | collective-permute-start | bytes 221192 | tf_op jit(solution)/shard_map/ppermute | solution.py:198
  3.8 1.9 %collective-permute-start = (bf16[8,4608]{1,0:T(8,128)(2,1)}, bf16[8,4608]{1,0:T(8,128)(2,1)S(1)}, u32[]{:S(2)}, u32[]{:S(2)}) collective-permute-start(bf16[8,4608]{1,0:T(8,128)(2,1)} %refs_0_.1), channel_id=1, source_target_pairs={{0,16},{1,17},{2,18},{3,19},{4,20},{5,21},{6,22},{7,23},{8,9},{9,8... | collective-permute-start | bytes 221192 | tf_op jit(solution)/shard_map/ppermute | solution.py:198
  5.8 1.9 %collective-permute-start.2 = (bf16[8,4608]{1,0:T(8,128)(2,1)}, bf16[8,4608]{1,0:T(8,128)(2,1)S(1)}, u32[]{:S(2)}, u32[]{:S(2)}) collective-permute-start(bf16[8,4608]{1,0:T(8,128)(2,1)} %refs_0_.1), channel_id=1, source_target_pairs={{0,16},{1,17},{2,18},{3,19},{4,20},{5,21},{6,22},{7,23},{8,11},{9,... | collective-permute-start | bytes 221192 | tf_op jit(solution)/shard_map/ppermute | solution.py:198
  8.2 1.5 %collective-permute-start.6 = (bf16[8,4608]{1,0:T(8,128)(2,1)S(1)}, bf16[8,4608]{1,0:T(8,128)(2,1)S(1)}, u32[]{:S(2)}, u32[]{:S(2)}) collective-permute-start(bf16[8,4608]{1,0:T(8,128)(2,1)S(1)} %collective-permute-done.5.refs_6_), channel_id=1, source_target_pairs={{0,16},{1,17},{2,18},{3,19},{4,20},{5,21},{6,22},{7,23},{8,9},{9,8... | collective-permute-start | bytes 221192 | tf_op jit(solution)/shard_map/ppermute | solution.py:198
  13.0 5.0 %collective-permute-start.8 = (bf16[8,4608]{1,0:T(8,128)(2,1)S(1)}, bf16[8,4608]{1,0:T(8,128)(2,1)S(1)}, u32[]{:S(2)}, u32[]{:S(2)}) collective-permute-start(bf16[8,4608]{1,0:T(8,128)(2,1)S(1)} %get-tuple-element.53), channel_id=1, source_target_pairs={{0,16},{1,17},{2,18},{3,19},{4,20},{5,21},{6,22},{7,23},{8,9},{9,8... | collective-permute-start | bytes 221192 | tf_op jit(solution)/shard_map/ppermute | solution.py:198
  18.1 1.9 %collective-permute-start.12 = (bf16[8,4608]{1,0:T(8,128)(2,1)S(1)}, bf16[8,4608]{1,0:T(8,128)(2,1)S(1)}, u32[]{:S(2)}, u32[]{:S(2)}) collective-permute-start(bf16[8,4608]{1,0:T(8,128)(2,1)S(1)} %get-tuple-element.56), channel_id=1, source_target_pairs={{0,16},{1,17},{2,18},{3,19},{4,20},{5,21},{6,22},{7,23},{8,14},{9,... | collective-permute-start | bytes 221192 | tf_op jit(solution)/shard_map/ppermute | solution.py:198
  20.1 1.9 %collective-permute-start.7 = (bf16[8,4608]{1,0:T(8,128)(2,1)S(1)}, bf16[8,4608]{1,0:T(8,128)(2,1)S(1)}, u32[]{:S(2)}, u32[]{:S(2)}) collective-permute-start(bf16[8,4608]{1,0:T(8,128)(2,1)S(1)} %get-tuple-element.51), channel_id=1, source_target_pairs={{0,16},{1,17},{2,18},{3,19},{4,20},{5,21},{6,22},{7,23},{8,15},{9,... | collective-permute-start | bytes 221192 | tf_op jit(solution)/shard_map/ppermute | solution.py:198
  22.4 1.8 %collective-permute-start.11 = (bf16[8,4608]{1,0:T(8,128)(2,1)S(1)}, bf16[8,4608]{1,0:T(8,128)(2,1)S(1)}, u32[]{:S(2)}, u32[]{:S(2)}) collective-permute-start(bf16[8,4608]{1,0:T(8,128)(2,1)S(1)} %add_convert_fusion.6), channel_id=1, source_target_pairs={{0,16},{1,17},{2,18},{3,19},{4,20},{5,21},{6,22},{7,23},{8,12},{9,... | collective-permute-start | bytes 221192 | tf_op jit(solution)/shard_map/ppermute | solution.py:198
  25.1 1.3 %collective-permute-done.9 = bf16[8,4608]{1,0:T(8,128)(2,1)S(1)} collective-permute-done((bf16[8,4608]{1,0:T(8,128)(2,1)S(1)}, bf16[8,4608]{1,0:T(8,128)(2,1)S(1)}, u32[]{:S(2)}, u32[]{:S(2)}) %collective-permute-start.9) | collective-permute-done | bytes 73760 | tf_op jit(solution)/shard_map/ppermute | solution.py:198
  27.4 1.7 %collective-permute-start.18 = (bf16[8,4608]{1,0:T(8,128)(2,1)S(1)}, bf16[8,4608]{1,0:T(8,128)(2,1)S(1)}, u32[]{:S(2)}, u32[]{:S(2)}) collective-permute-start(bf16[8,4608]{1,0:T(8,128)(2,1)S(1)} %get-tuple-element.96), channel_id=1, source_target_pairs={{0,8},{1,9},{2,10},{3,11},{4,12},{5,13},{6,14},{7,15},{8,4},{9,5},... | collective-permute-start | bytes 221192 | tf_op jit(solution)/shard_map/ppermute | solution.py:204
  30.2 1.6 %collective-permute-start.20 = (bf16[8,4608]{1,0:T(8,128)(2,1)S(1)}, bf16[8,4608]{1,0:T(8,128)(2,1)S(1)}, u32[]{:S(2)}, u32[]{:S(2)}) collective-permute-start(bf16[8,4608]{1,0:T(8,128)(2,1)S(1)} %get-tuple-element.96), channel_id=1, source_target_pairs={{0,8},{1,9},{2,10},{3,11},{4,12},{5,13},{6,14},{7,15},{8,6},{9,7},... | collective-permute-start | bytes 221192 | tf_op jit(solution)/shard_map/ppermute | solution.py:204
  32.2 1.9 %collective-permute-done.18.refs_4_ = bf16[8,4608]{1,0:T(8,128)(2,1)S(1)} collective-permute-done((bf16[8,4608]{1,0:T(8,128)(2,1)S(1)}, bf16[8,4608]{1,0:T(8,128)(2,1)S(1)}, u32[]{:S(2)}, u32[]{:S(2)}) %collective-permute-start.18) | collective-permute-done | bytes 73760 | tf_op jit(solution)/shard_map/ppermute | solution.py:204
  34.1 1.5 %collective-permute-start.17 = (bf16[8,4608]{1,0:T(8,128)(2,1)S(1)}, bf16[8,4608]{1,0:T(8,128)(2,1)S(1)}, u32[]{:S(2)}, u32[]{:S(2)}) collective-permute-start(bf16[8,4608]{1,0:T(8,128)(2,1)S(1)} %collective-permute-done.16.refs_2_), channel_id=1, source_target_pairs={{0,1},{1,0},{2,3},{3,2},{4,5},{5,4},{6,7},{7,6},{8,24},{9,25},{10,... | collective-permute-start | bytes 221192 | tf_op jit(solution)/shard_map/ppermute | solution.py:198
  36.1 2.2 %collective-permute-done.21.refs_7_ = bf16[8,4608]{1,0:T(8,128)(2,1)S(1)} collective-permute-done((bf16[8,4608]{1,0:T(8,128)(2,1)S(1)}, bf16[8,4608]{1,0:T(8,128)(2,1)S(1)}, u32[]{:S(2)}, u32[]{:S(2)}) %collective-permute-start.21) | collective-permute-done | bytes 73760 | tf_op jit(solution)/shard_map/ppermute | solution.py:204
  40.9 1.2 %collective-permute-start.27 = (bf16[8,4608]{1,0:T(8,128)(2,1)S(1)}, bf16[8,4608]{1,0:T(8,128)(2,1)S(1)}, u32[]{:S(2)}, u32[]{:S(2)}) collective-permute-start(bf16[8,4608]{1,0:T(8,128)(2,1)S(1)} %get-tuple-element.67), channel_id=1, source_target_pairs={{0,1},{1,0},{2,3},{3,2},{4,5},{5,4},{6,7},{7,6},{8,24},{9,25},{10,... | collective-permute-start | bytes 221192 | tf_op jit(solution)/shard_map/ppermute | solution.py:198
  42.1 3.3 %collective-permute-start.24 = (bf16[8,4608]{1,0:T(8,128)(2,1)S(1)}, bf16[8,4608]{1,0:T(8,128)(2,1)S(1)}, u32[]{:S(2)}, u32[]{:S(2)}) collective-permute-start(bf16[8,4608]{1,0:T(8,128)(2,1)S(1)} %get-tuple-element.63), channel_id=1, source_target_pairs={{0,8},{1,9},{2,10},{3,11},{4,12},{5,13},{6,14},{7,15},{8,0},{9,1},... | collective-permute-start | bytes 221192 | tf_op jit(solution)/shard_map/ppermute | solution.py:210
  45.8 1.3 %collective-permute-start.29 = (bf16[8,4608]{1,0:T(8,128)(2,1)S(1)}, bf16[8,4608]{1,0:T(8,128)(2,1)S(1)}, u32[]{:S(2)}, u32[]{:S(2)}) collective-permute-start(bf16[8,4608]{1,0:T(8,128)(2,1)S(1)} %get-tuple-element.68), channel_id=1, source_target_pairs={{0,13},{1,12},{2,15},{3,14},{4,9},{5,8},{6,11},{7,10},{8,0},{9,1},... | collective-permute-start | bytes 221192 | tf_op jit(solution)/shard_map/ppermute | solution.py:210
  51.0 2.7 %collective-permute-start.30 = (bf16[8,4608]{1,0:T(8,128)(2,1)S(1)}, bf16[8,4608]{1,0:T(8,128)(2,1)S(1)}, u32[]{:S(2)}, u32[]{:S(2)}) collective-permute-start(bf16[8,4608]{1,0:T(8,128)(2,1)S(1)} %get-tuple-element.94), channel_id=1, source_target_pairs={{24,8},{25,9},{26,10},{27,11},{28,12},{29,13},{30,14},{31,15},{8,0... | collective-permute-start | bytes 221192 | tf_op jit(solution)/shard_map/ppermute | solution.py:218
  53.7 1.3 %collective-permute-start.31 = (bf16[8,4608]{1,0:T(8,128)(2,1)S(1)}, bf16[8,4608]{1,0:T(8,128)(2,1)S(1)}, u32[]{:S(2)}, u32[]{:S(2)}) collective-permute-start(bf16[8,4608]{1,0:T(8,128)(2,1)S(1)} %get-tuple-element.94), channel_id=1, source_target_pairs={{24,9},{25,8},{26,11},{27,10},{28,13},{29,12},{30,15},{31,14},{8,0... | collective-permute-start | bytes 221192 | tf_op jit(solution)/shard_map/ppermute | solution.py:218
  55.9 2.6 %collective-permute-start.35 = (bf16[8,4608]{1,0:T(8,128)(2,1)S(1)}, bf16[8,4608]{1,0:T(8,128)(2,1)S(1)}, u32[]{:S(2)}, u32[]{:S(2)}) collective-permute-start(bf16[8,4608]{1,0:T(8,128)(2,1)S(1)} %get-tuple-element.94), channel_id=1, source_target_pairs={{24,13},{25,12},{26,15},{27,14},{28,9},{29,8},{30,11},{31,10},{8,0... | collective-permute-start | bytes 221192 | tf_op jit(solution)/shard_map/ppermute | solution.py:218
  62.1 3.8 %shard_map.80 = (bf16[8,8,512]{2,1,0:T(8,128)(2,1)}, bf16[8,4608]{1,0:T(8,128)(2,1)S(1)}, bf16[8,4608]{1,0:T(8,128)(2,1)S(1)}, bf16[8,4608]{1,0:T(8,128)(2,1)S(1...) custom-call(bf16[8,4608]{1,0:T(8,128)(2,1)S(1)} %collective-permute-, ...), custom_call_target="tpu_custom_call", output_to_operand_aliasing={{0}: (13, {})} | custom-call | flops 603979776 | bytes 9437184 | tf_op jit(solution)/shard_map/pallas_call | solution.py:226
  66.0 2.0 %collective-permute-start.41 = (bf16[8,4608]{1,0:T(8,128)(2,1)S(1)}, bf16[8,4608]{1,0:T(8,128)(2,1)S(1)}, u32[]{:S(2)}, u32[]{:S(2)}) collective-permute-start(bf16[8,4608]{1,0:T(8,128)(2,1)S(1)} %get-tuple-element.77), channel_id=1, source_target_pairs={{0,16},{1,17},{2,18},{3,19},{4,20},{5,21},{6,22},{7,23},{8,9},{9,8... | collective-permute-start | bytes 221192 | tf_op jit(solution)/shard_map/ppermute | solution.py:198
  68.1 1.9 %collective-permute-start.43 = (bf16[8,4608]{1,0:T(8,128)(2,1)S(1)}, bf16[8,4608]{1,0:T(8,128)(2,1)S(1)}, u32[]{:S(2)}, u32[]{:S(2)}) collective-permute-start(bf16[8,4608]{1,0:T(8,128)(2,1)S(1)} %get-tuple-element.78), channel_id=1, source_target_pairs={{0,16},{1,17},{2,18},{3,19},{4,20},{5,21},{6,22},{7,23},{8,14},{9,... | collective-permute-start | bytes 221192 | tf_op jit(solution)/shard_map/ppermute | solution.py:198
  70.3 1.8 %collective-permute-start.40 = (bf16[8,4608]{1,0:T(8,128)(2,1)S(1)}, bf16[8,4608]{1,0:T(8,128)(2,1)S(1)}, u32[]{:S(2)}, u32[]{:S(2)}) collective-permute-start(bf16[8,4608]{1,0:T(8,128)(2,1)S(1)} %add_convert_fusion.3), channel_id=1, source_target_pairs={{0,16},{1,17},{2,18},{3,19},{4,20},{5,21},{6,22},{7,23},{8,10},{9,... | collective-permute-start | bytes 221192 | tf_op jit(solution)/shard_map/ppermute | solution.py:198
  73.1 1.2 %collective-permute-done.44 = bf16[8,4608]{1,0:T(8,128)(2,1)S(1)} collective-permute-done((bf16[8,4608]{1,0:T(8,128)(2,1)S(1)}, bf16[8,4608]{1,0:T(8,128)(2,1)S(1)}, u32[]{:S(2)}, u32[]{:S(2)}) %collective-permute-start.44) | collective-permute-done | bytes 73760 | tf_op jit(solution)/shard_map/ppermute | solution.py:198
  75.2 1.4 %collective-permute-done.42 = bf16[8,4608]{1,0:T(8,128)(2,1)S(1)} collective-permute-done((bf16[8,4608]{1,0:T(8,128)(2,1)S(1)}, bf16[8,4608]{1,0:T(8,128)(2,1)S(1)}, u32[]{:S(2)}, u32[]{:S(2)}) %collective-permute-start.42) | collective-permute-done | bytes 73760 | tf_op jit(solution)/shard_map/ppermute | solution.py:198
  76.7 2.3 %collective-permute-start.47 = (bf16[8,4608]{1,0:T(8,128)(2,1)S(1)}, bf16[8,4608]{1,0:T(8,128)(2,1)S(1)}, u32[]{:S(2)}, u32[]{:S(2)}) collective-permute-start(bf16[8,4608]{1,0:T(8,128)(2,1)S(1)} %get-tuple-element.92), channel_id=1, source_target_pairs={{0,8},{1,9},{2,10},{3,11},{4,12},{5,13},{6,14},{7,15},{8,2},{9,3},... | collective-permute-start | bytes 221192 | tf_op jit(solution)/shard_map/ppermute | solution.py:204
  79.3 1.7 %collective-permute-start.45 = (bf16[8,4608]{1,0:T(8,128)(2,1)S(1)}, bf16[8,4608]{1,0:T(8,128)(2,1)S(1)}, u32[]{:S(2)}, u32[]{:S(2)}) collective-permute-start(bf16[8,4608]{1,0:T(8,128)(2,1)S(1)} %get-tuple-element.92), channel_id=1, source_target_pairs={{0,8},{1,9},{2,10},{3,11},{4,12},{5,13},{6,14},{7,15},{8,0},{9,1},... | collective-permute-start | bytes 221192 | tf_op jit(solution)/shard_map/ppermute | solution.py:204
  81.0 1.4 %collective-permute-start.51 = (bf16[8,4608]{1,0:T(8,128)(2,1)S(1)}, bf16[8,4608]{1,0:T(8,128)(2,1)S(1)}, u32[]{:S(2)}, u32[]{:S(2)}) collective-permute-start(bf16[8,4608]{1,0:T(8,128)(2,1)S(1)} %get-tuple-element.92), channel_id=1, source_target_pairs={{0,8},{1,9},{2,10},{3,11},{4,12},{5,13},{6,14},{7,15},{8,6},{9,7},... | collective-permute-start | bytes 221192 | tf_op jit(solution)/shard_map/ppermute | solution.py:204
  86.7 2.3 %collective-permute-done.52.refs_7_ = bf16[8,4608]{1,0:T(8,128)(2,1)S(1)} collective-permute-done((bf16[8,4608]{1,0:T(8,128)(2,1)S(1)}, bf16[8,4608]{1,0:T(8,128)(2,1)S(1)}, u32[]{:S(2)}, u32[]{:S(2)}) %collective-permute-start.52) | collective-permute-done | bytes 73760 | tf_op jit(solution)/shard_map/ppermute | solution.py:204
  89.6 2.5 %shard_map.81 = (bf16[8,8,512]{2,1,0:T(8,128)(2,1)}, bf16[8,4608]{1,0:T(8,128)(2,1)S(1)}, bf16[8,4608]{1,0:T(8,128)(2,1)S(1)}, bf16[8,4608]{1,0:T(8,128)(2,1)S(1...) custom-call(bf16[8,4608]{1,0:T(8,128)(2,1)S(1)} %collective-permute-, ...), custom_call_target="tpu_custom_call", output_to_operand_aliasing={{0}: (11, {})} | custom-call | flops 603979776 | bytes 9437184 | tf_op jit(solution)/shard_map/pallas_call | solution.py:226
  101.2 2.0 %collective-permute-start.61 = (f32[8,4608]{1,0:T(8,128)S(1)}, f32[8,4608]{1,0:T(8,128)S(1)}, u32[]{:S(2)}, u32[]{:S(2)}) collective-permute-start(f32[8,4608]{1,0:T(8,128)S(1)} %broadcast_select_fusion), channel_id=1, source_target_pairs={{0,8},{1,9},{2,10},{3,11},{4,12},{5,13},{6,14},{7,15},{8,0},{9,1},... | collective-permute-start | bytes 442376 | tf_op jit(solution)/shard_map/ppermute | solution.py:204
  (112 shorter events, 38.2 us)
Async XLA Ops:
  0.6 7.1 %collective-permute-start.3 = (bf16[8,4608]{1,0:T(8,128)(2,1)}, bf16[8,4608]{1,0:T(8,128)(2,1)S(1)}, u32[]{:S(2)}, u32[]{:S(2)}) collective-permute-start(bf16[8,4608]{1,0:T(8,128)(2,1)} %refs_0_.1), channel_id=1, source_target_pairs={{0,16},{1,17},{2,18},{3,19},{4,20},{5,21},{6,22},{7,23},{8,12},{9,... | collective-permute-start | bytes 221192 | tf_op jit(solution)/shard_map/ppermute | solution.py:198
  3.8 7.1 %collective-permute-start = (bf16[8,4608]{1,0:T(8,128)(2,1)}, bf16[8,4608]{1,0:T(8,128)(2,1)S(1)}, u32[]{:S(2)}, u32[]{:S(2)}) collective-permute-start(bf16[8,4608]{1,0:T(8,128)(2,1)} %refs_0_.1), channel_id=1, source_target_pairs={{0,16},{1,17},{2,18},{3,19},{4,20},{5,21},{6,22},{7,23},{8,9},{9,8... | collective-permute-start | bytes 221192 | tf_op jit(solution)/shard_map/ppermute | solution.py:198
  5.7 5.1 %collective-permute-start.1 = (bf16[8,4608]{1,0:T(8,128)(2,1)}, bf16[8,4608]{1,0:T(8,128)(2,1)S(1)}, u32[]{:S(2)}, u32[]{:S(2)}) collective-permute-start(bf16[8,4608]{1,0:T(8,128)(2,1)} %refs_0_.1), channel_id=1, source_target_pairs={{0,16},{1,17},{2,18},{3,19},{4,20},{5,21},{6,22},{7,23},{8,10},{9,... | collective-permute-start | bytes 221192 | tf_op jit(solution)/shard_map/ppermute | solution.py:198
  5.8 5.3 %collective-permute-start.2 = (bf16[8,4608]{1,0:T(8,128)(2,1)}, bf16[8,4608]{1,0:T(8,128)(2,1)S(1)}, u32[]{:S(2)}, u32[]{:S(2)}) collective-permute-start(bf16[8,4608]{1,0:T(8,128)(2,1)} %refs_0_.1), channel_id=1, source_target_pairs={{0,16},{1,17},{2,18},{3,19},{4,20},{5,21},{6,22},{7,23},{8,11},{9,... | collective-permute-start | bytes 221192 | tf_op jit(solution)/shard_map/ppermute | solution.py:198
  8.2 4.6 %collective-permute-start.6 = (bf16[8,4608]{1,0:T(8,128)(2,1)S(1)}, bf16[8,4608]{1,0:T(8,128)(2,1)S(1)}, u32[]{:S(2)}, u32[]{:S(2)}) collective-permute-start(bf16[8,4608]{1,0:T(8,128)(2,1)S(1)} %collective-permute-done.5.refs_6_), channel_id=1, source_target_pairs={{0,16},{1,17},{2,18},{3,19},{4,20},{5,21},{6,22},{7,23},{8,9},{9,8... | collective-permute-start | bytes 221192 | tf_op jit(solution)/shard_map/ppermute | solution.py:198
  13.0 9.1 %collective-permute-start.8 = (bf16[8,4608]{1,0:T(8,128)(2,1)S(1)}, bf16[8,4608]{1,0:T(8,128)(2,1)S(1)}, u32[]{:S(2)}, u32[]{:S(2)}) collective-permute-start(bf16[8,4608]{1,0:T(8,128)(2,1)S(1)} %get-tuple-element.53), channel_id=1, source_target_pairs={{0,16},{1,17},{2,18},{3,19},{4,20},{5,21},{6,22},{7,23},{8,9},{9,8... | collective-permute-start | bytes 221192 | tf_op jit(solution)/shard_map/ppermute | solution.py:198
  18.1 6.2 %collective-permute-start.12 = (bf16[8,4608]{1,0:T(8,128)(2,1)S(1)}, bf16[8,4608]{1,0:T(8,128)(2,1)S(1)}, u32[]{:S(2)}, u32[]{:S(2)}) collective-permute-start(bf16[8,4608]{1,0:T(8,128)(2,1)S(1)} %get-tuple-element.56), channel_id=1, source_target_pairs={{0,16},{1,17},{2,18},{3,19},{4,20},{5,21},{6,22},{7,23},{8,14},{9,... | collective-permute-start | bytes 221192 | tf_op jit(solution)/shard_map/ppermute | solution.py:198
  20.1 5.1 %collective-permute-start.7 = (bf16[8,4608]{1,0:T(8,128)(2,1)S(1)}, bf16[8,4608]{1,0:T(8,128)(2,1)S(1)}, u32[]{:S(2)}, u32[]{:S(2)}) collective-permute-start(bf16[8,4608]{1,0:T(8,128)(2,1)S(1)} %get-tuple-element.51), channel_id=1, source_target_pairs={{0,16},{1,17},{2,18},{3,19},{4,20},{5,21},{6,22},{7,23},{8,15},{9,... | collective-permute-start | bytes 221192 | tf_op jit(solution)/shard_map/ppermute | solution.py:198
  22.4 4.8 %collective-permute-start.11 = (bf16[8,4608]{1,0:T(8,128)(2,1)S(1)}, bf16[8,4608]{1,0:T(8,128)(2,1)S(1)}, u32[]{:S(2)}, u32[]{:S(2)}) collective-permute-start(bf16[8,4608]{1,0:T(8,128)(2,1)S(1)} %add_convert_fusion.6), channel_id=1, source_target_pairs={{0,16},{1,17},{2,18},{3,19},{4,20},{5,21},{6,22},{7,23},{8,12},{9,... | collective-permute-start | bytes 221192 | tf_op jit(solution)/shard_map/ppermute | solution.py:198
  27.4 6.7 %collective-permute-start.18 = (bf16[8,4608]{1,0:T(8,128)(2,1)S(1)}, bf16[8,4608]{1,0:T(8,128)(2,1)S(1)}, u32[]{:S(2)}, u32[]{:S(2)}) collective-permute-start(bf16[8,4608]{1,0:T(8,128)(2,1)S(1)} %get-tuple-element.96), channel_id=1, source_target_pairs={{0,8},{1,9},{2,10},{3,11},{4,12},{5,13},{6,14},{7,15},{8,4},{9,5},... | collective-permute-start | bytes 221192 | tf_op jit(solution)/shard_map/ppermute | solution.py:204
  29.1 6.5 %collective-permute-start.14 = (bf16[8,4608]{1,0:T(8,128)(2,1)S(1)}, bf16[8,4608]{1,0:T(8,128)(2,1)S(1)}, u32[]{:S(2)}, u32[]{:S(2)}) collective-permute-start(bf16[8,4608]{1,0:T(8,128)(2,1)S(1)} %get-tuple-element.96), channel_id=1, source_target_pairs={{0,8},{1,9},{2,10},{3,11},{4,12},{5,13},{6,14},{7,15},{8,0},{9,1},... | collective-permute-start | bytes 221192 | tf_op jit(solution)/shard_map/ppermute | solution.py:204
  30.2 6.0 %collective-permute-start.15 = (bf16[8,4608]{1,0:T(8,128)(2,1)S(1)}, bf16[8,4608]{1,0:T(8,128)(2,1)S(1)}, u32[]{:S(2)}, u32[]{:S(2)}) collective-permute-start(bf16[8,4608]{1,0:T(8,128)(2,1)S(1)} %get-tuple-element.96), channel_id=1, source_target_pairs={{0,8},{1,9},{2,10},{3,11},{4,12},{5,13},{6,14},{7,15},{8,1},{9,0},... | collective-permute-start | bytes 221192 | tf_op jit(solution)/shard_map/ppermute | solution.py:204
  30.2 6.0 %collective-permute-start.20 = (bf16[8,4608]{1,0:T(8,128)(2,1)S(1)}, bf16[8,4608]{1,0:T(8,128)(2,1)S(1)}, u32[]{:S(2)}, u32[]{:S(2)}) collective-permute-start(bf16[8,4608]{1,0:T(8,128)(2,1)S(1)} %get-tuple-element.96), channel_id=1, source_target_pairs={{0,8},{1,9},{2,10},{3,11},{4,12},{5,13},{6,14},{7,15},{8,6},{9,7},... | collective-permute-start | bytes 221192 | tf_op jit(solution)/shard_map/ppermute | solution.py:204
  31.8 6.5 %collective-permute-start.21 = (bf16[8,4608]{1,0:T(8,128)(2,1)S(1)}, bf16[8,4608]{1,0:T(8,128)(2,1)S(1)}, u32[]{:S(2)}, u32[]{:S(2)}) collective-permute-start(bf16[8,4608]{1,0:T(8,128)(2,1)S(1)} %get-tuple-element.96), channel_id=1, source_target_pairs={{0,8},{1,9},{2,10},{3,11},{4,12},{5,13},{6,14},{7,15},{8,7},{9,6},... | collective-permute-start | bytes 221192 | tf_op jit(solution)/shard_map/ppermute | solution.py:204
  34.1 4.9 %collective-permute-start.17 = (bf16[8,4608]{1,0:T(8,128)(2,1)S(1)}, bf16[8,4608]{1,0:T(8,128)(2,1)S(1)}, u32[]{:S(2)}, u32[]{:S(2)}) collective-permute-start(bf16[8,4608]{1,0:T(8,128)(2,1)S(1)} %collective-permute-done.16.refs_2_), channel_id=1, source_target_pairs={{0,1},{1,0},{2,3},{3,2},{4,5},{5,4},{6,7},{7,6},{8,24},{9,25},{10,... | collective-permute-start | bytes 221192 | tf_op jit(solution)/shard_map/ppermute | solution.py:198
  40.0 5.8 %collective-permute-start.22 = (bf16[8,4608]{1,0:T(8,128)(2,1)S(1)}, bf16[8,4608]{1,0:T(8,128)(2,1)S(1)}, u32[]{:S(2)}, u32[]{:S(2)}) collective-permute-start(bf16[8,4608]{1,0:T(8,128)(2,1)S(1)} %get-tuple-element.62), channel_id=1, source_target_pairs={{0,1},{1,0},{2,3},{3,2},{4,5},{5,4},{6,7},{7,6},{8,24},{9,25},{10,... | collective-permute-start | bytes 221192 | tf_op jit(solution)/shard_map/ppermute | solution.py:198
  40.9 6.2 %collective-permute-start.27 = (bf16[8,4608]{1,0:T(8,128)(2,1)S(1)}, bf16[8,4608]{1,0:T(8,128)(2,1)S(1)}, u32[]{:S(2)}, u32[]{:S(2)}) collective-permute-start(bf16[8,4608]{1,0:T(8,128)(2,1)S(1)} %get-tuple-element.67), channel_id=1, source_target_pairs={{0,1},{1,0},{2,3},{3,2},{4,5},{5,4},{6,7},{7,6},{8,24},{9,25},{10,... | collective-permute-start | bytes 221192 | tf_op jit(solution)/shard_map/ppermute | solution.py:198
  42.1 6.0 %collective-permute-start.24 = (bf16[8,4608]{1,0:T(8,128)(2,1)S(1)}, bf16[8,4608]{1,0:T(8,128)(2,1)S(1)}, u32[]{:S(2)}, u32[]{:S(2)}) collective-permute-start(bf16[8,4608]{1,0:T(8,128)(2,1)S(1)} %get-tuple-element.63), channel_id=1, source_target_pairs={{0,8},{1,9},{2,10},{3,11},{4,12},{5,13},{6,14},{7,15},{8,0},{9,1},... | collective-permute-start | bytes 221192 | tf_op jit(solution)/shard_map/ppermute | solution.py:210
  51.0 4.8 %collective-permute-start.30 = (bf16[8,4608]{1,0:T(8,128)(2,1)S(1)}, bf16[8,4608]{1,0:T(8,128)(2,1)S(1)}, u32[]{:S(2)}, u32[]{:S(2)}) collective-permute-start(bf16[8,4608]{1,0:T(8,128)(2,1)S(1)} %get-tuple-element.94), channel_id=1, source_target_pairs={{24,8},{25,9},{26,10},{27,11},{28,12},{29,13},{30,14},{31,15},{8,0... | collective-permute-start | bytes 221192 | tf_op jit(solution)/shard_map/ppermute | solution.py:218
  53.7 4.8 %collective-permute-start.31 = (bf16[8,4608]{1,0:T(8,128)(2,1)S(1)}, bf16[8,4608]{1,0:T(8,128)(2,1)S(1)}, u32[]{:S(2)}, u32[]{:S(2)}) collective-permute-start(bf16[8,4608]{1,0:T(8,128)(2,1)S(1)} %get-tuple-element.94), channel_id=1, source_target_pairs={{24,9},{25,8},{26,11},{27,10},{28,13},{29,12},{30,15},{31,14},{8,0... | collective-permute-start | bytes 221192 | tf_op jit(solution)/shard_map/ppermute | solution.py:218
  66.0 6.2 %collective-permute-start.41 = (bf16[8,4608]{1,0:T(8,128)(2,1)S(1)}, bf16[8,4608]{1,0:T(8,128)(2,1)S(1)}, u32[]{:S(2)}, u32[]{:S(2)}) collective-permute-start(bf16[8,4608]{1,0:T(8,128)(2,1)S(1)} %get-tuple-element.77), channel_id=1, source_target_pairs={{0,16},{1,17},{2,18},{3,19},{4,20},{5,21},{6,22},{7,23},{8,9},{9,8... | collective-permute-start | bytes 221192 | tf_op jit(solution)/shard_map/ppermute | solution.py:198
  68.1 5.1 %collective-permute-start.43 = (bf16[8,4608]{1,0:T(8,128)(2,1)S(1)}, bf16[8,4608]{1,0:T(8,128)(2,1)S(1)}, u32[]{:S(2)}, u32[]{:S(2)}) collective-permute-start(bf16[8,4608]{1,0:T(8,128)(2,1)S(1)} %get-tuple-element.78), channel_id=1, source_target_pairs={{0,16},{1,17},{2,18},{3,19},{4,20},{5,21},{6,22},{7,23},{8,14},{9,... | collective-permute-start | bytes 221192 | tf_op jit(solution)/shard_map/ppermute | solution.py:198
  70.3 4.8 %collective-permute-start.40 = (bf16[8,4608]{1,0:T(8,128)(2,1)S(1)}, bf16[8,4608]{1,0:T(8,128)(2,1)S(1)}, u32[]{:S(2)}, u32[]{:S(2)}) collective-permute-start(bf16[8,4608]{1,0:T(8,128)(2,1)S(1)} %add_convert_fusion.3), channel_id=1, source_target_pairs={{0,16},{1,17},{2,18},{3,19},{4,20},{5,21},{6,22},{7,23},{8,10},{9,... | collective-permute-start | bytes 221192 | tf_op jit(solution)/shard_map/ppermute | solution.py:198
  76.7 5.7 %collective-permute-start.47 = (bf16[8,4608]{1,0:T(8,128)(2,1)S(1)}, bf16[8,4608]{1,0:T(8,128)(2,1)S(1)}, u32[]{:S(2)}, u32[]{:S(2)}) collective-permute-start(bf16[8,4608]{1,0:T(8,128)(2,1)S(1)} %get-tuple-element.92), channel_id=1, source_target_pairs={{0,8},{1,9},{2,10},{3,11},{4,12},{5,13},{6,14},{7,15},{8,2},{9,3},... | collective-permute-start | bytes 221192 | tf_op jit(solution)/shard_map/ppermute | solution.py:204
  78.9 4.7 %collective-permute-start.49 = (bf16[8,4608]{1,0:T(8,128)(2,1)S(1)}, bf16[8,4608]{1,0:T(8,128)(2,1)S(1)}, u32[]{:S(2)}, u32[]{:S(2)}) collective-permute-start(bf16[8,4608]{1,0:T(8,128)(2,1)S(1)} %get-tuple-element.92), channel_id=1, source_target_pairs={{0,8},{1,9},{2,10},{3,11},{4,12},{5,13},{6,14},{7,15},{8,4},{9,5},... | collective-permute-start | bytes 221192 | tf_op jit(solution)/shard_map/ppermute | solution.py:204
  79.3 5.1 %collective-permute-start.45 = (bf16[8,4608]{1,0:T(8,128)(2,1)S(1)}, bf16[8,4608]{1,0:T(8,128)(2,1)S(1)}, u32[]{:S(2)}, u32[]{:S(2)}) collective-permute-start(bf16[8,4608]{1,0:T(8,128)(2,1)S(1)} %get-tuple-element.92), channel_id=1, source_target_pairs={{0,8},{1,9},{2,10},{3,11},{4,12},{5,13},{6,14},{7,15},{8,0},{9,1},... | collective-permute-start | bytes 221192 | tf_op jit(solution)/shard_map/ppermute | solution.py:204
  81.0 4.6 %collective-permute-start.46 = (bf16[8,4608]{1,0:T(8,128)(2,1)S(1)}, bf16[8,4608]{1,0:T(8,128)(2,1)S(1)}, u32[]{:S(2)}, u32[]{:S(2)}) collective-permute-start(bf16[8,4608]{1,0:T(8,128)(2,1)S(1)} %get-tuple-element.92), channel_id=1, source_target_pairs={{0,8},{1,9},{2,10},{3,11},{4,12},{5,13},{6,14},{7,15},{8,1},{9,0},... | collective-permute-start | bytes 221192 | tf_op jit(solution)/shard_map/ppermute | solution.py:204
  81.0 5.7 %collective-permute-start.51 = (bf16[8,4608]{1,0:T(8,128)(2,1)S(1)}, bf16[8,4608]{1,0:T(8,128)(2,1)S(1)}, u32[]{:S(2)}, u32[]{:S(2)}) collective-permute-start(bf16[8,4608]{1,0:T(8,128)(2,1)S(1)} %get-tuple-element.92), channel_id=1, source_target_pairs={{0,8},{1,9},{2,10},{3,11},{4,12},{5,13},{6,14},{7,15},{8,6},{9,7},... | collective-permute-start | bytes 221192 | tf_op jit(solution)/shard_map/ppermute | solution.py:204
  82.4 6.6 %collective-permute-start.52 = (bf16[8,4608]{1,0:T(8,128)(2,1)S(1)}, bf16[8,4608]{1,0:T(8,128)(2,1)S(1)}, u32[]{:S(2)}, u32[]{:S(2)}) collective-permute-start(bf16[8,4608]{1,0:T(8,128)(2,1)S(1)} %get-tuple-element.92), channel_id=1, source_target_pairs={{0,8},{1,9},{2,10},{3,11},{4,12},{5,13},{6,14},{7,15},{8,7},{9,6},... | collective-permute-start | bytes 221192 | tf_op jit(solution)/shard_map/ppermute | solution.py:204
  83.6 5.4 %collective-permute-start.48 = (bf16[8,4608]{1,0:T(8,128)(2,1)S(1)}, bf16[8,4608]{1,0:T(8,128)(2,1)S(1)}, u32[]{:S(2)}, u32[]{:S(2)}) collective-permute-start(bf16[8,4608]{1,0:T(8,128)(2,1)S(1)} %collective-permute-done.47.refs_2_), channel_id=1, source_target_pairs={{0,1},{1,0},{2,3},{3,2},{4,5},{5,4},{6,7},{7,6},{8,24},{9,25},{10,... | collective-permute-start | bytes 221192 | tf_op jit(solution)/shard_map/ppermute | solution.py:198
  84.4 5.1 %collective-permute-start.50 = (bf16[8,4608]{1,0:T(8,128)(2,1)S(1)}, bf16[8,4608]{1,0:T(8,128)(2,1)S(1)}, u32[]{:S(2)}, u32[]{:S(2)}) collective-permute-start(bf16[8,4608]{1,0:T(8,128)(2,1)S(1)} %collective-permute-done.49.refs_4_), channel_id=1, source_target_pairs={{0,1},{1,0},{2,3},{3,2},{4,5},{5,4},{6,7},{7,6},{8,24},{9,25},{10,... | collective-permute-start | bytes 221192 | tf_op jit(solution)/shard_map/ppermute | solution.py:198
  94.1 4.8 %collective-permute-start.56 = (bf16[8,4608]{1,0:T(8,128)(2,1)S(1)}, bf16[8,4608]{1,0:T(8,128)(2,1)S(1)}, u32[]{:S(2)}, u32[]{:S(2)}) collective-permute-start(bf16[8,4608]{1,0:T(8,128)(2,1)S(1)} %get-tuple-element.87), channel_id=1, source_target_pairs={{0,9},{1,8},{2,11},{3,10},{4,13},{5,12},{6,15},{7,14},{8,0},{9,1},... | collective-permute-start | bytes 221192 | tf_op jit(solution)/shard_map/ppermute | solution.py:210
  (31 other events, 128.9 us)

commit v4 on v2

v4 whole, which is shorter than its diff:
```python
import functools

import jax
import jax.numpy as jnp
from jax import lax
from jax.experimental import pallas as pl
from jax.experimental.pallas import tpu as pltpu
from jax.sharding import PartitionSpec as P

BLOCK = 128
AXES = ("layer", "feat")
PLANS = {
    "gather": [
        ((6, None), (1, None), (4, None), (2, None), (3, None), (7, 6), (5, 4)),
        ((0, None), (1, None), (2, None), (4, None), (6, None), (7, None), (5, 4), (3, 2)),
        ((1, None), (2, None), (0, None), (4, None), (6, None), (7, 6), (5, 4), (3, 2)),
        ((0, None), (1, None), (2, None), (4, None), (6, None), (7, None), (5, 4), (3, 2)),
    ],
    "sum": [
        ((5, 4), (3, 2), (7, None), (2, None), (4, None), (6, None), (1, None)),
        ((7, 6), (3, 2), (6, None), (0, None), (1, None), (4, None), (2, None), (5, None)),
        ((5, 4), (3, 2), (7, None), (2, None), (4, None), (6, None), (1, None)),
        ((7, 6), (3, 2), (1, None), (0, None), (6, None), (4, None), (2, None), (5, None)),
    ],
}


CHUNKS = 4


def fetch(source, target, sems):
    rows = target.shape[0] // CHUNKS
    moves = []
    for i in range(CHUNKS):
        part = pl.ds(i * rows, rows)
        moves.append(pltpu.make_async_copy(source.at[0, part], target.at[part], sems.at[i]))
    return moves


def gate_kernel(
    by_xor, act_ref, ids_ref, counts_ref, dec_ref, enc_ref,
    gate_ref, attr_ref, dec_out, enc_out, act, ids, counts, dec, sems, dec_sems, enc_sems,
):
    del attr_ref
    dec_moves = fetch(dec_ref, dec, dec_sems)
    enc_moves = fetch(enc_ref, enc_out, enc_sems)
    moves = [
        pltpu.make_async_copy(counts_ref, counts, sems.at[0]),
        pltpu.make_async_copy(ids_ref, ids, sems.at[1]),
        pltpu.make_async_copy(act_ref, act, sems.at[2]),
    ]
    for move in moves + dec_moves + enc_moves:
        move.start()
    feat_dev = act_ref.shape[2]
    step, cut = feat_dev // CHUNKS, 512
    for i, move in enumerate(dec_moves):
        move.wait()
        here = slice(i * step, (i + 1) * step)
        for c in range(0, dec.shape[1], cut):
            dec_out[c : c + cut, here] = dec[here, c : c + cut].T
    for move in moves:
        move.wait()
    feat_index = lax.axis_index("feat")
    tiles, tok_dev, feat_dev = act_ref.shape
    blk_dev = feat_dev // BLOCK
    width = ids_ref.shape[2]
    lane = lax.broadcasted_iota(jnp.int32, (1, width), 1)
    for k in range(tiles):
        tile = feat_index ^ k if by_xor else k
        listed = lane < counts[0, tile]
        mask = []
        for block in range(blk_dev):
            match = (ids[0, pl.ds(tile, 1), :] == feat_index * blk_dev + block) & listed
            hit = jnp.max(jnp.where(match, 1.0, 0.0), axis=1, keepdims=True)
            mask.append(jnp.broadcast_to(hit, (1, BLOCK)))
        row = jnp.concatenate(mask, axis=1)
        gate_ref[k * tok_dev : (k + 1) * tok_dev, :] = act[tile].astype(jnp.float32) * row
    for move in enc_moves:
        move.wait()


def attribute_kernel(layer, tiles, *refs):
    rows, (gate_ref, dec, enc, _), refs = refs[:tiles], refs[tiles : tiles + 4], refs[tiles + 4 :]
    attr_ref, parts, (h_ref, a_ref, b_ref, sem) = refs[0], refs[1 : tiles + 1], refs[tiles + 1 :]
    layer_index = lax.axis_index("layer")
    tok_dev, width = rows[0].shape
    feat_dev = gate_ref.shape[1]
    feat_index = lax.axis_index("feat")

    @pl.when(layer_index == layer)
    def _():
        for k in range(0, tiles, 2):
            pair = jnp.concatenate([rows[k][...], rows[k + 1][...]], axis=0)
            h_ref[k * tok_dev : (k + 2) * tok_dev, :] = pair
        cut = 256
        for f in range(0, feat_dev, cut):
            scores = jnp.dot(
                h_ref[...], dec[:, f : f + cut], preferred_element_type=jnp.float32
            )
            attributed = scores * gate_ref[:, f : f + cut]
            a_ref[:, f : f + cut] = attributed.astype(jnp.bfloat16)
            for k in range(tiles):
                block = attributed[k * tok_dev : (k + 1) * tok_dev, :]
                b_ref[feat_index ^ k, :, f : f + cut] = block.astype(jnp.bfloat16)
        done = pltpu.make_async_copy(b_ref, attr_ref, sem.at[0])
        done.start()
        cut = 512
        for c in range(0, width, cut):
            product = jnp.dot(
                a_ref[...], enc[:, c : c + cut], preferred_element_type=jnp.float32
            )
            for k in range(tiles):
                part = product[k * tok_dev : (k + 1) * tok_dev, :]
                parts[k][:, c : c + cut] = part.astype(jnp.bfloat16)
        done.wait()


def body(top_grad, decoder, encoder, activations, block_ids, block_counts):
    layers = lax.axis_size("layer")
    tiles = lax.axis_size("feat")
    layer_index = lax.axis_index("layer")
    feat_index = lax.axis_index("feat")
    feat_dev, width = decoder.shape[1:]
    tok_dev = top_grad.shape[0]
    direct = tiles == 8

    vmem = pl.BlockSpec(memory_space=pltpu.VMEM)
    hbm = pl.BlockSpec(memory_space=pl.ANY)
    weight_bytes = 4 * feat_dev * width
    act_tiles = activations.reshape(tiles, tok_dev, feat_dev)
    gate, attr, dec, enc = pl.pallas_call(
        functools.partial(gate_kernel, direct),
        out_shape=(
            jax.ShapeDtypeStruct((tiles * tok_dev, feat_dev), jnp.float32),
            pltpu.HBM(act_tiles.shape, act_tiles.dtype),
            pltpu.VMEM((width, feat_dev), decoder.dtype),
            pltpu.VMEM((feat_dev, width), encoder.dtype),
        ),
        in_specs=[hbm] * 5,
        out_specs=(vmem, hbm, vmem, vmem),
        scratch_shapes=[
            pltpu.VMEM(act_tiles.shape, act_tiles.dtype),
            pltpu.VMEM(block_ids.shape, block_ids.dtype),
            pltpu.SMEM(block_counts.shape, block_counts.dtype),
            pltpu.VMEM((feat_dev, width), decoder.dtype),
            pltpu.SemaphoreType.DMA((3,)),
            pltpu.SemaphoreType.DMA((CHUNKS,)),
            pltpu.SemaphoreType.DMA((CHUNKS,)),
        ],
        compiler_params=pltpu.CompilerParams(vmem_limit_bytes=16 * 2**20),
        cost_estimate=pl.CostEstimate(flops=0, bytes_accessed=weight_bytes, transcendentals=0),
    )(
        pltpu.with_memory_space_constraint(act_tiles, pltpu.HBM),
        pltpu.with_memory_space_constraint(block_ids, pltpu.HBM),
        pltpu.with_memory_space_constraint(block_counts, pltpu.HBM),
        pltpu.with_memory_space_constraint(decoder, pltpu.HBM),
        pltpu.with_memory_space_constraint(encoder, pltpu.HBM),
    )

    def link(layer, to_layer, k):
        return [(layer * tiles + i, (to_layer % layers) * tiles + (i ^ k)) for i in range(tiles)]

    def within(value, k, odd=1):
        pairs = []
        for l in range(layers):
            pairs += link(l, l, k) if l % 2 == odd else link(l, l + 2, 0)
        return lax.ppermute(value, AXES, pairs)

    def down(value, k):
        pairs = []
        for l in range(layers):
            pairs += link(l, l - 1, k) if l % 2 else link(l, l + 1, 0)
        return lax.ppermute(value, AXES, pairs)

    def up(value, k):
        pairs = []
        for l in range(layers):
            pairs += link(l, l - 1, 0) if l % 2 else link(l, l + 1, k)
        return lax.ppermute(value, AXES, pairs)

    def skip(value, k, top):
        pairs = link(top, top - 2, k) + link(top - 2, top - 3, 0)
        pairs += link(top - 3, top - 1, 0) + link(top - 1, top, 0)
        for l in range(layers):
            if not top - 3 <= l <= top:
                pairs += link(l, l ^ 1, 0)
        return lax.ppermute(value, AXES, pairs)

    def attribute_direct(layer, rows, attr):
        block = jax.ShapeDtypeStruct((tok_dev, width), jnp.bfloat16)
        outs = pl.pallas_call(
            functools.partial(attribute_kernel, layer, tiles),
            out_shape=(pltpu.HBM(attr.shape, attr.dtype), *[block] * tiles),
            in_specs=[vmem] * (tiles + 3) + [hbm],
            out_specs=(hbm,) + (vmem,) * tiles,
            scratch_shapes=[
                pltpu.VMEM((tiles * tok_dev, width), jnp.bfloat16),
                pltpu.VMEM((tiles * tok_dev, feat_dev), jnp.bfloat16),
                pltpu.VMEM(attr.shape, attr.dtype),
                pltpu.SemaphoreType.DMA((1,)),
            ],
            input_output_aliases={tiles + 3: 0},
            compiler_params=pltpu.CompilerParams(vmem_limit_bytes=8 * 2**20),
            cost_estimate=pl.CostEstimate(
                flops=4 * tiles * tok_dev * feat_dev * width,
                bytes_accessed=weight_bytes,
                transcendentals=0,
            ),
        )(
            *rows,
            gate,
            pltpu.with_memory_space_constraint(dec, pltpu.VMEM),
            pltpu.with_memory_space_constraint(enc, pltpu.VMEM),
            attr,
        )
        return outs[0], list(outs[1:])

    def attribute(rows):
        scores = lax.dot_general(
            jnp.concatenate(rows, 0),
            decoder[0],
            (((1,), (1,)), ((), ())),
            preferred_element_type=jnp.float32,
        )
        attributed = (scores * gate).astype(jnp.bfloat16)
        part = jnp.dot(attributed, encoder[0], preferred_element_type=jnp.float32).astype(jnp.bfloat16)
        return attributed, part.reshape(tiles, tok_dev, width)

    def total(start, terms):
        for term in terms:
            start = start + term.astype(jnp.float32)
        return start

    def exchanged(values):
        return list(lax.all_to_all(values, "feat", 0, 0, tiled=True))

    def gather(value, move, odd, plan):
        rows = {0: value}
        for k, p in plan:
            rows[k] = move(value, k) if p is None else within(rows[p], k ^ p, odd)
        return [rows[k] for k in range(tiles)]

    def collect(start, part, move, odd, plan):
        met = {k: [] for k in range(tiles)}
        terms = []
        for k, p in plan:
            term = part[k]
            if met[k]:
                term = total(term.astype(jnp.float32), met[k]).astype(jnp.bfloat16)
                term = lax.optimization_barrier(term)
            if p is None:
                terms.append(move(term, k))
            else:
                met[p].append(within(term, k ^ p, odd))
        if all(k for k, _ in plan):
            terms = [part[0]] + met[0] + terms
        return total(start, terms)

    grads = [None] * layers
    grad = top_grad.astype(jnp.float32)
    sent = top_grad
    if direct:
        for high in range(layers - 1, 0, -2):
            plan = 0 if high == layers - 1 else 2
            if plan == 0:
                rows = gather(sent, within, 1, PLANS["gather"][0])
            else:
                move = functools.partial(skip, top=high + 2)
                rows = gather(sent, move, 1, PLANS["gather"][2])
                grad = rows[0].astype(jnp.float32)
            attr, part = attribute_direct(high, rows, attr)
            grad = collect(grad, part, within, 1, PLANS["sum"][plan])
            grads[high] = grad
            rows = gather(grad.astype(jnp.bfloat16), down, 0, PLANS["gather"][plan + 1])
            low = high - 1
            attr, part = attribute_direct(low, rows, attr)
            grad = collect(grad, part, up, 0, PLANS["sum"][plan + 1])
            grads[low] = grad
            sent = grad.astype(jnp.bfloat16)
        lower = grads[0]
        for high in range(3, layers, 2):
            lower = jnp.where(layer_index == high, grads[high - 1], lower)
        lower = down(lower, 0)
        grad = jnp.where(layer_index % 2 == 1, grad, lower)
        for high in range(1, layers, 2):
            grad = jnp.where(layer_index == high, grads[high], grad)
    else:
        for layer in range(layers - 1, -1, -1):
            rows = exchanged(jnp.broadcast_to(sent[None], (tiles,) + sent.shape))
            attributed, part = attribute(rows)
            attributed = attributed.reshape(attr.shape)
            attr = jnp.where(layer_index == layer, attributed, attr)
            grads[layer] = grad = total(grad, exchanged(part))
            pairs = [q for l in range(layers) for q in link(l, l - 1, 0)]
            sent = lax.ppermute(grad.astype(jnp.bfloat16), AXES, pairs)
            grad = sent.astype(jnp.float32)
        grad = grads[0]
        for layer in range(1, layers):
            grad = jnp.where(layer_index == layer, grads[layer], grad)
    return attr.reshape(1, tiles * tok_dev, feat_dev), grad[None]


def solution(mesh):
    placed = (
        P("feat", None),
        P("layer", "feat", None),
        P("layer", "feat", None),
        P("layer", None, "feat"),
        P("layer", None, None),
        P("layer", None),
    )
    return jax.shard_map(
        body,
        mesh=mesh,
        in_specs=placed,
        out_specs=(P("layer", None, "feat"), P("layer", "feat", None)),
        check_vma=False,
    )
```

time: 115 us -> 100 us (0.87)
  starting transfers between devices: 75.6 us -> 62 us
  Pallas kernels: 7.51 us -> 5.92 us
    ppermute x16 -> x12, starting transfers between devices: 15.3 us -> 6.71 us  [up(): return lax.ppermute(value, AXES, pairs)]
    ppermute x21 -> x32, starting transfers between devices: 26.4 us -> 34.3 us  [within(): return lax.ppermute(value, AXES, pairs)]
    ppermute x17 -> x13, starting transfers between devices: 20.4 us -> 12.7 us  [down(): return lax.ppermute(value, AXES, pairs)]
    ppermute x21 -> x32, waiting for transfers between devices: 9.59 us -> 16.1 us  [within(): return lax.ppermute(value, AXES, pairs)]
    ppermute x8 -> x5, starting transfers between devices: 13.4 us -> 8.33 us  [skip(): return lax.ppermute(value, AXES, pairs)]
    ppermute x17 -> x13, waiting for transfers between devices: 14.1 us -> 9.06 us  [down(): return lax.ppermute(value, AXES, pairs)]
    pallas_call x4, Pallas kernels: 6.41 us -> 1.89 us  [attribute_direct(): pl.pallas_call(functools.partial(attribute_kernel, layer, tiles), out_sha...]
    pallas_call x1, Pallas kernels: 1.1 us -> 4.03 us  [body(): pl.pallas_call(functools.partial(gate_kernel, direct), out_shape=(jax.Sha...]
  transfers between devices with their start and end apart: 62 -> 62, of which waited for: 29 -> 29; matrix products, arithmetic and copies ran while one was open for 0% -> 0% of each run, Pallas kernels for 1% -> 4%
where the time goes in v4:
time: 100 us
  starting transfers between devices  62 us (62%)
  waiting for transfers between devices  30 us (30%)
  Pallas kernels  5.92 us (6%)
  other arithmetic  1.19 us (1%)
    ppermute x32, starting transfers between devices, within(): return lax.ppermute(value, AXES, pairs)  34.3 us
    ppermute x32, waiting for transfers between devices, within(): return lax.ppermute(value, AXES, pairs)  16.1 us
    ppermute x13, starting transfers between devices, down(): return lax.ppermute(value, AXES, pairs)  12.7 us
    ppermute x13, waiting for transfers between devices, down(): return lax.ppermute(value, AXES, pairs)  9.06 us
    ppermute x5, starting transfers between devices, skip(): return lax.ppermute(value, AXES, pairs)  8.33 us
    ppermute x12, starting transfers between devices, up(): return lax.ppermute(value, AXES, pairs)  6.71 us
    ppermute x12, waiting for transfers between devices, up(): return lax.ppermute(value, AXES, pairs)  4.81 us
    pallas_call x1, Pallas kernels, body(): pl.pallas_call(functools.partial(gate_kernel, direct), out_shape=(jax.Sha...  4.03 us
  transfers between devices with their start and end apart: 62, of which 29 were waited for; matrix products, arithmetic and copies ran while one was open for 0% of the time, Pallas kernels for 4%

profile of v4, /device:TPU:0, one launch (start us, length us, event | category | flops | bytes accessed | tf_op | source)
XLA Modules:
  0.0 100.0 jit_solution(17642288205437487372)
XLA Ops:
  0.6 3.0 %collective-permute-start.3 = (bf16[8,4608]{1,0:T(8,128)(2,1)}, bf16[8,4608]{1,0:T(8,128)(2,1)S(1)}, u32[]{:S(2)}, u32[]{:S(2)}) collective-permute-start(bf16[8,4608]{1,0:T(8,128)(2,1)} %refs_0_.1), channel_id=1, source_target_pairs={{0,16},{1,17},{2,18},{3,19},{4,20},{5,21},{6,22},{7,23},{8,12},{9,... | collective-permute-start | bytes 221192 | tf_op jit(solution)/shard_map/ppermute | solution.py:167
  3.7 1.9 %collective-permute-start = (bf16[8,4608]{1,0:T(8,128)(2,1)}, bf16[8,4608]{1,0:T(8,128)(2,1)S(1)}, u32[]{:S(2)}, u32[]{:S(2)}) collective-permute-start(bf16[8,4608]{1,0:T(8,128)(2,1)} %refs_0_.1), channel_id=1, source_target_pairs={{0,16},{1,17},{2,18},{3,19},{4,20},{5,21},{6,22},{7,23},{8,9},{9,8... | collective-permute-start | bytes 221192 | tf_op jit(solution)/shard_map/ppermute | solution.py:167
  5.8 1.9 %collective-permute-start.2 = (bf16[8,4608]{1,0:T(8,128)(2,1)}, bf16[8,4608]{1,0:T(8,128)(2,1)S(1)}, u32[]{:S(2)}, u32[]{:S(2)}) collective-permute-start(bf16[8,4608]{1,0:T(8,128)(2,1)} %refs_0_.1), channel_id=1, source_target_pairs={{0,16},{1,17},{2,18},{3,19},{4,20},{5,21},{6,22},{7,23},{8,11},{9,... | collective-permute-start | bytes 221192 | tf_op jit(solution)/shard_map/ppermute | solution.py:167
  8.2 1.5 %collective-permute-start.6 = (bf16[8,4608]{1,0:T(8,128)(2,1)S(1)}, bf16[8,4608]{1,0:T(8,128)(2,1)S(1)}, u32[]{:S(2)}, u32[]{:S(2)}) collective-permute-start(bf16[8,4608]{1,0:T(8,128)(2,1)S(1)} %collective-permute-done.5.refs_6_), channel_id=1, source_target_pairs={{0,16},{1,17},{2,18},{3,19},{4,20},{5,21},{6,22},{7,23},{8,9},{9,8... | collective-permute-start | bytes 221192 | tf_op jit(solution)/shard_map/ppermute | solution.py:167
  9.8 4.0 %shard_map.77 = (f32[64,512]{1,0:T(8,128)S(1)}, bf16[8,8,512]{2,1,0:T(8,128)(2,1)}, bf16[4608,512]{1,0:T(8,128)(2,1)S(1)}, bf16[512,4608]{1,0:T(8,128)(2,1)S(1)}) custom-call(bf16[8,8,512]{2,1,0:T(8,128)(2,1)} %bitcast.5, s32[1,8,16]{2,1,0:T(8,128)} %ids_ref.1, s32[1,8]{1,0:T(1,128)} %counts_ref.1, bf16[1,512,4608]{2,1,0:T(8,128)(2,1)} %dec_ref.1, ...), custom_call_target="tpu_custom_call" | custom-call | bytes 9437184 | tf_op jit(solution)/shard_map/pallas_call | solution.py:131
  14.5 1.5 %collective-permute-start.10 = (bf16[8,4608]{1,0:T(8,128)(2,1)S(1)}, bf16[8,4608]{1,0:T(8,128)(2,1)S(1)}, u32[]{:S(2)}, u32[]{:S(2)}) collective-permute-start(bf16[8,4608]{1,0:T(8,128)(2,1)S(1)} %get-tuple-element.51), channel_id=1, source_target_pairs={{0,16},{1,17},{2,18},{3,19},{4,20},{5,21},{6,22},{7,23},{8,9},{9,8... | collective-permute-start | bytes 221192 | tf_op jit(solution)/shard_map/ppermute | solution.py:167
  16.5 1.5 %collective-permute-start.13 = (bf16[8,4608]{1,0:T(8,128)(2,1)S(1)}, bf16[8,4608]{1,0:T(8,128)(2,1)S(1)}, u32[]{:S(2)}, u32[]{:S(2)}) collective-permute-start(bf16[8,4608]{1,0:T(8,128)(2,1)S(1)} %get-tuple-element.53), channel_id=1, source_target_pairs={{0,16},{1,17},{2,18},{3,19},{4,20},{5,21},{6,22},{7,23},{8,9},{9,8... | collective-permute-start | bytes 221192 | tf_op jit(solution)/shard_map/ppermute | solution.py:167
  18.5 1.6 %collective-permute-start.9 = (bf16[8,4608]{1,0:T(8,128)(2,1)S(1)}, bf16[8,4608]{1,0:T(8,128)(2,1)S(1)}, u32[]{:S(2)}, u32[]{:S(2)}) collective-permute-start(bf16[8,4608]{1,0:T(8,128)(2,1)S(1)} %add_convert_fusion.7), channel_id=1, source_target_pairs={{0,16},{1,17},{2,18},{3,19},{4,20},{5,21},{6,22},{7,23},{8,10},{9,... | collective-permute-start | bytes 221192 | tf_op jit(solution)/shard_map/ppermute | solution.py:167
  23.2 1.4 %collective-permute-done.11 = bf16[8,4608]{1,0:T(8,128)(2,1)S(1)} collective-permute-done((bf16[8,4608]{1,0:T(8,128)(2,1)S(1)}, bf16[8,4608]{1,0:T(8,128)(2,1)S(1)}, u32[]{:S(2)}, u32[]{:S(2)}) %collective-permute-start.11) | collective-permute-done | bytes 73760 | tf_op jit(solution)/shard_map/ppermute | solution.py:167
  24.7 1.3 %collective-permute-start.16 = (bf16[8,4608]{1,0:T(8,128)(2,1)S(1)}, bf16[8,4608]{1,0:T(8,128)(2,1)S(1)}, u32[]{:S(2)}, u32[]{:S(2)}) collective-permute-start(bf16[8,4608]{1,0:T(8,128)(2,1)S(1)} %get-tuple-element.86), channel_id=1, source_target_pairs={{0,8},{1,9},{2,10},{3,11},{4,12},{5,13},{6,14},{7,15},{8,2},{9,3},... | collective-permute-start | bytes 221192 | tf_op jit(solution)/shard_map/ppermute | solution.py:173
  26.4 1.4 %collective-permute-start.14 = (bf16[8,4608]{1,0:T(8,128)(2,1)S(1)}, bf16[8,4608]{1,0:T(8,128)(2,1)S(1)}, u32[]{:S(2)}, u32[]{:S(2)}) collective-permute-start(bf16[8,4608]{1,0:T(8,128)(2,1)S(1)} %get-tuple-element.86), channel_id=1, source_target_pairs={{0,8},{1,9},{2,10},{3,11},{4,12},{5,13},{6,14},{7,15},{8,0},{9,1},... | collective-permute-start | bytes 221192 | tf_op jit(solution)/shard_map/ppermute | solution.py:173
  27.8 1.7 %collective-permute-start.20 = (bf16[8,4608]{1,0:T(8,128)(2,1)S(1)}, bf16[8,4608]{1,0:T(8,128)(2,1)S(1)}, u32[]{:S(2)}, u32[]{:S(2)}) collective-permute-start(bf16[8,4608]{1,0:T(8,128)(2,1)S(1)} %get-tuple-element.86), channel_id=1, source_target_pairs={{0,8},{1,9},{2,10},{3,11},{4,12},{5,13},{6,14},{7,15},{8,6},{9,7},... | collective-permute-start | bytes 221192 | tf_op jit(solution)/shard_map/ppermute | solution.py:173
  29.7 1.7 %collective-permute-done.18.refs_4_ = bf16[8,4608]{1,0:T(8,128)(2,1)S(1)} collective-permute-done((bf16[8,4608]{1,0:T(8,128)(2,1)S(1)}, bf16[8,4608]{1,0:T(8,128)(2,1)S(1)}, u32[]{:S(2)}, u32[]{:S(2)}) %collective-permute-start.18) | collective-permute-done | bytes 73760 | tf_op jit(solution)/shard_map/ppermute | solution.py:173
  31.4 1.5 %collective-permute-start.17 = (bf16[8,4608]{1,0:T(8,128)(2,1)S(1)}, bf16[8,4608]{1,0:T(8,128)(2,1)S(1)}, u32[]{:S(2)}, u32[]{:S(2)}) collective-permute-start(bf16[8,4608]{1,0:T(8,128)(2,1)S(1)} %collective-permute-done.16.refs_2_), channel_id=1, source_target_pairs={{0,1},{1,0},{2,3},{3,2},{4,5},{5,4},{6,7},{7,6},{8,24},{9,25},{10,... | collective-permute-start | bytes 221192 | tf_op jit(solution)/shard_map/ppermute | solution.py:167
  33.5 2.6 %collective-permute-done.21.refs_7_ = bf16[8,4608]{1,0:T(8,128)(2,1)S(1)} collective-permute-done((bf16[8,4608]{1,0:T(8,128)(2,1)S(1)}, bf16[8,4608]{1,0:T(8,128)(2,1)S(1)}, u32[]{:S(2)}, u32[]{:S(2)}) %collective-permute-start.21) | collective-permute-done | bytes 73760 | tf_op jit(solution)/shard_map/ppermute | solution.py:173
  38.1 1.3 %collective-permute-start.27 = (bf16[8,4608]{1,0:T(8,128)(2,1)S(1)}, bf16[8,4608]{1,0:T(8,128)(2,1)S(1)}, u32[]{:S(2)}, u32[]{:S(2)}) collective-permute-start(bf16[8,4608]{1,0:T(8,128)(2,1)S(1)} %get-tuple-element.61), channel_id=1, source_target_pairs={{0,1},{1,0},{2,3},{3,2},{4,5},{5,4},{6,7},{7,6},{8,24},{9,25},{10,... | collective-permute-start | bytes 221192 | tf_op jit(solution)/shard_map/ppermute | solution.py:167
  42.6 1.8 %collective-permute-start.23 = (bf16[8,4608]{1,0:T(8,128)(2,1)S(1)}, bf16[8,4608]{1,0:T(8,128)(2,1)S(1)}, u32[]{:S(2)}, u32[]{:S(2)}) collective-permute-start(bf16[8,4608]{1,0:T(8,128)(2,1)S(1)} %add_convert_fusion.5), channel_id=1, source_target_pairs={{0,14},{1,15},{2,12},{3,13},{4,10},{5,11},{6,8},{7,9},{8,0},{9,1},... | collective-permute-start | bytes 221192 | tf_op jit(solution)/shard_map/ppermute | solution.py:179
  44.6 1.8 %collective-permute-done.23 = bf16[8,4608]{1,0:T(8,128)(2,1)S(1)} collective-permute-done((bf16[8,4608]{1,0:T(8,128)(2,1)S(1)}, bf16[8,4608]{1,0:T(8,128)(2,1)S(1)}, u32[]{:S(2)}, u32[]{:S(2)}) %collective-permute-start.23) | collective-permute-done | bytes 73760 | tf_op jit(solution)/shard_map/ppermute | solution.py:179
  47.2 4.4 %collective-permute-start.32 = (bf16[8,4608]{1,0:T(8,128)(2,1)S(1)}, bf16[8,4608]{1,0:T(8,128)(2,1)S(1)}, u32[]{:S(2)}, u32[]{:S(2)}) collective-permute-start(bf16[8,4608]{1,0:T(8,128)(2,1)S(1)} %get-tuple-element.84), channel_id=1, source_target_pairs={{24,10},{25,11},{26,8},{27,9},{28,14},{29,15},{30,12},{31,13},{8,0... | collective-permute-start | bytes 221192 | tf_op jit(solution)/shard_map/ppermute | solution.py:187
  51.6 1.9 %collective-permute-start.34 = (bf16[8,4608]{1,0:T(8,128)(2,1)S(1)}, bf16[8,4608]{1,0:T(8,128)(2,1)S(1)}, u32[]{:S(2)}, u32[]{:S(2)}) collective-permute-start(bf16[8,4608]{1,0:T(8,128)(2,1)S(1)} %get-tuple-element.84), channel_id=1, source_target_pairs={{24,12},{25,13},{26,14},{27,15},{28,8},{29,9},{30,10},{31,11},{8,0... | collective-permute-start | bytes 221192 | tf_op jit(solution)/shard_map/ppermute | solution.py:187
  53.6 1.9 %collective-permute-start.31 = (bf16[8,4608]{1,0:T(8,128)(2,1)S(1)}, bf16[8,4608]{1,0:T(8,128)(2,1)S(1)}, u32[]{:S(2)}, u32[]{:S(2)}) collective-permute-start(bf16[8,4608]{1,0:T(8,128)(2,1)S(1)} %get-tuple-element.84), channel_id=1, source_target_pairs={{24,9},{25,8},{26,11},{27,10},{28,13},{29,12},{30,15},{31,14},{8,0... | collective-permute-start | bytes 221192 | tf_op jit(solution)/shard_map/ppermute | solution.py:187
  55.9 1.9 %collective-permute-start.35 = (bf16[8,4608]{1,0:T(8,128)(2,1)S(1)}, bf16[8,4608]{1,0:T(8,128)(2,1)S(1)}, u32[]{:S(2)}, u32[]{:S(2)}) collective-permute-start(bf16[8,4608]{1,0:T(8,128)(2,1)S(1)} %collective-permute-done.34.refs_4_), channel_id=1, source_target_pairs={{0,16},{1,17},{2,18},{3,19},{4,20},{5,21},{6,22},{7,23},{8,9},{9,8... | collective-permute-start | bytes 221192 | tf_op jit(solution)/shard_map/ppermute | solution.py:167
  58.6 1.3 %collective-permute-done.33.refs_3_ = bf16[8,4608]{1,0:T(8,128)(2,1)S(1)} collective-permute-done((bf16[8,4608]{1,0:T(8,128)(2,1)S(1)}, bf16[8,4608]{1,0:T(8,128)(2,1)S(1)}, u32[]{:S(2)}, u32[]{:S(2)}) %collective-permute-start.33) | collective-permute-done | bytes 73760 | tf_op jit(solution)/shard_map/ppermute | solution.py:167
  60.6 1.5 %collective-permute-done.37.refs_7_ = bf16[8,4608]{1,0:T(8,128)(2,1)S(1)} collective-permute-done((bf16[8,4608]{1,0:T(8,128)(2,1)S(1)}, bf16[8,4608]{1,0:T(8,128)(2,1)S(1)}, u32[]{:S(2)}, u32[]{:S(2)}) %collective-permute-start.37) | collective-permute-done | bytes 73760 | tf_op jit(solution)/shard_map/ppermute | solution.py:167
  67.1 1.3 %collective-permute-start.40 = (bf16[8,4608]{1,0:T(8,128)(2,1)S(1)}, bf16[8,4608]{1,0:T(8,128)(2,1)S(1)}, u32[]{:S(2)}, u32[]{:S(2)}) collective-permute-start(bf16[8,4608]{1,0:T(8,128)(2,1)S(1)} %add_convert_fusion.3), channel_id=1, source_target_pairs={{0,16},{1,17},{2,18},{3,19},{4,20},{5,21},{6,22},{7,23},{8,10},{9,... | collective-permute-start | bytes 221192 | tf_op jit(solution)/shard_map/ppermute | solution.py:167
  71.5 1.3 %collective-permute-done.42 = bf16[8,4608]{1,0:T(8,128)(2,1)S(1)} collective-permute-done((bf16[8,4608]{1,0:T(8,128)(2,1)S(1)}, bf16[8,4608]{1,0:T(8,128)(2,1)S(1)}, u32[]{:S(2)}, u32[]{:S(2)}) %collective-permute-start.42) | collective-permute-done | bytes 73760 | tf_op jit(solution)/shard_map/ppermute | solution.py:167
  72.9 1.5 %collective-permute-start.47 = (bf16[8,4608]{1,0:T(8,128)(2,1)S(1)}, bf16[8,4608]{1,0:T(8,128)(2,1)S(1)}, u32[]{:S(2)}, u32[]{:S(2)}) collective-permute-start(bf16[8,4608]{1,0:T(8,128)(2,1)S(1)} %get-tuple-element.82), channel_id=1, source_target_pairs={{0,8},{1,9},{2,10},{3,11},{4,12},{5,13},{6,14},{7,15},{8,2},{9,3},... | collective-permute-start | bytes 221192 | tf_op jit(solution)/shard_map/ppermute | solution.py:173
  74.4 2.1 %collective-permute-start.45 = (bf16[8,4608]{1,0:T(8,128)(2,1)S(1)}, bf16[8,4608]{1,0:T(8,128)(2,1)S(1)}, u32[]{:S(2)}, u32[]{:S(2)}) collective-permute-start(bf16[8,4608]{1,0:T(8,128)(2,1)S(1)} %get-tuple-element.82), channel_id=1, source_target_pairs={{0,8},{1,9},{2,10},{3,11},{4,12},{5,13},{6,14},{7,15},{8,0},{9,1},... | collective-permute-start | bytes 221192 | tf_op jit(solution)/shard_map/ppermute | solution.py:173
  82.2 2.1 %collective-permute-done.52.refs_7_ = bf16[8,4608]{1,0:T(8,128)(2,1)S(1)} collective-permute-done((bf16[8,4608]{1,0:T(8,128)(2,1)S(1)}, bf16[8,4608]{1,0:T(8,128)(2,1)S(1)}, u32[]{:S(2)}, u32[]{:S(2)}) %collective-permute-start.52) | collective-permute-done | bytes 73760 | tf_op jit(solution)/shard_map/ppermute | solution.py:173
  85.0 1.8 %shard_map.81 = (bf16[8,8,512]{2,1,0:T(8,128)(2,1)}, bf16[8,4608]{1,0:T(8,128)(2,1)S(1)}, bf16[8,4608]{1,0:T(8,128)(2,1)S(1)}, bf16[8,4608]{1,0:T(8,128)(2,1)S(1...) custom-call(bf16[8,4608]{1,0:T(8,128)(2,1)S(1)} %collective-permute-, ...), custom_call_target="tpu_custom_call", output_to_operand_aliasing={{0}: (11, {})} | custom-call | flops 603979776 | bytes 9437184 | tf_op jit(solution)/shard_map/pallas_call | solution.py:191
  93.8 1.6 %collective-permute-done.56 = bf16[8,4608]{1,0:T(8,128)(2,1)S(1)} collective-permute-done((bf16[8,4608]{1,0:T(8,128)(2,1)S(1)}, bf16[8,4608]{1,0:T(8,128)(2,1)S(1)}, u32[]{:S(2)}, u32[]{:S(2)}) %collective-permute-start.56) | collective-permute-done | bytes 73760 | tf_op jit(solution)/shard_map/ppermute | solution.py:179
  96.1 2.1 %collective-permute-start.61 = (f32[8,4608]{1,0:T(8,128)S(1)}, f32[8,4608]{1,0:T(8,128)S(1)}, u32[]{:S(2)}, u32[]{:S(2)}) collective-permute-start(f32[8,4608]{1,0:T(8,128)S(1)} %broadcast_select_fusion), channel_id=1, source_target_pairs={{0,8},{1,9},{2,10},{3,11},{4,12},{5,13},{6,14},{7,15},{8,0},{9,1},... | collective-permute-start | bytes 442376 | tf_op jit(solution)/shard_map/ppermute | solution.py:173
  (112 shorter events, 38.9 us)
Async XLA Ops:
  0.6 7.1 %collective-permute-start.3 = (bf16[8,4608]{1,0:T(8,128)(2,1)}, bf16[8,4608]{1,0:T(8,128)(2,1)S(1)}, u32[]{:S(2)}, u32[]{:S(2)}) collective-permute-start(bf16[8,4608]{1,0:T(8,128)(2,1)} %refs_0_.1), channel_id=1, source_target_pairs={{0,16},{1,17},{2,18},{3,19},{4,20},{5,21},{6,22},{7,23},{8,12},{9,... | collective-permute-start | bytes 221192 | tf_op jit(solution)/shard_map/ppermute | solution.py:167
  3.7 10.0 %collective-permute-start = (bf16[8,4608]{1,0:T(8,128)(2,1)}, bf16[8,4608]{1,0:T(8,128)(2,1)S(1)}, u32[]{:S(2)}, u32[]{:S(2)}) collective-permute-start(bf16[8,4608]{1,0:T(8,128)(2,1)} %refs_0_.1), channel_id=1, source_target_pairs={{0,16},{1,17},{2,18},{3,19},{4,20},{5,21},{6,22},{7,23},{8,9},{9,8... | collective-permute-start | bytes 221192 | tf_op jit(solution)/shard_map/ppermute | solution.py:167
  5.7 8.1 %collective-permute-start.1 = (bf16[8,4608]{1,0:T(8,128)(2,1)}, bf16[8,4608]{1,0:T(8,128)(2,1)S(1)}, u32[]{:S(2)}, u32[]{:S(2)}) collective-permute-start(bf16[8,4608]{1,0:T(8,128)(2,1)} %refs_0_.1), channel_id=1, source_target_pairs={{0,16},{1,17},{2,18},{3,19},{4,20},{5,21},{6,22},{7,23},{8,10},{9,... | collective-permute-start | bytes 221192 | tf_op jit(solution)/shard_map/ppermute | solution.py:167
  5.8 8.0 %collective-permute-start.2 = (bf16[8,4608]{1,0:T(8,128)(2,1)}, bf16[8,4608]{1,0:T(8,128)(2,1)S(1)}, u32[]{:S(2)}, u32[]{:S(2)}) collective-permute-start(bf16[8,4608]{1,0:T(8,128)(2,1)} %refs_0_.1), channel_id=1, source_target_pairs={{0,16},{1,17},{2,18},{3,19},{4,20},{5,21},{6,22},{7,23},{8,11},{9,... | collective-permute-start | bytes 221192 | tf_op jit(solution)/shard_map/ppermute | solution.py:167
  7.7 6.1 %collective-permute-start.4 = (bf16[8,4608]{1,0:T(8,128)(2,1)S(1)}, bf16[8,4608]{1,0:T(8,128)(2,1)S(1)}, u32[]{:S(2)}, u32[]{:S(2)}) collective-permute-start(bf16[8,4608]{1,0:T(8,128)(2,1)S(1)} %collective-permute-done.3.refs_4_), channel_id=1, source_target_pairs={{0,16},{1,17},{2,18},{3,19},{4,20},{5,21},{6,22},{7,23},{8,9},{9,8... | collective-permute-start | bytes 221192 | tf_op jit(solution)/shard_map/ppermute | solution.py:167
  8.2 5.6 %collective-permute-start.6 = (bf16[8,4608]{1,0:T(8,128)(2,1)S(1)}, bf16[8,4608]{1,0:T(8,128)(2,1)S(1)}, u32[]{:S(2)}, u32[]{:S(2)}) collective-permute-start(bf16[8,4608]{1,0:T(8,128)(2,1)S(1)} %collective-permute-done.5.refs_6_), channel_id=1, source_target_pairs={{0,16},{1,17},{2,18},{3,19},{4,20},{5,21},{6,22},{7,23},{8,9},{9,8... | collective-permute-start | bytes 221192 | tf_op jit(solution)/shard_map/ppermute | solution.py:167
  14.5 5.7 %collective-permute-start.10 = (bf16[8,4608]{1,0:T(8,128)(2,1)S(1)}, bf16[8,4608]{1,0:T(8,128)(2,1)S(1)}, u32[]{:S(2)}, u32[]{:S(2)}) collective-permute-start(bf16[8,4608]{1,0:T(8,128)(2,1)S(1)} %get-tuple-element.51), channel_id=1, source_target_pairs={{0,16},{1,17},{2,18},{3,19},{4,20},{5,21},{6,22},{7,23},{8,9},{9,8... | collective-permute-start | bytes 221192 | tf_op jit(solution)/shard_map/ppermute | solution.py:167
  16.0 4.7 %collective-permute-start.12 = (bf16[8,4608]{1,0:T(8,128)(2,1)S(1)}, bf16[8,4608]{1,0:T(8,128)(2,1)S(1)}, u32[]{:S(2)}, u32[]{:S(2)}) collective-permute-start(bf16[8,4608]{1,0:T(8,128)(2,1)S(1)} %get-tuple-element.52), channel_id=1, source_target_pairs={{0,16},{1,17},{2,18},{3,19},{4,20},{5,21},{6,22},{7,23},{8,14},{9,... | collective-permute-start | bytes 221192 | tf_op jit(solution)/shard_map/ppermute | solution.py:167
  24.7 4.8 %collective-permute-start.16 = (bf16[8,4608]{1,0:T(8,128)(2,1)S(1)}, bf16[8,4608]{1,0:T(8,128)(2,1)S(1)}, u32[]{:S(2)}, u32[]{:S(2)}) collective-permute-start(bf16[8,4608]{1,0:T(8,128)(2,1)S(1)} %get-tuple-element.86), channel_id=1, source_target_pairs={{0,8},{1,9},{2,10},{3,11},{4,12},{5,13},{6,14},{7,15},{8,2},{9,3},... | collective-permute-start | bytes 221192 | tf_op jit(solution)/shard_map/ppermute | solution.py:173
  26.0 5.5 %collective-permute-start.18 = (bf16[8,4608]{1,0:T(8,128)(2,1)S(1)}, bf16[8,4608]{1,0:T(8,128)(2,1)S(1)}, u32[]{:S(2)}, u32[]{:S(2)}) collective-permute-start(bf16[8,4608]{1,0:T(8,128)(2,1)S(1)} %get-tuple-element.86), channel_id=1, source_target_pairs={{0,8},{1,9},{2,10},{3,11},{4,12},{5,13},{6,14},{7,15},{8,4},{9,5},... | collective-permute-start | bytes 221192 | tf_op jit(solution)/shard_map/ppermute | solution.py:173
  26.4 6.5 %collective-permute-start.14 = (bf16[8,4608]{1,0:T(8,128)(2,1)S(1)}, bf16[8,4608]{1,0:T(8,128)(2,1)S(1)}, u32[]{:S(2)}, u32[]{:S(2)}) collective-permute-start(bf16[8,4608]{1,0:T(8,128)(2,1)S(1)} %get-tuple-element.86), channel_id=1, source_target_pairs={{0,8},{1,9},{2,10},{3,11},{4,12},{5,13},{6,14},{7,15},{8,0},{9,1},... | collective-permute-start | bytes 221192 | tf_op jit(solution)/shard_map/ppermute | solution.py:173
  27.8 5.7 %collective-permute-start.15 = (bf16[8,4608]{1,0:T(8,128)(2,1)S(1)}, bf16[8,4608]{1,0:T(8,128)(2,1)S(1)}, u32[]{:S(2)}, u32[]{:S(2)}) collective-permute-start(bf16[8,4608]{1,0:T(8,128)(2,1)S(1)} %get-tuple-element.86), channel_id=1, source_target_pairs={{0,8},{1,9},{2,10},{3,11},{4,12},{5,13},{6,14},{7,15},{8,1},{9,0},... | collective-permute-start | bytes 221192 | tf_op jit(solution)/shard_map/ppermute | solution.py:173
  27.8 5.7 %collective-permute-start.20 = (bf16[8,4608]{1,0:T(8,128)(2,1)S(1)}, bf16[8,4608]{1,0:T(8,128)(2,1)S(1)}, u32[]{:S(2)}, u32[]{:S(2)}) collective-permute-start(bf16[8,4608]{1,0:T(8,128)(2,1)S(1)} %get-tuple-element.86), channel_id=1, source_target_pairs={{0,8},{1,9},{2,10},{3,11},{4,12},{5,13},{6,14},{7,15},{8,6},{9,7},... | collective-permute-start | bytes 221192 | tf_op jit(solution)/shard_map/ppermute | solution.py:173
  29.4 6.6 %collective-permute-start.21 = (bf16[8,4608]{1,0:T(8,128)(2,1)S(1)}, bf16[8,4608]{1,0:T(8,128)(2,1)S(1)}, u32[]{:S(2)}, u32[]{:S(2)}) collective-permute-start(bf16[8,4608]{1,0:T(8,128)(2,1)S(1)} %get-tuple-element.86), channel_id=1, source_target_pairs={{0,8},{1,9},{2,10},{3,11},{4,12},{5,13},{6,14},{7,15},{8,7},{9,6},... | collective-permute-start | bytes 221192 | tf_op jit(solution)/shard_map/ppermute | solution.py:173
  31.4 5.1 %collective-permute-start.17 = (bf16[8,4608]{1,0:T(8,128)(2,1)S(1)}, bf16[8,4608]{1,0:T(8,128)(2,1)S(1)}, u32[]{:S(2)}, u32[]{:S(2)}) collective-permute-start(bf16[8,4608]{1,0:T(8,128)(2,1)S(1)} %collective-permute-done.16.refs_2_), channel_id=1, source_target_pairs={{0,1},{1,0},{2,3},{3,2},{4,5},{5,4},{6,7},{7,6},{8,24},{9,25},{10,... | collective-permute-start | bytes 221192 | tf_op jit(solution)/shard_map/ppermute | solution.py:167
  39.5 5.0 %collective-permute-start.24 = (bf16[8,4608]{1,0:T(8,128)(2,1)S(1)}, bf16[8,4608]{1,0:T(8,128)(2,1)S(1)}, u32[]{:S(2)}, u32[]{:S(2)}) collective-permute-start(bf16[8,4608]{1,0:T(8,128)(2,1)S(1)} %get-tuple-element.57), channel_id=1, source_target_pairs={{0,8},{1,9},{2,10},{3,11},{4,12},{5,13},{6,14},{7,15},{8,0},{9,1},... | collective-permute-start | bytes 221192 | tf_op jit(solution)/shard_map/ppermute | solution.py:179
  39.7 4.9 %collective-permute-start.25 = (bf16[8,4608]{1,0:T(8,128)(2,1)S(1)}, bf16[8,4608]{1,0:T(8,128)(2,1)S(1)}, u32[]{:S(2)}, u32[]{:S(2)}) collective-permute-start(bf16[8,4608]{1,0:T(8,128)(2,1)S(1)} %get-tuple-element.58), channel_id=1, source_target_pairs={{0,9},{1,8},{2,11},{3,10},{4,13},{5,12},{6,15},{7,14},{8,0},{9,1},... | collective-permute-start | bytes 221192 | tf_op jit(solution)/shard_map/ppermute | solution.py:179
  47.2 8.3 %collective-permute-start.32 = (bf16[8,4608]{1,0:T(8,128)(2,1)S(1)}, bf16[8,4608]{1,0:T(8,128)(2,1)S(1)}, u32[]{:S(2)}, u32[]{:S(2)}) collective-permute-start(bf16[8,4608]{1,0:T(8,128)(2,1)S(1)} %get-tuple-element.84), channel_id=1, source_target_pairs={{24,10},{25,11},{26,8},{27,9},{28,14},{29,15},{30,12},{31,13},{8,0... | collective-permute-start | bytes 221192 | tf_op jit(solution)/shard_map/ppermute | solution.py:187
  53.5 5.1 %collective-permute-start.30 = (bf16[8,4608]{1,0:T(8,128)(2,1)S(1)}, bf16[8,4608]{1,0:T(8,128)(2,1)S(1)}, u32[]{:S(2)}, u32[]{:S(2)}) collective-permute-start(bf16[8,4608]{1,0:T(8,128)(2,1)S(1)} %get-tuple-element.84), channel_id=1, source_target_pairs={{24,8},{25,9},{26,10},{27,11},{28,12},{29,13},{30,14},{31,15},{8,0... | collective-permute-start | bytes 221192 | tf_op jit(solution)/shard_map/ppermute | solution.py:187
  53.6 5.0 %collective-permute-start.31 = (bf16[8,4608]{1,0:T(8,128)(2,1)S(1)}, bf16[8,4608]{1,0:T(8,128)(2,1)S(1)}, u32[]{:S(2)}, u32[]{:S(2)}) collective-permute-start(bf16[8,4608]{1,0:T(8,128)(2,1)S(1)} %get-tuple-element.84), channel_id=1, source_target_pairs={{24,9},{25,8},{26,11},{27,10},{28,13},{29,12},{30,15},{31,14},{8,0... | collective-permute-start | bytes 221192 | tf_op jit(solution)/shard_map/ppermute | solution.py:187
  55.9 4.7 %collective-permute-start.35 = (bf16[8,4608]{1,0:T(8,128)(2,1)S(1)}, bf16[8,4608]{1,0:T(8,128)(2,1)S(1)}, u32[]{:S(2)}, u32[]{:S(2)}) collective-permute-start(bf16[8,4608]{1,0:T(8,128)(2,1)S(1)} %collective-permute-done.34.refs_4_), channel_id=1, source_target_pairs={{0,16},{1,17},{2,18},{3,19},{4,20},{5,21},{6,22},{7,23},{8,9},{9,8... | collective-permute-start | bytes 221192 | tf_op jit(solution)/shard_map/ppermute | solution.py:167
  62.2 4.9 %collective-permute-start.39 = (bf16[8,4608]{1,0:T(8,128)(2,1)S(1)}, bf16[8,4608]{1,0:T(8,128)(2,1)S(1)}, u32[]{:S(2)}, u32[]{:S(2)}) collective-permute-start(bf16[8,4608]{1,0:T(8,128)(2,1)S(1)} %get-tuple-element.67), channel_id=1, source_target_pairs={{0,16},{1,17},{2,18},{3,19},{4,20},{5,21},{6,22},{7,23},{8,9},{9,8... | collective-permute-start | bytes 221192 | tf_op jit(solution)/shard_map/ppermute | solution.py:167
  63.0 5.4 %collective-permute-start.41 = (bf16[8,4608]{1,0:T(8,128)(2,1)S(1)}, bf16[8,4608]{1,0:T(8,128)(2,1)S(1)}, u32[]{:S(2)}, u32[]{:S(2)}) collective-permute-start(bf16[8,4608]{1,0:T(8,128)(2,1)S(1)} %get-tuple-element.69), channel_id=1, source_target_pairs={{0,16},{1,17},{2,18},{3,19},{4,20},{5,21},{6,22},{7,23},{8,9},{9,8... | collective-permute-start | bytes 221192 | tf_op jit(solution)/shard_map/ppermute | solution.py:167
  64.2 5.0 %collective-permute-start.38 = (bf16[8,4608]{1,0:T(8,128)(2,1)S(1)}, bf16[8,4608]{1,0:T(8,128)(2,1)S(1)}, u32[]{:S(2)}, u32[]{:S(2)}) collective-permute-start(bf16[8,4608]{1,0:T(8,128)(2,1)S(1)} %get-tuple-element.65), channel_id=1, source_target_pairs={{0,16},{1,17},{2,18},{3,19},{4,20},{5,21},{6,22},{7,23},{8,15},{9,... | collective-permute-start | bytes 221192 | tf_op jit(solution)/shard_map/ppermute | solution.py:167
  72.9 4.8 %collective-permute-start.47 = (bf16[8,4608]{1,0:T(8,128)(2,1)S(1)}, bf16[8,4608]{1,0:T(8,128)(2,1)S(1)}, u32[]{:S(2)}, u32[]{:S(2)}) collective-permute-start(bf16[8,4608]{1,0:T(8,128)(2,1)S(1)} %get-tuple-element.82), channel_id=1, source_target_pairs={{0,8},{1,9},{2,10},{3,11},{4,12},{5,13},{6,14},{7,15},{8,2},{9,3},... | collective-permute-start | bytes 221192 | tf_op jit(solution)/shard_map/ppermute | solution.py:173
  74.4 4.7 %collective-permute-start.49 = (bf16[8,4608]{1,0:T(8,128)(2,1)S(1)}, bf16[8,4608]{1,0:T(8,128)(2,1)S(1)}, u32[]{:S(2)}, u32[]{:S(2)}) collective-permute-start(bf16[8,4608]{1,0:T(8,128)(2,1)S(1)} %get-tuple-element.82), channel_id=1, source_target_pairs={{0,8},{1,9},{2,10},{3,11},{4,12},{5,13},{6,14},{7,15},{8,4},{9,5},... | collective-permute-start | bytes 221192 | tf_op jit(solution)/shard_map/ppermute | solution.py:173
  74.4 5.5 %collective-permute-start.45 = (bf16[8,4608]{1,0:T(8,128)(2,1)S(1)}, bf16[8,4608]{1,0:T(8,128)(2,1)S(1)}, u32[]{:S(2)}, u32[]{:S(2)}) collective-permute-start(bf16[8,4608]{1,0:T(8,128)(2,1)S(1)} %get-tuple-element.82), channel_id=1, source_target_pairs={{0,8},{1,9},{2,10},{3,11},{4,12},{5,13},{6,14},{7,15},{8,0},{9,1},... | collective-permute-start | bytes 221192 | tf_op jit(solution)/shard_map/ppermute | solution.py:173
  76.5 5.7 %collective-permute-start.51 = (bf16[8,4608]{1,0:T(8,128)(2,1)S(1)}, bf16[8,4608]{1,0:T(8,128)(2,1)S(1)}, u32[]{:S(2)}, u32[]{:S(2)}) collective-permute-start(bf16[8,4608]{1,0:T(8,128)(2,1)S(1)} %get-tuple-element.82), channel_id=1, source_target_pairs={{0,8},{1,9},{2,10},{3,11},{4,12},{5,13},{6,14},{7,15},{8,6},{9,7},... | collective-permute-start | bytes 221192 | tf_op jit(solution)/shard_map/ppermute | solution.py:173
  77.7 6.5 %collective-permute-start.52 = (bf16[8,4608]{1,0:T(8,128)(2,1)S(1)}, bf16[8,4608]{1,0:T(8,128)(2,1)S(1)}, u32[]{:S(2)}, u32[]{:S(2)}) collective-permute-start(bf16[8,4608]{1,0:T(8,128)(2,1)S(1)} %get-tuple-element.82), channel_id=1, source_target_pairs={{0,8},{1,9},{2,10},{3,11},{4,12},{5,13},{6,14},{7,15},{8,7},{9,6},... | collective-permute-start | bytes 221192 | tf_op jit(solution)/shard_map/ppermute | solution.py:173
  79.1 5.2 %collective-permute-start.48 = (bf16[8,4608]{1,0:T(8,128)(2,1)S(1)}, bf16[8,4608]{1,0:T(8,128)(2,1)S(1)}, u32[]{:S(2)}, u32[]{:S(2)}) collective-permute-start(bf16[8,4608]{1,0:T(8,128)(2,1)S(1)} %collective-permute-done.47.refs_2_), channel_id=1, source_target_pairs={{0,1},{1,0},{2,3},{3,2},{4,5},{5,4},{6,7},{7,6},{8,24},{9,25},{10,... | collective-permute-start | bytes 221192 | tf_op jit(solution)/shard_map/ppermute | solution.py:167
  80.0 5.0 %collective-permute-start.50 = (bf16[8,4608]{1,0:T(8,128)(2,1)S(1)}, bf16[8,4608]{1,0:T(8,128)(2,1)S(1)}, u32[]{:S(2)}, u32[]{:S(2)}) collective-permute-start(bf16[8,4608]{1,0:T(8,128)(2,1)S(1)} %collective-permute-done.49.refs_4_), channel_id=1, source_target_pairs={{0,1},{1,0},{2,3},{3,2},{4,5},{5,4},{6,7},{7,6},{8,24},{9,25},{10,... | collective-permute-start | bytes 221192 | tf_op jit(solution)/shard_map/ppermute | solution.py:167
  88.9 4.8 %collective-permute-start.54 = (bf16[8,4608]{1,0:T(8,128)(2,1)S(1)}, bf16[8,4608]{1,0:T(8,128)(2,1)S(1)}, u32[]{:S(2)}, u32[]{:S(2)}) collective-permute-start(bf16[8,4608]{1,0:T(8,128)(2,1)S(1)} %get-tuple-element.75), channel_id=1, source_target_pairs={{0,8},{1,9},{2,10},{3,11},{4,12},{5,13},{6,14},{7,15},{8,0},{9,1},... | collective-permute-start | bytes 221192 | tf_op jit(solution)/shard_map/ppermute | solution.py:179
  (31 other events, 126.5 us)

commit v5 on v4

--- a/solution.py
+++ b/solution.py
@@ -280,7 +280,7 @@
         lower = grads[0]
         for high in range(3, layers, 2):
             lower = jnp.where(layer_index == high, grads[high - 1], lower)
-        lower = down(lower, 0)
+        lower = down(lower.astype(jnp.bfloat16), 0).astype(jnp.float32)
         grad = jnp.where(layer_index % 2 == 1, grad, lower)
         for high in range(1, layers, 2):
             grad = jnp.where(layer_index == high, grads[high], grad)

time: 100 us -> 100 us (level)
  no operation moved by 1% of the time
where the time goes in v5:
time: 100 us; the launch traced here: 99.9 us
  starting transfers between devices  62 us (62%)
  waiting for transfers between devices  29.9 us (30%)
  Pallas kernels  5.92 us (6%)
  other arithmetic  1.2 us (1%)
    ppermute x32, starting transfers between devices, within(): return lax.ppermute(value, AXES, pairs)  34.2 us
    ppermute x32, waiting for transfers between devices, within(): return lax.ppermute(value, AXES, pairs)  16.1 us
    ppermute x13, starting transfers between devices, down(): return lax.ppermute(value, AXES, pairs)  12.7 us
    ppermute x13, waiting for transfers between devices, down(): return lax.ppermute(value, AXES, pairs)  8.97 us
    ppermute x5, starting transfers between devices, skip(): return lax.ppermute(value, AXES, pairs)  8.33 us
    ppermute x12, starting transfers between devices, up(): return lax.ppermute(value, AXES, pairs)  6.71 us
    ppermute x12, waiting for transfers between devices, up(): return lax.ppermute(value, AXES, pairs)  4.82 us
    pallas_call x1, Pallas kernels, body(): pl.pallas_call(functools.partial(gate_kernel, direct), out_shape=(jax.Sha...  4.03 us
  transfers between devices with their start and end apart: 62, of which 29 were waited for; matrix products, arithmetic and copies ran while one was open for 0% of the time, Pallas kernels for 4%

profile of v5, /device:TPU:0, one launch (start us, length us, event | category | flops | bytes accessed | tf_op | source)
XLA Modules:
  0.0 99.9 jit_solution(11941704049565930989)
XLA Ops:
  0.6 3.0 %collective-permute-start.3 = (bf16[8,4608]{1,0:T(8,128)(2,1)}, bf16[8,4608]{1,0:T(8,128)(2,1)S(1)}, u32[]{:S(2)}, u32[]{:S(2)}) collective-permute-start(bf16[8,4608]{1,0:T(8,128)(2,1)} %refs_0_.1), channel_id=1, source_target_pairs={{0,16},{1,17},{2,18},{3,19},{4,20},{5,21},{6,22},{7,23},{8,12},{9,... | collective-permute-start | bytes 221192 | tf_op jit(solution)/shard_map/ppermute | solution.py:167
  3.7 1.9 %collective-permute-start = (bf16[8,4608]{1,0:T(8,128)(2,1)}, bf16[8,4608]{1,0:T(8,128)(2,1)S(1)}, u32[]{:S(2)}, u32[]{:S(2)}) collective-permute-start(bf16[8,4608]{1,0:T(8,128)(2,1)} %refs_0_.1), channel_id=1, source_target_pairs={{0,16},{1,17},{2,18},{3,19},{4,20},{5,21},{6,22},{7,23},{8,9},{9,8... | collective-permute-start | bytes 221192 | tf_op jit(solution)/shard_map/ppermute | solution.py:167
  5.8 1.9 %collective-permute-start.2 = (bf16[8,4608]{1,0:T(8,128)(2,1)}, bf16[8,4608]{1,0:T(8,128)(2,1)S(1)}, u32[]{:S(2)}, u32[]{:S(2)}) collective-permute-start(bf16[8,4608]{1,0:T(8,128)(2,1)} %refs_0_.1), channel_id=1, source_target_pairs={{0,16},{1,17},{2,18},{3,19},{4,20},{5,21},{6,22},{7,23},{8,11},{9,... | collective-permute-start | bytes 221192 | tf_op jit(solution)/shard_map/ppermute | solution.py:167
  8.2 1.5 %collective-permute-start.6 = (bf16[8,4608]{1,0:T(8,128)(2,1)S(1)}, bf16[8,4608]{1,0:T(8,128)(2,1)S(1)}, u32[]{:S(2)}, u32[]{:S(2)}) collective-permute-start(bf16[8,4608]{1,0:T(8,128)(2,1)S(1)} %collective-permute-done.5.refs_6_), channel_id=1, source_target_pairs={{0,16},{1,17},{2,18},{3,19},{4,20},{5,21},{6,22},{7,23},{8,9},{9,8... | collective-permute-start | bytes 221192 | tf_op jit(solution)/shard_map/ppermute | solution.py:167
  9.8 4.0 %shard_map.77 = (f32[64,512]{1,0:T(8,128)S(1)}, bf16[8,8,512]{2,1,0:T(8,128)(2,1)}, bf16[4608,512]{1,0:T(8,128)(2,1)S(1)}, bf16[512,4608]{1,0:T(8,128)(2,1)S(1)}) custom-call(bf16[8,8,512]{2,1,0:T(8,128)(2,1)} %bitcast.5, s32[1,8,16]{2,1,0:T(8,128)} %ids_ref.1, s32[1,8]{1,0:T(1,128)} %counts_ref.1, bf16[1,512,4608]{2,1,0:T(8,128)(2,1)} %dec_ref.1, ...), custom_call_target="tpu_custom_call" | custom-call | bytes 9437184 | tf_op jit(solution)/shard_map/pallas_call | solution.py:131
  14.5 1.5 %collective-permute-start.10 = (bf16[8,4608]{1,0:T(8,128)(2,1)S(1)}, bf16[8,4608]{1,0:T(8,128)(2,1)S(1)}, u32[]{:S(2)}, u32[]{:S(2)}) collective-permute-start(bf16[8,4608]{1,0:T(8,128)(2,1)S(1)} %get-tuple-element.51), channel_id=1, source_target_pairs={{0,16},{1,17},{2,18},{3,19},{4,20},{5,21},{6,22},{7,23},{8,9},{9,8... | collective-permute-start | bytes 221192 | tf_op jit(solution)/shard_map/ppermute | solution.py:167
  16.5 1.5 %collective-permute-start.13 = (bf16[8,4608]{1,0:T(8,128)(2,1)S(1)}, bf16[8,4608]{1,0:T(8,128)(2,1)S(1)}, u32[]{:S(2)}, u32[]{:S(2)}) collective-permute-start(bf16[8,4608]{1,0:T(8,128)(2,1)S(1)} %get-tuple-element.53), channel_id=1, source_target_pairs={{0,16},{1,17},{2,18},{3,19},{4,20},{5,21},{6,22},{7,23},{8,9},{9,8... | collective-permute-start | bytes 221192 | tf_op jit(solution)/shard_map/ppermute | solution.py:167
  18.5 1.6 %collective-permute-start.9 = (bf16[8,4608]{1,0:T(8,128)(2,1)S(1)}, bf16[8,4608]{1,0:T(8,128)(2,1)S(1)}, u32[]{:S(2)}, u32[]{:S(2)}) collective-permute-start(bf16[8,4608]{1,0:T(8,128)(2,1)S(1)} %add_convert_fusion.7), channel_id=1, source_target_pairs={{0,16},{1,17},{2,18},{3,19},{4,20},{5,21},{6,22},{7,23},{8,10},{9,... | collective-permute-start | bytes 221192 | tf_op jit(solution)/shard_map/ppermute | solution.py:167
  23.2 1.4 %collective-permute-done.11 = bf16[8,4608]{1,0:T(8,128)(2,1)S(1)} collective-permute-done((bf16[8,4608]{1,0:T(8,128)(2,1)S(1)}, bf16[8,4608]{1,0:T(8,128)(2,1)S(1)}, u32[]{:S(2)}, u32[]{:S(2)}) %collective-permute-start.11) | collective-permute-done | bytes 73760 | tf_op jit(solution)/shard_map/ppermute | solution.py:167
  24.7 1.3 %collective-permute-start.16 = (bf16[8,4608]{1,0:T(8,128)(2,1)S(1)}, bf16[8,4608]{1,0:T(8,128)(2,1)S(1)}, u32[]{:S(2)}, u32[]{:S(2)}) collective-permute-start(bf16[8,4608]{1,0:T(8,128)(2,1)S(1)} %get-tuple-element.84), channel_id=1, source_target_pairs={{0,8},{1,9},{2,10},{3,11},{4,12},{5,13},{6,14},{7,15},{8,2},{9,3},... | collective-permute-start | bytes 221192 | tf_op jit(solution)/shard_map/ppermute | solution.py:173
  26.4 1.4 %collective-permute-start.14 = (bf16[8,4608]{1,0:T(8,128)(2,1)S(1)}, bf16[8,4608]{1,0:T(8,128)(2,1)S(1)}, u32[]{:S(2)}, u32[]{:S(2)}) collective-permute-start(bf16[8,4608]{1,0:T(8,128)(2,1)S(1)} %get-tuple-element.84), channel_id=1, source_target_pairs={{0,8},{1,9},{2,10},{3,11},{4,12},{5,13},{6,14},{7,15},{8,0},{9,1},... | collective-permute-start | bytes 221192 | tf_op jit(solution)/shard_map/ppermute | solution.py:173
  27.8 1.7 %collective-permute-start.20 = (bf16[8,4608]{1,0:T(8,128)(2,1)S(1)}, bf16[8,4608]{1,0:T(8,128)(2,1)S(1)}, u32[]{:S(2)}, u32[]{:S(2)}) collective-permute-start(bf16[8,4608]{1,0:T(8,128)(2,1)S(1)} %get-tuple-element.84), channel_id=1, source_target_pairs={{0,8},{1,9},{2,10},{3,11},{4,12},{5,13},{6,14},{7,15},{8,6},{9,7},... | collective-permute-start | bytes 221192 | tf_op jit(solution)/shard_map/ppermute | solution.py:173
  29.7 1.7 %collective-permute-done.18.refs_4_ = bf16[8,4608]{1,0:T(8,128)(2,1)S(1)} collective-permute-done((bf16[8,4608]{1,0:T(8,128)(2,1)S(1)}, bf16[8,4608]{1,0:T(8,128)(2,1)S(1)}, u32[]{:S(2)}, u32[]{:S(2)}) %collective-permute-start.18) | collective-permute-done | bytes 73760 | tf_op jit(solution)/shard_map/ppermute | solution.py:173
  31.4 1.5 %collective-permute-start.17 = (bf16[8,4608]{1,0:T(8,128)(2,1)S(1)}, bf16[8,4608]{1,0:T(8,128)(2,1)S(1)}, u32[]{:S(2)}, u32[]{:S(2)}) collective-permute-start(bf16[8,4608]{1,0:T(8,128)(2,1)S(1)} %collective-permute-done.16.refs_2_), channel_id=1, source_target_pairs={{0,1},{1,0},{2,3},{3,2},{4,5},{5,4},{6,7},{7,6},{8,24},{9,25},{10,... | collective-permute-start | bytes 221192 | tf_op jit(solution)/shard_map/ppermute | solution.py:167
  33.5 2.6 %collective-permute-done.21.refs_7_ = bf16[8,4608]{1,0:T(8,128)(2,1)S(1)} collective-permute-done((bf16[8,4608]{1,0:T(8,128)(2,1)S(1)}, bf16[8,4608]{1,0:T(8,128)(2,1)S(1)}, u32[]{:S(2)}, u32[]{:S(2)}) %collective-permute-start.21) | collective-permute-done | bytes 73760 | tf_op jit(solution)/shard_map/ppermute | solution.py:173
  38.1 1.3 %collective-permute-start.27 = (bf16[8,4608]{1,0:T(8,128)(2,1)S(1)}, bf16[8,4608]{1,0:T(8,128)(2,1)S(1)}, u32[]{:S(2)}, u32[]{:S(2)}) collective-permute-start(bf16[8,4608]{1,0:T(8,128)(2,1)S(1)} %get-tuple-element.61), channel_id=1, source_target_pairs={{0,1},{1,0},{2,3},{3,2},{4,5},{5,4},{6,7},{7,6},{8,24},{9,25},{10,... | collective-permute-start | bytes 221192 | tf_op jit(solution)/shard_map/ppermute | solution.py:167
  42.6 1.8 %collective-permute-start.23 = (bf16[8,4608]{1,0:T(8,128)(2,1)S(1)}, bf16[8,4608]{1,0:T(8,128)(2,1)S(1)}, u32[]{:S(2)}, u32[]{:S(2)}) collective-permute-start(bf16[8,4608]{1,0:T(8,128)(2,1)S(1)} %add_convert_fusion.5), channel_id=1, source_target_pairs={{0,14},{1,15},{2,12},{3,13},{4,10},{5,11},{6,8},{7,9},{8,0},{9,1},... | collective-permute-start | bytes 221192 | tf_op jit(solution)/shard_map/ppermute | solution.py:179
  44.6 1.8 %collective-permute-done.23 = bf16[8,4608]{1,0:T(8,128)(2,1)S(1)} collective-permute-done((bf16[8,4608]{1,0:T(8,128)(2,1)S(1)}, bf16[8,4608]{1,0:T(8,128)(2,1)S(1)}, u32[]{:S(2)}, u32[]{:S(2)}) %collective-permute-start.23) | collective-permute-done | bytes 73760 | tf_op jit(solution)/shard_map/ppermute | solution.py:179
  47.2 4.4 %collective-permute-start.32 = (bf16[8,4608]{1,0:T(8,128)(2,1)S(1)}, bf16[8,4608]{1,0:T(8,128)(2,1)S(1)}, u32[]{:S(2)}, u32[]{:S(2)}) collective-permute-start(bf16[8,4608]{1,0:T(8,128)(2,1)S(1)} %convert_add_fusion.2), channel_id=1, source_target_pairs={{24,10},{25,11},{26,8},{27,9},{28,14},{29,15},{30,12},{31,13},{8,0... | collective-permute-start | bytes 221192 | tf_op jit(solution)/shard_map/ppermute | solution.py:187
  51.6 1.9 %collective-permute-start.34 = (bf16[8,4608]{1,0:T(8,128)(2,1)S(1)}, bf16[8,4608]{1,0:T(8,128)(2,1)S(1)}, u32[]{:S(2)}, u32[]{:S(2)}) collective-permute-start(bf16[8,4608]{1,0:T(8,128)(2,1)S(1)} %convert_add_fusion.2), channel_id=1, source_target_pairs={{24,12},{25,13},{26,14},{27,15},{28,8},{29,9},{30,10},{31,11},{8,0... | collective-permute-start | bytes 221192 | tf_op jit(solution)/shard_map/ppermute | solution.py:187
  53.6 1.9 %collective-permute-start.31 = (bf16[8,4608]{1,0:T(8,128)(2,1)S(1)}, bf16[8,4608]{1,0:T(8,128)(2,1)S(1)}, u32[]{:S(2)}, u32[]{:S(2)}) collective-permute-start(bf16[8,4608]{1,0:T(8,128)(2,1)S(1)} %convert_add_fusion.2), channel_id=1, source_target_pairs={{24,9},{25,8},{26,11},{27,10},{28,13},{29,12},{30,15},{31,14},{8,0... | collective-permute-start | bytes 221192 | tf_op jit(solution)/shard_map/ppermute | solution.py:187
  55.9 1.9 %collective-permute-start.35 = (bf16[8,4608]{1,0:T(8,128)(2,1)S(1)}, bf16[8,4608]{1,0:T(8,128)(2,1)S(1)}, u32[]{:S(2)}, u32[]{:S(2)}) collective-permute-start(bf16[8,4608]{1,0:T(8,128)(2,1)S(1)} %collective-permute-done.34.refs_4_), channel_id=1, source_target_pairs={{0,16},{1,17},{2,18},{3,19},{4,20},{5,21},{6,22},{7,23},{8,9},{9,8... | collective-permute-start | bytes 221192 | tf_op jit(solution)/shard_map/ppermute | solution.py:167
  58.6 1.3 %collective-permute-done.33.refs_3_ = bf16[8,4608]{1,0:T(8,128)(2,1)S(1)} collective-permute-done((bf16[8,4608]{1,0:T(8,128)(2,1)S(1)}, bf16[8,4608]{1,0:T(8,128)(2,1)S(1)}, u32[]{:S(2)}, u32[]{:S(2)}) %collective-permute-start.33) | collective-permute-done | bytes 73760 | tf_op jit(solution)/shard_map/ppermute | solution.py:167
  60.6 1.5 %collective-permute-done.37.refs_7_ = bf16[8,4608]{1,0:T(8,128)(2,1)S(1)} collective-permute-done((bf16[8,4608]{1,0:T(8,128)(2,1)S(1)}, bf16[8,4608]{1,0:T(8,128)(2,1)S(1)}, u32[]{:S(2)}, u32[]{:S(2)}) %collective-permute-start.37) | collective-permute-done | bytes 73760 | tf_op jit(solution)/shard_map/ppermute | solution.py:167
  67.1 1.3 %collective-permute-start.40 = (bf16[8,4608]{1,0:T(8,128)(2,1)S(1)}, bf16[8,4608]{1,0:T(8,128)(2,1)S(1)}, u32[]{:S(2)}, u32[]{:S(2)}) collective-permute-start(bf16[8,4608]{1,0:T(8,128)(2,1)S(1)} %add_convert_fusion.3), channel_id=1, source_target_pairs={{0,16},{1,17},{2,18},{3,19},{4,20},{5,21},{6,22},{7,23},{8,10},{9,... | collective-permute-start | bytes 221192 | tf_op jit(solution)/shard_map/ppermute | solution.py:167
  71.5 1.3 %collective-permute-done.42 = bf16[8,4608]{1,0:T(8,128)(2,1)S(1)} collective-permute-done((bf16[8,4608]{1,0:T(8,128)(2,1)S(1)}, bf16[8,4608]{1,0:T(8,128)(2,1)S(1)}, u32[]{:S(2)}, u32[]{:S(2)}) %collective-permute-start.42) | collective-permute-done | bytes 73760 | tf_op jit(solution)/shard_map/ppermute | solution.py:167
  72.9 1.5 %collective-permute-start.47 = (bf16[8,4608]{1,0:T(8,128)(2,1)S(1)}, bf16[8,4608]{1,0:T(8,128)(2,1)S(1)}, u32[]{:S(2)}, u32[]{:S(2)}) collective-permute-start(bf16[8,4608]{1,0:T(8,128)(2,1)S(1)} %get-tuple-element.82), channel_id=1, source_target_pairs={{0,8},{1,9},{2,10},{3,11},{4,12},{5,13},{6,14},{7,15},{8,2},{9,3},... | collective-permute-start | bytes 221192 | tf_op jit(solution)/shard_map/ppermute | solution.py:173
  74.4 2.1 %collective-permute-start.45 = (bf16[8,4608]{1,0:T(8,128)(2,1)S(1)}, bf16[8,4608]{1,0:T(8,128)(2,1)S(1)}, u32[]{:S(2)}, u32[]{:S(2)}) collective-permute-start(bf16[8,4608]{1,0:T(8,128)(2,1)S(1)} %get-tuple-element.82), channel_id=1, source_target_pairs={{0,8},{1,9},{2,10},{3,11},{4,12},{5,13},{6,14},{7,15},{8,0},{9,1},... | collective-permute-start | bytes 221192 | tf_op jit(solution)/shard_map/ppermute | solution.py:173
  82.2 2.1 %collective-permute-done.52.refs_7_ = bf16[8,4608]{1,0:T(8,128)(2,1)S(1)} collective-permute-done((bf16[8,4608]{1,0:T(8,128)(2,1)S(1)}, bf16[8,4608]{1,0:T(8,128)(2,1)S(1)}, u32[]{:S(2)}, u32[]{:S(2)}) %collective-permute-start.52) | collective-permute-done | bytes 73760 | tf_op jit(solution)/shard_map/ppermute | solution.py:173
  85.0 1.8 %shard_map.81 = (bf16[8,8,512]{2,1,0:T(8,128)(2,1)}, bf16[8,4608]{1,0:T(8,128)(2,1)S(1)}, bf16[8,4608]{1,0:T(8,128)(2,1)S(1)}, bf16[8,4608]{1,0:T(8,128)(2,1)S(1...) custom-call(bf16[8,4608]{1,0:T(8,128)(2,1)S(1)} %collective-permute-, ...), custom_call_target="tpu_custom_call", output_to_operand_aliasing={{0}: (11, {})} | custom-call | flops 603979776 | bytes 9437184 | tf_op jit(solution)/shard_map/pallas_call | solution.py:191
  93.8 1.6 %collective-permute-done.56 = bf16[8,4608]{1,0:T(8,128)(2,1)S(1)} collective-permute-done((bf16[8,4608]{1,0:T(8,128)(2,1)S(1)}, bf16[8,4608]{1,0:T(8,128)(2,1)S(1)}, u32[]{:S(2)}, u32[]{:S(2)}) %collective-permute-start.56) | collective-permute-done | bytes 73760 | tf_op jit(solution)/shard_map/ppermute | solution.py:179
  96.1 2.1 %collective-permute-start.61 = (bf16[8,4608]{1,0:T(8,128)(2,1)S(1)}, bf16[8,4608]{1,0:T(8,128)(2,1)S(1)}, u32[]{:S(2)}, u32[]{:S(2)}) collective-permute-start(bf16[8,4608]{1,0:T(8,128)(2,1)S(1)} %select_convert_fusion), channel_id=1, source_target_pairs={{0,8},{1,9},{2,10},{3,11},{4,12},{5,13},{6,14},{7,15},{8,0},{9,1},... | collective-permute-start | bytes 221192 | tf_op jit(solution)/shard_map/ppermute | solution.py:173
  (112 shorter events, 38.8 us)
Async XLA Ops:
  0.6 7.1 %collective-permute-start.3 = (bf16[8,4608]{1,0:T(8,128)(2,1)}, bf16[8,4608]{1,0:T(8,128)(2,1)S(1)}, u32[]{:S(2)}, u32[]{:S(2)}) collective-permute-start(bf16[8,4608]{1,0:T(8,128)(2,1)} %refs_0_.1), channel_id=1, source_target_pairs={{0,16},{1,17},{2,18},{3,19},{4,20},{5,21},{6,22},{7,23},{8,12},{9,... | collective-permute-start | bytes 221192 | tf_op jit(solution)/shard_map/ppermute | solution.py:167
  3.7 10.0 %collective-permute-start = (bf16[8,4608]{1,0:T(8,128)(2,1)}, bf16[8,4608]{1,0:T(8,128)(2,1)S(1)}, u32[]{:S(2)}, u32[]{:S(2)}) collective-permute-start(bf16[8,4608]{1,0:T(8,128)(2,1)} %refs_0_.1), channel_id=1, source_target_pairs={{0,16},{1,17},{2,18},{3,19},{4,20},{5,21},{6,22},{7,23},{8,9},{9,8... | collective-permute-start | bytes 221192 | tf_op jit(solution)/shard_map/ppermute | solution.py:167
  5.7 8.1 %collective-permute-start.1 = (bf16[8,4608]{1,0:T(8,128)(2,1)}, bf16[8,4608]{1,0:T(8,128)(2,1)S(1)}, u32[]{:S(2)}, u32[]{:S(2)}) collective-permute-start(bf16[8,4608]{1,0:T(8,128)(2,1)} %refs_0_.1), channel_id=1, source_target_pairs={{0,16},{1,17},{2,18},{3,19},{4,20},{5,21},{6,22},{7,23},{8,10},{9,... | collective-permute-start | bytes 221192 | tf_op jit(solution)/shard_map/ppermute | solution.py:167
  5.8 8.0 %collective-permute-start.2 = (bf16[8,4608]{1,0:T(8,128)(2,1)}, bf16[8,4608]{1,0:T(8,128)(2,1)S(1)}, u32[]{:S(2)}, u32[]{:S(2)}) collective-permute-start(bf16[8,4608]{1,0:T(8,128)(2,1)} %refs_0_.1), channel_id=1, source_target_pairs={{0,16},{1,17},{2,18},{3,19},{4,20},{5,21},{6,22},{7,23},{8,11},{9,... | collective-permute-start | bytes 221192 | tf_op jit(solution)/shard_map/ppermute | solution.py:167
  7.7 6.1 %collective-permute-start.4 = (bf16[8,4608]{1,0:T(8,128)(2,1)S(1)}, bf16[8,4608]{1,0:T(8,128)(2,1)S(1)}, u32[]{:S(2)}, u32[]{:S(2)}) collective-permute-start(bf16[8,4608]{1,0:T(8,128)(2,1)S(1)} %collective-permute-done.3.refs_4_), channel_id=1, source_target_pairs={{0,16},{1,17},{2,18},{3,19},{4,20},{5,21},{6,22},{7,23},{8,9},{9,8... | collective-permute-start | bytes 221192 | tf_op jit(solution)/shard_map/ppermute | solution.py:167
  8.2 5.6 %collective-permute-start.6 = (bf16[8,4608]{1,0:T(8,128)(2,1)S(1)}, bf16[8,4608]{1,0:T(8,128)(2,1)S(1)}, u32[]{:S(2)}, u32[]{:S(2)}) collective-permute-start(bf16[8,4608]{1,0:T(8,128)(2,1)S(1)} %collective-permute-done.5.refs_6_), channel_id=1, source_target_pairs={{0,16},{1,17},{2,18},{3,19},{4,20},{5,21},{6,22},{7,23},{8,9},{9,8... | collective-permute-start | bytes 221192 | tf_op jit(solution)/shard_map/ppermute | solution.py:167
  14.5 5.7 %collective-permute-start.10 = (bf16[8,4608]{1,0:T(8,128)(2,1)S(1)}, bf16[8,4608]{1,0:T(8,128)(2,1)S(1)}, u32[]{:S(2)}, u32[]{:S(2)}) collective-permute-start(bf16[8,4608]{1,0:T(8,128)(2,1)S(1)} %get-tuple-element.51), channel_id=1, source_target_pairs={{0,16},{1,17},{2,18},{3,19},{4,20},{5,21},{6,22},{7,23},{8,9},{9,8... | collective-permute-start | bytes 221192 | tf_op jit(solution)/shard_map/ppermute | solution.py:167
  16.0 4.7 %collective-permute-start.12 = (bf16[8,4608]{1,0:T(8,128)(2,1)S(1)}, bf16[8,4608]{1,0:T(8,128)(2,1)S(1)}, u32[]{:S(2)}, u32[]{:S(2)}) collective-permute-start(bf16[8,4608]{1,0:T(8,128)(2,1)S(1)} %get-tuple-element.52), channel_id=1, source_target_pairs={{0,16},{1,17},{2,18},{3,19},{4,20},{5,21},{6,22},{7,23},{8,14},{9,... | collective-permute-start | bytes 221192 | tf_op jit(solution)/shard_map/ppermute | solution.py:167
  24.7 4.8 %collective-permute-start.16 = (bf16[8,4608]{1,0:T(8,128)(2,1)S(1)}, bf16[8,4608]{1,0:T(8,128)(2,1)S(1)}, u32[]{:S(2)}, u32[]{:S(2)}) collective-permute-start(bf16[8,4608]{1,0:T(8,128)(2,1)S(1)} %get-tuple-element.84), channel_id=1, source_target_pairs={{0,8},{1,9},{2,10},{3,11},{4,12},{5,13},{6,14},{7,15},{8,2},{9,3},... | collective-permute-start | bytes 221192 | tf_op jit(solution)/shard_map/ppermute | solution.py:173
  26.0 5.5 %collective-permute-start.18 = (bf16[8,4608]{1,0:T(8,128)(2,1)S(1)}, bf16[8,4608]{1,0:T(8,128)(2,1)S(1)}, u32[]{:S(2)}, u32[]{:S(2)}) collective-permute-start(bf16[8,4608]{1,0:T(8,128)(2,1)S(1)} %get-tuple-element.84), channel_id=1, source_target_pairs={{0,8},{1,9},{2,10},{3,11},{4,12},{5,13},{6,14},{7,15},{8,4},{9,5},... | collective-permute-start | bytes 221192 | tf_op jit(solution)/shard_map/ppermute | solution.py:173
  26.4 6.5 %collective-permute-start.14 = (bf16[8,4608]{1,0:T(8,128)(2,1)S(1)}, bf16[8,4608]{1,0:T(8,128)(2,1)S(1)}, u32[]{:S(2)}, u32[]{:S(2)}) collective-permute-start(bf16[8,4608]{1,0:T(8,128)(2,1)S(1)} %get-tuple-element.84), channel_id=1, source_target_pairs={{0,8},{1,9},{2,10},{3,11},{4,12},{5,13},{6,14},{7,15},{8,0},{9,1},... | collective-permute-start | bytes 221192 | tf_op jit(solution)/shard_map/ppermute | solution.py:173
  27.8 5.7 %collective-permute-start.15 = (bf16[8,4608]{1,0:T(8,128)(2,1)S(1)}, bf16[8,4608]{1,0:T(8,128)(2,1)S(1)}, u32[]{:S(2)}, u32[]{:S(2)}) collective-permute-start(bf16[8,4608]{1,0:T(8,128)(2,1)S(1)} %get-tuple-element.84), channel_id=1, source_target_pairs={{0,8},{1,9},{2,10},{3,11},{4,12},{5,13},{6,14},{7,15},{8,1},{9,0},... | collective-permute-start | bytes 221192 | tf_op jit(solution)/shard_map/ppermute | solution.py:173
  27.8 5.7 %collective-permute-start.20 = (bf16[8,4608]{1,0:T(8,128)(2,1)S(1)}, bf16[8,4608]{1,0:T(8,128)(2,1)S(1)}, u32[]{:S(2)}, u32[]{:S(2)}) collective-permute-start(bf16[8,4608]{1,0:T(8,128)(2,1)S(1)} %get-tuple-element.84), channel_id=1, source_target_pairs={{0,8},{1,9},{2,10},{3,11},{4,12},{5,13},{6,14},{7,15},{8,6},{9,7},... | collective-permute-start | bytes 221192 | tf_op jit(solution)/shard_map/ppermute | solution.py:173
  29.4 6.6 %collective-permute-start.21 = (bf16[8,4608]{1,0:T(8,128)(2,1)S(1)}, bf16[8,4608]{1,0:T(8,128)(2,1)S(1)}, u32[]{:S(2)}, u32[]{:S(2)}) collective-permute-start(bf16[8,4608]{1,0:T(8,128)(2,1)S(1)} %get-tuple-element.84), channel_id=1, source_target_pairs={{0,8},{1,9},{2,10},{3,11},{4,12},{5,13},{6,14},{7,15},{8,7},{9,6},... | collective-permute-start | bytes 221192 | tf_op jit(solution)/shard_map/ppermute | solution.py:173
  31.4 5.1 %collective-permute-start.17 = (bf16[8,4608]{1,0:T(8,128)(2,1)S(1)}, bf16[8,4608]{1,0:T(8,128)(2,1)S(1)}, u32[]{:S(2)}, u32[]{:S(2)}) collective-permute-start(bf16[8,4608]{1,0:T(8,128)(2,1)S(1)} %collective-permute-done.16.refs_2_), channel_id=1, source_target_pairs={{0,1},{1,0},{2,3},{3,2},{4,5},{5,4},{6,7},{7,6},{8,24},{9,25},{10,... | collective-permute-start | bytes 221192 | tf_op jit(solution)/shard_map/ppermute | solution.py:167
  39.5 5.0 %collective-permute-start.24 = (bf16[8,4608]{1,0:T(8,128)(2,1)S(1)}, bf16[8,4608]{1,0:T(8,128)(2,1)S(1)}, u32[]{:S(2)}, u32[]{:S(2)}) collective-permute-start(bf16[8,4608]{1,0:T(8,128)(2,1)S(1)} %get-tuple-element.57), channel_id=1, source_target_pairs={{0,8},{1,9},{2,10},{3,11},{4,12},{5,13},{6,14},{7,15},{8,0},{9,1},... | collective-permute-start | bytes 221192 | tf_op jit(solution)/shard_map/ppermute | solution.py:179
  39.7 4.9 %collective-permute-start.25 = (bf16[8,4608]{1,0:T(8,128)(2,1)S(1)}, bf16[8,4608]{1,0:T(8,128)(2,1)S(1)}, u32[]{:S(2)}, u32[]{:S(2)}) collective-permute-start(bf16[8,4608]{1,0:T(8,128)(2,1)S(1)} %get-tuple-element.58), channel_id=1, source_target_pairs={{0,9},{1,8},{2,11},{3,10},{4,13},{5,12},{6,15},{7,14},{8,0},{9,1},... | collective-permute-start | bytes 221192 | tf_op jit(solution)/shard_map/ppermute | solution.py:179
  47.2 8.3 %collective-permute-start.32 = (bf16[8,4608]{1,0:T(8,128)(2,1)S(1)}, bf16[8,4608]{1,0:T(8,128)(2,1)S(1)}, u32[]{:S(2)}, u32[]{:S(2)}) collective-permute-start(bf16[8,4608]{1,0:T(8,128)(2,1)S(1)} %convert_add_fusion.2), channel_id=1, source_target_pairs={{24,10},{25,11},{26,8},{27,9},{28,14},{29,15},{30,12},{31,13},{8,0... | collective-permute-start | bytes 221192 | tf_op jit(solution)/shard_map/ppermute | solution.py:187
  53.5 5.1 %collective-permute-start.30 = (bf16[8,4608]{1,0:T(8,128)(2,1)S(1)}, bf16[8,4608]{1,0:T(8,128)(2,1)S(1)}, u32[]{:S(2)}, u32[]{:S(2)}) collective-permute-start(bf16[8,4608]{1,0:T(8,128)(2,1)S(1)} %convert_add_fusion.2), channel_id=1, source_target_pairs={{24,8},{25,9},{26,10},{27,11},{28,12},{29,13},{30,14},{31,15},{8,0... | collective-permute-start | bytes 221192 | tf_op jit(solution)/shard_map/ppermute | solution.py:187
  53.6 5.0 %collective-permute-start.31 = (bf16[8,4608]{1,0:T(8,128)(2,1)S(1)}, bf16[8,4608]{1,0:T(8,128)(2,1)S(1)}, u32[]{:S(2)}, u32[]{:S(2)}) collective-permute-start(bf16[8,4608]{1,0:T(8,128)(2,1)S(1)} %convert_add_fusion.2), channel_id=1, source_target_pairs={{24,9},{25,8},{26,11},{27,10},{28,13},{29,12},{30,15},{31,14},{8,0... | collective-permute-start | bytes 221192 | tf_op jit(solution)/shard_map/ppermute | solution.py:187
  55.9 4.7 %collective-permute-start.35 = (bf16[8,4608]{1,0:T(8,128)(2,1)S(1)}, bf16[8,4608]{1,0:T(8,128)(2,1)S(1)}, u32[]{:S(2)}, u32[]{:S(2)}) collective-permute-start(bf16[8,4608]{1,0:T(8,128)(2,1)S(1)} %collective-permute-done.34.refs_4_), channel_id=1, source_target_pairs={{0,16},{1,17},{2,18},{3,19},{4,20},{5,21},{6,22},{7,23},{8,9},{9,8... | collective-permute-start | bytes 221192 | tf_op jit(solution)/shard_map/ppermute | solution.py:167
  62.2 4.9 %collective-permute-start.39 = (bf16[8,4608]{1,0:T(8,128)(2,1)S(1)}, bf16[8,4608]{1,0:T(8,128)(2,1)S(1)}, u32[]{:S(2)}, u32[]{:S(2)}) collective-permute-start(bf16[8,4608]{1,0:T(8,128)(2,1)S(1)} %get-tuple-element.67), channel_id=1, source_target_pairs={{0,16},{1,17},{2,18},{3,19},{4,20},{5,21},{6,22},{7,23},{8,9},{9,8... | collective-permute-start | bytes 221192 | tf_op jit(solution)/shard_map/ppermute | solution.py:167
  63.0 5.4 %collective-permute-start.41 = (bf16[8,4608]{1,0:T(8,128)(2,1)S(1)}, bf16[8,4608]{1,0:T(8,128)(2,1)S(1)}, u32[]{:S(2)}, u32[]{:S(2)}) collective-permute-start(bf16[8,4608]{1,0:T(8,128)(2,1)S(1)} %get-tuple-element.69), channel_id=1, source_target_pairs={{0,16},{1,17},{2,18},{3,19},{4,20},{5,21},{6,22},{7,23},{8,9},{9,8... | collective-permute-start | bytes 221192 | tf_op jit(solution)/shard_map/ppermute | solution.py:167
  64.2 5.0 %collective-permute-start.38 = (bf16[8,4608]{1,0:T(8,128)(2,1)S(1)}, bf16[8,4608]{1,0:T(8,128)(2,1)S(1)}, u32[]{:S(2)}, u32[]{:S(2)}) collective-permute-start(bf16[8,4608]{1,0:T(8,128)(2,1)S(1)} %get-tuple-element.65), channel_id=1, source_target_pairs={{0,16},{1,17},{2,18},{3,19},{4,20},{5,21},{6,22},{7,23},{8,15},{9,... | collective-permute-start | bytes 221192 | tf_op jit(solution)/shard_map/ppermute | solution.py:167
  72.9 4.8 %collective-permute-start.47 = (bf16[8,4608]{1,0:T(8,128)(2,1)S(1)}, bf16[8,4608]{1,0:T(8,128)(2,1)S(1)}, u32[]{:S(2)}, u32[]{:S(2)}) collective-permute-start(bf16[8,4608]{1,0:T(8,128)(2,1)S(1)} %get-tuple-element.82), channel_id=1, source_target_pairs={{0,8},{1,9},{2,10},{3,11},{4,12},{5,13},{6,14},{7,15},{8,2},{9,3},... | collective-permute-start | bytes 221192 | tf_op jit(solution)/shard_map/ppermute | solution.py:173
  74.4 4.7 %collective-permute-start.49 = (bf16[8,4608]{1,0:T(8,128)(2,1)S(1)}, bf16[8,4608]{1,0:T(8,128)(2,1)S(1)}, u32[]{:S(2)}, u32[]{:S(2)}) collective-permute-start(bf16[8,4608]{1,0:T(8,128)(2,1)S(1)} %get-tuple-element.82), channel_id=1, source_target_pairs={{0,8},{1,9},{2,10},{3,11},{4,12},{5,13},{6,14},{7,15},{8,4},{9,5},... | collective-permute-start | bytes 221192 | tf_op jit(solution)/shard_map/ppermute | solution.py:173
  74.4 5.5 %collective-permute-start.45 = (bf16[8,4608]{1,0:T(8,128)(2,1)S(1)}, bf16[8,4608]{1,0:T(8,128)(2,1)S(1)}, u32[]{:S(2)}, u32[]{:S(2)}) collective-permute-start(bf16[8,4608]{1,0:T(8,128)(2,1)S(1)} %get-tuple-element.82), channel_id=1, source_target_pairs={{0,8},{1,9},{2,10},{3,11},{4,12},{5,13},{6,14},{7,15},{8,0},{9,1},... | collective-permute-start | bytes 221192 | tf_op jit(solution)/shard_map/ppermute | solution.py:173
  76.5 5.7 %collective-permute-start.51 = (bf16[8,4608]{1,0:T(8,128)(2,1)S(1)}, bf16[8,4608]{1,0:T(8,128)(2,1)S(1)}, u32[]{:S(2)}, u32[]{:S(2)}) collective-permute-start(bf16[8,4608]{1,0:T(8,128)(2,1)S(1)} %get-tuple-element.82), channel_id=1, source_target_pairs={{0,8},{1,9},{2,10},{3,11},{4,12},{5,13},{6,14},{7,15},{8,6},{9,7},... | collective-permute-start | bytes 221192 | tf_op jit(solution)/shard_map/ppermute | solution.py:173
  77.7 6.5 %collective-permute-start.52 = (bf16[8,4608]{1,0:T(8,128)(2,1)S(1)}, bf16[8,4608]{1,0:T(8,128)(2,1)S(1)}, u32[]{:S(2)}, u32[]{:S(2)}) collective-permute-start(bf16[8,4608]{1,0:T(8,128)(2,1)S(1)} %get-tuple-element.82), channel_id=1, source_target_pairs={{0,8},{1,9},{2,10},{3,11},{4,12},{5,13},{6,14},{7,15},{8,7},{9,6},... | collective-permute-start | bytes 221192 | tf_op jit(solution)/shard_map/ppermute | solution.py:173
  79.1 5.2 %collective-permute-start.48 = (bf16[8,4608]{1,0:T(8,128)(2,1)S(1)}, bf16[8,4608]{1,0:T(8,128)(2,1)S(1)}, u32[]{:S(2)}, u32[]{:S(2)}) collective-permute-start(bf16[8,4608]{1,0:T(8,128)(2,1)S(1)} %collective-permute-done.47.refs_2_), channel_id=1, source_target_pairs={{0,1},{1,0},{2,3},{3,2},{4,5},{5,4},{6,7},{7,6},{8,24},{9,25},{10,... | collective-permute-start | bytes 221192 | tf_op jit(solution)/shard_map/ppermute | solution.py:167
  80.0 5.0 %collective-permute-start.50 = (bf16[8,4608]{1,0:T(8,128)(2,1)S(1)}, bf16[8,4608]{1,0:T(8,128)(2,1)S(1)}, u32[]{:S(2)}, u32[]{:S(2)}) collective-permute-start(bf16[8,4608]{1,0:T(8,128)(2,1)S(1)} %collective-permute-done.49.refs_4_), channel_id=1, source_target_pairs={{0,1},{1,0},{2,3},{3,2},{4,5},{5,4},{6,7},{7,6},{8,24},{9,25},{10,... | collective-permute-start | bytes 221192 | tf_op jit(solution)/shard_map/ppermute | solution.py:167
  88.9 4.8 %collective-permute-start.54 = (bf16[8,4608]{1,0:T(8,128)(2,1)S(1)}, bf16[8,4608]{1,0:T(8,128)(2,1)S(1)}, u32[]{:S(2)}, u32[]{:S(2)}) collective-permute-start(bf16[8,4608]{1,0:T(8,128)(2,1)S(1)} %get-tuple-element.75), channel_id=1, source_target_pairs={{0,8},{1,9},{2,10},{3,11},{4,12},{5,13},{6,14},{7,15},{8,0},{9,1},... | collective-permute-start | bytes 221192 | tf_op jit(solution)/shard_map/ppermute | solution.py:179
  (31 other events, 126.4 us)
